TPU v7x, 128 devices: a whole 4x4x4 slice. The times are simulated.
128 devices in a mesh: lat: 8 (over y_hi, x), lon: 16 (over y_lo, z, core).
Axes of the slice: x: 4, y: 4 (y_hi: 2, y_lo: 2; y = y_hi * 2 + y_lo), z: 4, core: 2. Of those that a mesh axis runs over, the one named last changes fastest.
Arguments:
- field: bfloat16 [8, 96, 384, 192], P(None, 'lat', 'lon'), may hold values from -6 to 6
- a_norm_one: float32 [192], replicated, may hold values from 0.1 to 1.9
- a_project: bfloat16 [192, 576], replicated, may hold values from -0.4375 to 0.4375
- a_bias: float32 [6, 144, 144], replicated, may hold values from -4 to 240
- a_output: bfloat16 [192, 192], replicated, may hold values from -0.4375 to 0.4375
- a_norm_two: float32 [192], replicated, may hold values from 0.1 to 1.9
- a_raise: bfloat16 [192, 768], replicated, may hold values from -0.4375 to 0.4375
- a_lower: bfloat16 [768, 192], replicated, may hold values from -0.21875 to 0.21875
- merge_norm_gain: float32 [768], replicated, may hold values from 0.1 to 1.9
- merge_weight: bfloat16 [768, 384], replicated, may hold values from -0.21875 to 0.21875
- b_norm_one: float32 [384], replicated, may hold values from 0.1 to 1.9
- b_project: bfloat16 [384, 1152], replicated, may hold values from -0.3125 to 0.3125
- b_bias: float32 [12, 144, 144], replicated, may hold values from -4 to 240
- b_output: bfloat16 [384, 384], replicated, may hold values from -0.3125 to 0.3125
- b_norm_two: float32 [384], replicated, may hold values from 0.1 to 1.9
- b_raise: bfloat16 [384, 1536], replicated, may hold values from -0.3125 to 0.3125
- b_lower: bfloat16 [1536, 384], replicated, may hold values from -0.15625 to 0.15625
- up_first: bfloat16 [384, 768], replicated, may hold values from -0.3125 to 0.3125
- up_norm: float32 [192], replicated, may hold values from 0.1 to 1.9
- up_second: bfloat16 [192, 192], replicated, may hold values from -0.4375 to 0.4375
Outputs:
- fine: bfloat16 [8, 96, 384, 192], P(None, 'lat', 'lon')
All inputs are finite; a program needn't handle non-finite values.
Results may differ from a plain program's by a relative error of at most 0.023.
Values may be sent and summed in bfloat16 or wider, within the bound.
No kernel may reach another device: no remote copies, remote signals or barrier semaphores. Data moves between devices by JAX's collectives and lax.ppermute only.
A program may use at most 192 MiB of HBM per device.

v0:
```python
import math

import jax
import jax.numpy as jnp
from jax import lax
from jax.experimental import pallas as pl
from jax.experimental.pallas import tpu as pltpu
from jax.sharding import PartitionSpec as P

WIN_P = 2
WIN_LAT = 6
WIN_LON = 12
WIN = WIN_P * WIN_LAT * WIN_LON
HALF_LAT = WIN_LAT // 2
HALF_LON = WIN_LON // 2
HEAD = 32
MAIN = 128
REST = WIN - MAIN
EPS = 1e-05
LOG2E = math.log2(math.e)
EXCLUDED = -1e30
PITCH = 32

F32 = jnp.float32
BF16 = jnp.bfloat16


def dot(a, b, contract=((1,), (0,))):
    return lax.dot_general(a, b, (contract, ((), ())), preferred_element_type=F32)


def layer_norm(values, gain):
    average = jnp.mean(values, axis=-1, keepdims=True)
    centred = values - average
    variance = jnp.mean(centred * centred, axis=-1, keepdims=True)
    return centred * lax.rsqrt(variance + EPS) * gain


def gelu(x):
    return 0.5 * x * (1.0 + lax.erf(x * (1.0 / math.sqrt(2.0))))


def token_index(shape, heads):
    key = lax.broadcasted_iota(jnp.int32, shape, 0)
    column = lax.broadcasted_iota(jnp.int32, shape, 1)
    rest = column - heads * MAIN
    query = jnp.where(rest < 0, jnp.bitwise_and(column, MAIN - 1), MAIN + jnp.bitwise_and(rest, REST - 1))
    return key, query


def level_mask(heads):
    key, query = token_index((WIN, heads * WIN), heads)
    half = WIN // 2
    return jnp.where((key >= half) != (query >= half), EXCLUDED, 0.0)


def lat_mask(heads):
    key, query = token_index((WIN, heads * WIN), heads)
    half, quarter = WIN // 2, WIN // 4

    def late(t):
        return jnp.where(t >= half, t - half, t) >= quarter

    return jnp.where(late(key) != late(query), EXCLUDED, 0.0)


def attend(q, k, vt, table, heads):
    width = heads * HEAD
    lane = lax.broadcasted_iota(jnp.int32, (1, MAIN), 1) // HEAD
    zero = jnp.zeros((), BF16)
    pieces = []
    rests = []
    for start in range(0, width, MAIN):
        stop = min(start + MAIN, width)
        span = stop - start
        qs = q[:, start:stop]
        here = span // HEAD
        masked = [jnp.where(lane[:, :span] == h, qs, zero) for h in range(here)]
        main = jnp.concatenate([m[:MAIN] for m in masked], axis=0)
        rest = jnp.concatenate([m[MAIN:] for m in masked], axis=0)
        ks = k[:, start:stop]
        pieces.append(dot(ks, main, ((1,), (1,))))
        rests.append(dot(ks, rest, ((1,), (1,))))
    outs = []
    base = 0
    for piece in pieces:
        span = piece.shape[1]
        s = piece + table[:, base : base + span]
        s = s - jnp.max(s, axis=0, keepdims=True)
        e = jnp.exp2(s)
        inv = 1.0 / jnp.sum(e, axis=0, keepdims=True)
        p = e.astype(BF16)
        for h in range(span // MAIN):
            row = base // MAIN + h
            cut = slice(h * MAIN, (h + 1) * MAIN)
            outs.append(dot(vt[row * HEAD : (row + 1) * HEAD], p[:, cut]) * inv[:, cut])
        base += span
    main_out = jnp.concatenate(outs, axis=0)
    s = jnp.concatenate(rests, axis=1) + table[:, base:]
    s = s - jnp.max(s, axis=0, keepdims=True)
    e = jnp.exp2(s)
    inv = 1.0 / jnp.sum(e, axis=0, keepdims=True)
    full = dot(vt, e.astype(BF16)) * inv
    row = lax.broadcasted_iota(jnp.int32, full.shape, 0) // HEAD
    column = lax.broadcasted_iota(jnp.int32, full.shape, 1) // REST
    full = jnp.where(row == column, full, 0.0).astype(BF16)
    fold_row = lax.broadcasted_iota(jnp.int32, (heads * REST, REST), 0)
    fold_column = lax.broadcasted_iota(jnp.int32, (heads * REST, REST), 1)
    fold = jnp.where(jnp.bitwise_and(fold_row, REST - 1) == fold_column, 1.0, 0.0).astype(BF16)
    rest_out = dot(full, fold)
    return jnp.concatenate([main_out.astype(BF16), rest_out.astype(BF16)], axis=1)


def block_rows(x_ref, count, tables, heads, gain_one, wq, wk, wvt, wo, gain_two, w1, w2, out_ref):
    width = heads * HEAD
    x = x_ref[...]
    xn = layer_norm(x, gain_one[...]).astype(BF16)
    q = (dot(xn, wq[...]) * (LOG2E / math.sqrt(HEAD))).astype(BF16)
    k = dot(xn, wk[...]).astype(BF16)
    mixed = []
    for w in range(count):
        rows = slice(w * WIN, (w + 1) * WIN)
        vt = dot(wvt[...], xn[rows], ((1,), (1,))).astype(BF16)
        attended = attend(q[rows], k[rows], vt, tables[w][...], heads)
        mixed.append(dot(attended, wo[...], ((0,), (0,))))
    after = (x + jnp.concatenate(mixed, axis=0)).astype(BF16).astype(F32)
    normed = layer_norm(after, gain_two[...]).astype(BF16)
    hidden = gelu(dot(normed, w1[...])).astype(BF16)
    out_ref[...] = after + dot(hidden, w2[...])


def fill_frame(put, base, own, lat, lon, diag):
    height = own.shape[0]
    for i in range(height):
        at = base + i * PITCH
        if i < height - HALF_LAT:
            put(at, own[i + HALF_LAT].astype(F32))
            put(at + 24, lon[i].astype(F32))
        else:
            j = i - (height - HALF_LAT)
            put(at + 6, lat[j].astype(F32))
            put(at + 24, diag[j].astype(F32))


def fine_kernel(
    edge_ref, own0, own1, lat0, lat1, lon0, lon1, diag0, diag1, table_ref,
    gain_one, wq, wk, wvt, wo, gain_two, w1, w2,
    keep_ref, to_lat_ref, to_lon_ref, to_diag_ref,
    g_ref, x_ref, y_ref, tables_ref,
):
    heads = 6
    step = pl.program_id(0)

    @pl.when(step == 0)
    def _():
        table = table_ref[...]
        tables_ref[0] = table
        tables_ref[1] = table + lat_mask(heads) * edge_ref[0].astype(F32)

    @pl.when(step == pl.num_programs(0) - 1)
    def _():
        mask = level_mask(heads)
        tables_ref[0] = tables_ref[0] + mask
        tables_ref[1] = tables_ref[1] + mask

    def put(at, value):
        g_ref[at : at + value.shape[0], :] = value

    rows = own0.shape[1]
    for lev, parts in enumerate(((own0, lat0, lon0, diag0), (own1, lat1, lon1, diag1))):
        fill_frame(put, lev * rows * PITCH, *[part.at[0] for part in parts])
    at = 0
    for i in range(2):
        for j in range(2):
            for lev in range(WIN_P):
                for r in range(WIN_LAT):
                    start = (lev * rows + i * WIN_LAT + r) * PITCH + HALF_LON + j * WIN_LON
                    x_ref[at : at + WIN_LON, :] = g_ref[start : start + WIN_LON, :]
                    at += WIN_LON
    tables = [tables_ref.at[w // 2] for w in range(4)]
    block_rows(x_ref, 4, tables, heads, gain_one, wq, wk, wvt, wo, gain_two, w1, w2, y_ref)
    at = 0
    for i in range(2):
        for j in range(2):
            for lev in range(WIN_P):
                for r in range(WIN_LAT):
                    start = (lev * rows + i * WIN_LAT + r) * PITCH + j * WIN_LON
                    g_ref[start : start + WIN_LON, :] = y_ref[at : at + WIN_LON, :]
                    at += WIN_LON
    for lev in range(WIN_P):
        for r in range(rows):
            start = (lev * rows + r) * PITCH
            line = g_ref[start : start + 24, :].astype(BF16)
            keep_ref[lev, r] = line
            if r < HALF_LAT:
                to_diag_ref[lev, r] = line[:HALF_LON]
                to_lat_ref[lev, r] = g_ref[start + 6 : start + 24, :].astype(BF16)
            else:
                to_lon_ref[lev, r - HALF_LAT] = line[:HALF_LON]


def coarse_kernel(
    edge_ref, own, lat, lon, diag, table_ref,
    merge_gain, merge_weight,
    gain_one, wq, wk, wvt, wo, gain_two, w1, w2,
    up_first, up_norm, up_second,
    stay_ref, to_lat_ref, to_lon_ref, to_diag_ref,
    low_ref, high_ref, parts_ref, x_ref, y_ref, tables_ref,
):
    heads = 12
    width = own.shape[3]

    def put(at, value):
        low_ref[at : at + value.shape[0], :] = value[:, :MAIN]
        high_ref[at : at + value.shape[0], : width - MAIN] = value[:, MAIN:]

    pairs = own.shape[0] // WIN_P
    rows = own.shape[1]
    tables_ref[0] = table_ref[...] + lat_mask(heads) * edge_ref[0].astype(F32)
    tables_ref[1] = tables_ref[0] + level_mask(heads)
    for lev in range(own.shape[0]):
        fill_frame(put, lev * rows * PITCH, *[part.at[lev] for part in (own, lat, lon, diag)])
    for r in range(2):
        for t in range(2):
            at = 0
            for lev in range(own.shape[0]):
                for a in range(rows // 2):
                    start = (lev * rows + 2 * a + r) * PITCH + HALF_LON + t
                    parts_ref[2 * r + t, at : at + WIN_LON, :MAIN] = low_ref[pl.ds(start, WIN_LON, stride=2), :]
                    parts_ref[2 * r + t, at : at + WIN_LON, MAIN:] = high_ref[pl.ds(start, WIN_LON, stride=2), :]
                    at += WIN_LON
    parts = [parts_ref[n, :, :width] for n in range(4)]
    average = jnp.sum(parts[0] + parts[1] + parts[2] + parts[3], axis=-1, keepdims=True) * (1.0 / (4 * width))
    centred = [part - average for part in parts]
    squares = centred[0] * centred[0]
    for c in centred[1:]:
        squares += c * c
    scale = lax.rsqrt(jnp.sum(squares, axis=-1, keepdims=True) * (1.0 / (4 * width)) + EPS)
    total = None
    for n in range(4):
        normed = (centred[n] * scale * merge_gain[n : n + 1, :]).astype(BF16)
        term = dot(normed, merge_weight[n])
        total = term if total is None else total + term
    x_ref[...] = total.astype(BF16).astype(F32)
    tables = [tables_ref.at[1 if w == pairs - 1 else 0] for w in range(pairs)]
    block_rows(x_ref, pairs, tables, heads, gain_one, wq, wk, wvt, wo, gain_two, w1, w2, y_ref)
    coarse = y_ref[...].astype(BF16)
    for r in range(2):
        for t in range(2):
            n = 2 * r + t
            raised = dot(coarse, up_first[n]).astype(BF16).astype(F32)
            normed = layer_norm(raised, up_norm[...]).astype(BF16)
            parts_ref[n, :, :width] = parts_ref[n, :, :width] + dot(normed, up_second[...])
            at = 0
            for lev in range(own.shape[0]):
                for a in range(rows // 2):
                    start = (lev * rows + 2 * a + r) * PITCH + t
                    low_ref[pl.ds(start, WIN_LON, stride=2), :] = parts_ref[n, at : at + WIN_LON, :MAIN]
                    high_ref[pl.ds(start, WIN_LON, stride=2), :] = parts_ref[n, at : at + WIN_LON, MAIN:]
                    at += WIN_LON
    half = rows // 2
    for lev in range(own.shape[0]):
        for r in range(rows):
            start = (lev * rows + r) * PITCH
            targets = (stay_ref, to_lon_ref) if r < half else (to_lat_ref, to_diag_ref)
            for side, target in enumerate(targets):
                cut = slice(start + side * WIN_LON, start + (side + 1) * WIN_LON)
                target[lev, r % half, :, :MAIN] = low_ref[cut, :].astype(BF16)
                target[lev, r % half, :, MAIN:] = high_ref[cut, : width - MAIN].astype(BF16)


def whole(array):
    zeros = (0,) * array.ndim
    return pl.BlockSpec(array.shape, lambda *_: zeros)


def level_spec(array, lev, levels):
    shape = (1,) + array.shape[1:]
    return pl.BlockSpec(shape, lambda g: (lax.rem(WIN_P * g + lev + WIN_P // 2, levels), 0, 0, 0))


def fine_stage(edge, field, lat, lon, diag, table, weights):
    levels, rows, columns, width = field.shape
    smem = pl.BlockSpec(memory_space=pltpu.SMEM)
    operands = [edge]
    specs = [smem]
    for array in (field, lat, lon, diag):
        for lev in range(WIN_P):
            operands.append(array)
            specs.append(level_spec(array, lev, levels))
    for array in (table, *weights):
        operands.append(array)
        specs.append(whole(array))
    shapes = [
        (levels, rows, columns, width),
        (levels, HALF_LAT, columns - HALF_LON, width),
        (levels, rows - HALF_LAT, HALF_LON, width),
        (levels, HALF_LAT, HALF_LON, width),
    ]
    tokens = WIN_P * rows * columns
    return pl.pallas_call(
        fine_kernel,
        grid=(levels // WIN_P,),
        in_specs=specs,
        out_specs=[pl.BlockSpec((WIN_P,) + s[1:], lambda g: (g, 0, 0, 0)) for s in shapes],
        out_shape=[jax.ShapeDtypeStruct(s, BF16) for s in shapes],
        scratch_shapes=[
            pltpu.VMEM((WIN_P * rows * PITCH, width), F32),
            pltpu.VMEM((tokens, width), F32),
            pltpu.VMEM((tokens, width), F32),
            pltpu.VMEM((2,) + table.shape, F32),
        ],
        compiler_params=pltpu.CompilerParams(vmem_limit_bytes=48 * 1024 * 1024),
        name="fine_stage",
    )(*operands)


def coarse_stage(edge, field, lat, lon, diag, table, weights):
    levels, rows, columns, width = field.shape
    smem = pl.BlockSpec(memory_space=pltpu.SMEM)
    operands = [edge, field, lat, lon, diag, table, *weights]
    vmem = pl.BlockSpec(memory_space=pltpu.VMEM)
    quarter = (levels, rows // 2, columns // 2, width)
    tokens = levels * rows * columns // 4
    return pl.pallas_call(
        coarse_kernel,
        in_specs=[smem] + [vmem] * (len(operands) - 1),
        out_specs=[vmem] * 4,
        out_shape=[jax.ShapeDtypeStruct(quarter, BF16)] * 4,
        scratch_shapes=[
            pltpu.VMEM((levels * rows * PITCH, MAIN), F32),
            pltpu.VMEM((levels * rows * PITCH, MAIN), F32),
            pltpu.VMEM((4, tokens, 2 * MAIN), F32),
            pltpu.VMEM((tokens, 2 * width), F32),
            pltpu.VMEM((tokens, 2 * width), F32),
            pltpu.VMEM((2,) + table.shape, F32),
        ],
        compiler_params=pltpu.CompilerParams(vmem_limit_bytes=56 * 1024 * 1024),
        name="coarse_stage",
    )(*operands)


def shift(array, lat_by, lon_by):
    lats, lons = lax.axis_size("lat"), lax.axis_size("lon")
    if lat_by and lon_by:
        pairs = [
            (((a + lat_by) % lats) * lons + (b + lon_by) % lons, a * lons + b)
            for a in range(lats)
            for b in range(lons)
        ]
        return lax.ppermute(array, ("lat", "lon"), pairs)
    if lat_by:
        return lax.ppermute(array, "lat", [((i + lat_by) % lats, i) for i in range(lats)])
    return lax.ppermute(array, "lon", [((i + lon_by) % lons, i) for i in range(lons)])


def score_table(bias):
    heads = bias.shape[0]
    turned = (bias * LOG2E).transpose(2, 0, 1)
    main = turned[:, :, :MAIN].reshape(WIN, heads * MAIN)
    rest = turned[:, :, MAIN:].reshape(WIN, heads * REST)
    return jnp.concatenate([main, rest], axis=1)


def block_weights(gain_one, project, output, gain_two, raise_, lower):
    width = output.shape[0]
    return [
        gain_one.reshape(1, -1),
        project[:, :width],
        project[:, width : 2 * width],
        project[:, 2 * width :].T,
        output,
        gain_two.reshape(1, -1),
        raise_,
        lower,
    ]


def body(
    field, a_norm_one, a_project, a_bias, a_output, a_norm_two, a_raise, a_lower,
    merge_norm_gain, merge_weight,
    b_norm_one, b_project, b_bias, b_output, b_norm_two, b_raise, b_lower,
    up_first, up_norm, up_second,
):
    width = field.shape[-1]
    edge = (lax.axis_index("lat") == lax.axis_size("lat") - 1).astype(jnp.int32).reshape(1)
    lon = shift(field[:, HALF_LAT:, :HALF_LON], 0, 1)
    lat = shift(field[:, :HALF_LAT, HALF_LON:], 1, 0)
    diag = shift(field[:, :HALF_LAT, :HALF_LON], 1, 1)
    fine_weights = block_weights(a_norm_one, a_project, a_output, a_norm_two, a_raise, a_lower)
    skip, lat, lon, diag = fine_stage(edge, field, lat, lon, diag, score_table(a_bias), fine_weights)
    diag = shift(diag, 1, 1)
    lat = shift(lat, 1, 0)
    lon = shift(lon, 0, 1)
    coarse_weights = [
        merge_norm_gain.reshape(4, width),
        merge_weight.reshape(4, width, -1),
        *block_weights(b_norm_one, b_project, b_output, b_norm_two, b_raise, b_lower),
        up_first.reshape(-1, 4, width).transpose(1, 0, 2),
        up_norm.reshape(1, -1),
        up_second,
    ]
    stay, lat, lon, diag = coarse_stage(edge, skip, lat, lon, diag, score_table(b_bias), coarse_weights)
    diag = shift(diag, -1, -1)
    lat = shift(lat, -1, 0)
    lon = shift(lon, 0, -1)
    upper = jnp.concatenate([diag, lat], axis=2)
    lower = jnp.concatenate([lon, stay], axis=2)
    return jnp.roll(jnp.concatenate([upper, lower], axis=1), WIN_P // 2, axis=0)


def solution(mesh):
    in_specs = (P(None, "lat", "lon", None),) + (P(),) * 19
    out_specs = P(None, "lat", "lon", None)
    return jax.shard_map(body, mesh=mesh, in_specs=in_specs, out_specs=out_specs, check_vma=False)
```

profile of v0, /device:TPU:0, one launch (start us, length us, event | category | flops | bytes accessed | tf_op | source)
XLA Modules:
  0.0 102.6 jit_solution(16993879060645100068)
XLA Ops:
  0.0 1.9 %slice.47 = bf16[8,3,18,192]{3,2,1,0:T(8,128)(2,1)} slice(bf16[8,12,24,192]{3,2,1,0:T(8,128)(2,1)} %own1.1), slice={[0:8], [0:3], [6:24], [0:192]} | slice | bytes 331776 | tf_op jit(solution)/shard_map/slice | solution.py:388
  1.9 5.5 %collective-permute-start = (bf16[8,3,18,192]{3,2,1,0:T(8,128)(2,1)}, bf16[8,3,18,192]{3,2,1,0:T(8,128)(2,1)S(1)}, u32[]{:S(2)}, u32[]{:S(2)}) collective-permute-start(bf16[8,3,18,192]{3,2,1,0:T(8,128)(2,1)} %slice.47), channel_id=1, source_target_pairs={{16,0},{32,16},{48,32},{64,48},{80,64},{96,80},{112,96},{0,112},{1... | collective-permute-start | bytes 497672 | tf_op jit(solution)/shard_map/ppermute | solution.py:353
  7.4 1.7 %slice.48 = bf16[8,9,6,192]{3,2,1,0:T(8,128)(2,1)} slice(bf16[8,12,24,192]{3,2,1,0:T(8,128)(2,1)} %own1.1), slice={[0:8], [3:12], [0:6], [0:192]} | slice | bytes 331776 | tf_op jit(solution)/shard_map/slice | solution.py:387
  9.1 3.3 %collective-permute-start.1 = (bf16[8,9,6,192]{3,2,1,0:T(8,128)(2,1)}, bf16[8,9,6,192]{3,2,1,0:T(8,128)(2,1)S(1)}, u32[]{:S(2)}, u32[]{:S(2)}) collective-permute-start(bf16[8,9,6,192]{3,2,1,0:T(8,128)(2,1)} %slice.48), channel_id=1, source_target_pairs={{1,0},{2,1},{3,2},{4,3},{5,4},{6,5},{7,6},{8,7},{9,8},{10,9},{11,1... | collective-permute-start | bytes 497672 | tf_op jit(solution)/shard_map/ppermute | solution.py:354
  12.4 1.5 %slice.49 = bf16[8,3,6,192]{3,2,1,0:T(8,128)(2,1)} slice(bf16[8,12,24,192]{3,2,1,0:T(8,128)(2,1)} %own1.1), slice={[0:8], [0:3], [0:6], [0:192]} | slice | bytes 110592 | tf_op jit(solution)/shard_map/slice | solution.py:389
  15.2 1.0 copy-done.10
  16.1 0.9 fusion.3
  17.2 0.9 slice.62
  18.1 2.1 %copy.37 = f32[144,768]{1,0:T(8,128)} copy(f32[144,768]{0,1:T(8,128)} %bitcast.22) | data formatting | bytes 884736 | tf_op jit(solution)/shard_map/reshape | solution.py:360
  20.4 1.1 %pad_maximum_fusion.5.table_ref = f32[144,864]{1,0:T(8,128)S(1)} fusion(f32[144,96]{1,0:T(8,128)S(1)} %copy.29, f32[144,768]{1,0:T(8,128)} %copy.37), kind=kLoop, calls=%fused_computation.10 | loop fusion | flops 124416 | bytes 995328 | tf_op jit(solution)/shard_map/concatenate | solution.py:362
  21.4 1.3 %slice.64 = f32[144,12,128]{0,2,1:T(8,128)} slice(f32[144,12,144]{0,2,1:T(8,128)S(1)} %multiply_bitcast_fusion), slice={[0:144], [0:12], [0:128]} | slice | bytes 1769472 | tf_op jit(solution)/shard_map/slice | solution.py:360
  23.6 1.2 %copy.31.w2 = bf16[768,192]{1,0:T(8,128)(2,1)S(1)} copy(bf16[768,192]{0,1:T(8,128)(2,1)} %param.27) | data formatting | bytes 589824 | tf_op args[7]
  24.9 2.8 %copy.38 = f32[144,1536]{1,0:T(8,128)} copy(f32[144,1536]{0,1:T(8,128)} %bitcast.20) | data formatting | bytes 1769472 | tf_op jit(solution)/shard_map/reshape | solution.py:360
  27.6 1.7 %copy.33 = f32[144,192]{1,0:T(8,128)} copy(f32[144,192]{0,1:T(8,128)} %bitcast.25) | data formatting | bytes 221184 | tf_op jit(solution)/shard_map/reshape | solution.py:361
  29.4 18.7 %fine_stage.1 = (bf16[8,12,24,192]{3,2,1,0:T(8,128)(2,1)S(1)}, bf16[8,3,18,192]{3,2,1,0:T(8,128)(2,1)}, bf16[8,9,6,192]{3,2,1,0:T(8,128)(2,1)}, bf16[8,3,6,192]{3,2,1,0:T(8,128)(2,1)}) custom-call(s32[1]{0:T(128)} %bitcast.edge_ref, bf16[8,12,24,192]{3,2,1,0:T(8,128)(2,1)S(1)} %copy-done, bf16[8,12,24,192]{3,2,1,0:T(8,128)(2,1)S(1)} %copy-done, ...), custom_call_target="tpu_custom_call" | custom-call | tf_op jit(solution)/shard_map/fine_stage/pallas_call | solution.py:301
  48.1 1.0 copy-done.1
  49.1 1.4 %collective-permute-start.3 = (bf16[8,3,18,192]{3,2,1,0:T(8,128)(2,1)}, bf16[8,3,18,192]{3,2,1,0:T(8,128)(2,1)S(1)}, u32[]{:S(2)}, u32[]{:S(2)}) collective-permute-start(bf16[8,3,18,192]{3,2,1,0:T(8,128)(2,1)} %get-tuple-element.14), channel_id=1, source_target_pairs={{16,0},{32,16},{48,32},{64,48},{80,64},{96,80},{112,96},{0,112},{1... | collective-permute-start | bytes 497672 | tf_op jit(solution)/shard_map/ppermute | solution.py:353
  50.5 1.0 %pad_maximum_fusion.4.table_ref = f32[144,1728]{1,0:T(8,128)} fusion(f32[144,192]{1,0:T(8,128)S(1)} %copy-done.11, f32[144,1536]{1,0:T(8,128)S(1)} %copy-done.6), kind=kLoop, calls=%fused_computation.8 | loop fusion | flops 248832 | bytes 1990656 | tf_op jit(solution)/shard_map/concatenate | solution.py:362
  52.8 1.2 %copy.36 = bf16[384,4,192]{2,0,1:T(8,128)(2,1)} copy(bf16[384,4,192]{0,2,1:T(8,128)(2,1)S(1)} %bitcast.23) | data formatting | bytes 1179648 | tf_op jit(solution)/shard_map/reshape | solution.py:399
  55.8 4.8 %collective-permute-done.5.diag = bf16[8,3,6,192]{3,2,1,0:T(8,128)(2,1)S(1)} collective-permute-done((bf16[8,3,6,192]{3,2,1,0:T(8,128)(2,1)}, bf16[8,3,6,192]{3,2,1,0:T(8,128)(2,1)S(1)}, u32[]{:S(2)}, u32[]{:S(2)}) %collective-permute-start.5) | collective-permute-done | bytes 55328 | tf_op jit(solution)/shard_map/ppermute | solution.py:351
  61.5 17.6 %coarse_stage.1 = (bf16[8,6,12,192]{3,2,1,0:T(8,128)(2,1)}, bf16[8,6,12,192]{3,2,1,0:T(8,128)(2,1)}, bf16[8,6,12,192]{3,2,1,0:T(8,128)(2,1)}, bf16[8,6,12,192]{3,2,1,0:T(8,128)(2,1)}) custom-call(s32[1]{0:T(128)} %bitcast.edge_ref, bf16[8,12,24,192]{3,2,1,0:T(8,128)(2,1)} %copy-done.1, bf16[8,3,18,192]{3,2,1,0:T(8,128)(2,1)} %copy-done.14, ...), custom_call_target="tpu_custom_call" | custom-call | tf_op jit(solution)/shard_map/coarse_stage/pallas_call | solution.py:325
  79.2 16.5 %collective-permute-done.6 = bf16[8,6,12,192]{3,2,1,0:T(8,128)(2,1)S(1)} collective-permute-done((bf16[8,6,12,192]{3,2,1,0:T(8,128)(2,1)}, bf16[8,6,12,192]{3,2,1,0:T(8,128)(2,1)S(1)}, u32[]{:S(2)}, u32[]{:S(2)}) %collective-permute-start.6) | collective-permute-done | bytes 221216 | tf_op jit(solution)/shard_map/ppermute | solution.py:351
  95.7 4.4 %collective-permute-done.7 = bf16[8,6,12,192]{3,2,1,0:T(8,128)(2,1)S(1)} collective-permute-done((bf16[8,6,12,192]{3,2,1,0:T(8,128)(2,1)}, bf16[8,6,12,192]{3,2,1,0:T(8,128)(2,1)S(1)}, u32[]{:S(2)}, u32[]{:S(2)}) %collective-permute-start.7) | collective-permute-done | bytes 221216 | tf_op jit(solution)/shard_map/ppermute | solution.py:353
  100.1 2.5 %fusion.1 = bf16[8,12,24,192]{3,2,1,0:T(8,128)(2,1)} fusion(bf16[8,6,12,192]{3,2,1,0:T(8,128)(2,1)} %get-tuple-element.20, bf16[8,6,12,192]{3,2,1,0:T(8,128)(2,1)S(1)} %collective-permute-done.8, bf16[8,6,12,192]{3,2,1,0:T(8,128)(2,1)S(1)} %collective-permute-done.7, bf16[8,6,12,192]{3,2,1,0:T(8,128)(2,1)S(1)} %collective-permute-done.6), kind=kLoop, calls=%fused_computation.3 | loop fusion | flops 7077888 | bytes 1769472 | tf_op jit(solution)/shard_map/jit(_roll_static)/concatenate | solution.py:409
  (62 shorter events, 6.3 us)
Async XLA Ops:
  0.0 14.9 %copy-start.9 = (f32[6,144,144]{2,1,0:T(8,128)S(1)}, f32[6,144,144]{2,1,0:T(8,128)}, u32[]{:S(2)}) copy-start(f32[6,144,144]{2,1,0:T(8,128)} %param.23) | copy-start | bytes 1492996
  0.0 14.9 %copy-start.7 = (f32[12,144,144]{2,1,0:T(8,128)S(1)}, f32[12,144,144]{2,1,0:T(8,128)}, u32[]{:S(2)}) copy-start(f32[12,144,144]{2,1,0:T(8,128)} %param.32) | copy-start | bytes 2985988
  1.9 27.4 %collective-permute-start = (bf16[8,3,18,192]{3,2,1,0:T(8,128)(2,1)}, bf16[8,3,18,192]{3,2,1,0:T(8,128)(2,1)S(1)}, u32[]{:S(2)}, u32[]{:S(2)}) collective-permute-start(bf16[8,3,18,192]{3,2,1,0:T(8,128)(2,1)} %slice.47), channel_id=1, source_target_pairs={{16,0},{32,16},{48,32},{64,48},{80,64},{96,80},{112,96},{0,112},{1... | collective-permute-start | bytes 497672 | tf_op jit(solution)/shard_map/ppermute | solution.py:353
  9.1 20.3 %collective-permute-start.1 = (bf16[8,9,6,192]{3,2,1,0:T(8,128)(2,1)}, bf16[8,9,6,192]{3,2,1,0:T(8,128)(2,1)S(1)}, u32[]{:S(2)}, u32[]{:S(2)}) collective-permute-start(bf16[8,9,6,192]{3,2,1,0:T(8,128)(2,1)} %slice.48), channel_id=1, source_target_pairs={{1,0},{2,1},{3,2},{4,3},{5,4},{6,5},{7,6},{8,7},{9,8},{10,9},{11,1... | collective-permute-start | bytes 497672 | tf_op jit(solution)/shard_map/ppermute | solution.py:354
  13.9 15.4 %collective-permute-start.2 = (bf16[8,3,6,192]{3,2,1,0:T(8,128)(2,1)}, bf16[8,3,6,192]{3,2,1,0:T(8,128)(2,1)S(1)}, u32[]{:S(2)}, u32[]{:S(2)}) collective-permute-start(bf16[8,3,6,192]{3,2,1,0:T(8,128)(2,1)} %slice.49), channel_id=1, source_target_pairs={{17,0},{18,1},{19,2},{20,3},{21,4},{22,5},{23,6},{24,7},{25,8},{26... | collective-permute-start | bytes 165896 | tf_op jit(solution)/shard_map/ppermute | solution.py:351
  15.0 2.1 %copy-start.13 = (bf16[192,576]{1,0:T(8,128)(2,1)S(1)}, bf16[192,576]{1,0:T(8,128)(2,1)}, u32[]{:S(2)}) copy-start(bf16[192,576]{1,0:T(8,128)(2,1)} %param.22) | copy-start | bytes 663556
  23.6 5.8 %copy-start = (bf16[8,12,24,192]{3,2,1,0:T(8,128)(2,1)S(1)}, bf16[8,12,24,192]{3,2,1,0:T(8,128)(2,1)}, u32[]{:S(2)}) copy-start(bf16[8,12,24,192]{3,2,1,0:T(8,128)(2,1)} %own1.1) | copy-start | bytes 2654212
  23.6 5.8 %copy-start.2 = (bf16[192,768]{1,0:T(8,128)(2,1)S(1)}, bf16[192,768]{1,0:T(8,128)(2,1)}, u32[]{:S(2)}) copy-start(bf16[192,768]{1,0:T(8,128)(2,1)} %w1.2) | copy-start | bytes 884740
  23.6 5.8 %copy-start.3 = (bf16[192,192]{1,0:T(8,128)(2,1)S(1)}, bf16[192,192]{1,0:T(8,128)(2,1)}, u32[]{:S(2)}) copy-start(bf16[192,192]{1,0:T(8,128)(2,1)} %wo.2) | copy-start | bytes 221188
  23.6 5.8 %copy-start.4 = (f32[192]{0:T(256)S(1)}, f32[192]{0:T(256)}, u32[]{:S(2)}) copy-start(f32[192]{0:T(256)} %param.21) | copy-start | bytes 2308
  23.6 5.8 %copy-start.5 = (f32[192]{0:T(256)S(1)}, f32[192]{0:T(256)}, u32[]{:S(2)}) copy-start(f32[192]{0:T(256)} %param.25) | copy-start | bytes 2308
  29.4 21.1 %copy-start.6 = (f32[144,1536]{1,0:T(8,128)S(1)}, f32[144,1536]{1,0:T(8,128)}, u32[]{:S(2)}) copy-start(f32[144,1536]{1,0:T(8,128)} %copy.38) | copy-start | bytes 2654212
  29.4 21.1 %copy-start.11 = (f32[144,192]{1,0:T(8,128)S(1)}, f32[144,192]{1,0:T(8,128)}, u32[]{:S(2)}) copy-start(f32[144,192]{1,0:T(8,128)} %copy.33) | copy-start | bytes 331780
  49.1 2.5 %copy-start.8 = (bf16[384,384]{1,0:T(8,128)(2,1)S(1)}, bf16[384,384]{1,0:T(8,128)(2,1)}, u32[]{:S(2)}) copy-start(bf16[384,384]{1,0:T(8,128)(2,1)} %get-tuple-element.21) | copy-start | bytes 884740
  49.1 3.4 %copy-start.12 = (bf16[384,768]{1,0:T(8,128)(2,1)S(1)}, bf16[384,768]{1,0:T(8,128)(2,1)}, u32[]{:S(2)}) copy-start(bf16[384,768]{1,0:T(8,128)(2,1)} %param.37) | copy-start | bytes 1769476
  49.1 11.5 %collective-permute-start.3 = (bf16[8,3,18,192]{3,2,1,0:T(8,128)(2,1)}, bf16[8,3,18,192]{3,2,1,0:T(8,128)(2,1)S(1)}, u32[]{:S(2)}, u32[]{:S(2)}) collective-permute-start(bf16[8,3,18,192]{3,2,1,0:T(8,128)(2,1)} %get-tuple-element.14), channel_id=1, source_target_pairs={{16,0},{32,16},{48,32},{64,48},{80,64},{96,80},{112,96},{0,112},{1... | collective-permute-start | bytes 497672 | tf_op jit(solution)/shard_map/ppermute | solution.py:353
  50.5 10.1 %collective-permute-start.4 = (bf16[8,9,6,192]{3,2,1,0:T(8,128)(2,1)}, bf16[8,9,6,192]{3,2,1,0:T(8,128)(2,1)S(1)}, u32[]{:S(2)}, u32[]{:S(2)}) collective-permute-start(bf16[8,9,6,192]{3,2,1,0:T(8,128)(2,1)} %get-tuple-element.15), channel_id=1, source_target_pairs={{1,0},{2,1},{3,2},{4,3},{5,4},{6,5},{7,6},{8,7},{9,8},{10,9},{11,1... | collective-permute-start | bytes 497672 | tf_op jit(solution)/shard_map/ppermute | solution.py:354
  50.5 10.1 %collective-permute-start.5 = (bf16[8,3,6,192]{3,2,1,0:T(8,128)(2,1)}, bf16[8,3,6,192]{3,2,1,0:T(8,128)(2,1)S(1)}, u32[]{:S(2)}, u32[]{:S(2)}) collective-permute-start(bf16[8,3,6,192]{3,2,1,0:T(8,128)(2,1)} %get-tuple-element.16), channel_id=1, source_target_pairs={{17,0},{18,1},{19,2},{20,3},{21,4},{22,5},{23,6},{24,7},{25,8},{26... | collective-permute-start | bytes 165896 | tf_op jit(solution)/shard_map/ppermute | solution.py:351
  51.6 2.4 %copy-start.17 = (f32[768]{0:T(1024)S(1)}, f32[768]{0:T(1024)}, u32[]{:S(2)}) copy-start(f32[768]{0:T(1024)} %param.28) | copy-start | bytes 9220
  51.6 3.1 %copy-start.18 = (f32[384]{0:T(512)S(1)}, f32[384]{0:T(512)}, u32[]{:S(2)}) copy-start(f32[384]{0:T(512)} %param.30) | copy-start | bytes 4612
  51.6 3.7 %copy-start.19 = (f32[384]{0:T(512)S(1)}, f32[384]{0:T(512)}, u32[]{:S(2)}) copy-start(f32[384]{0:T(512)} %param.34) | copy-start | bytes 4612
  79.1 16.6 %collective-permute-start.6 = (bf16[8,6,12,192]{3,2,1,0:T(8,128)(2,1)}, bf16[8,6,12,192]{3,2,1,0:T(8,128)(2,1)S(1)}, u32[]{:S(2)}, u32[]{:S(2)}) collective-permute-start(bf16[8,6,12,192]{3,2,1,0:T(8,128)(2,1)} %get-tuple-element.17), channel_id=1, source_target_pairs={{127,0},{112,1},{113,2},{114,3},{115,4},{116,5},{117,6},{118,7},{1... | collective-permute-start | bytes 663560 | tf_op jit(solution)/shard_map/ppermute | solution.py:351
  79.1 21.0 %collective-permute-start.7 = (bf16[8,6,12,192]{3,2,1,0:T(8,128)(2,1)}, bf16[8,6,12,192]{3,2,1,0:T(8,128)(2,1)S(1)}, u32[]{:S(2)}, u32[]{:S(2)}) collective-permute-start(bf16[8,6,12,192]{3,2,1,0:T(8,128)(2,1)} %get-tuple-element.18), channel_id=1, source_target_pairs={{112,0},{0,16},{16,32},{32,48},{48,64},{64,80},{80,96},{96,112},{1... | collective-permute-start | bytes 663560 | tf_op jit(solution)/shard_map/ppermute | solution.py:353
  79.2 20.9 %collective-permute-start.8 = (bf16[8,6,12,192]{3,2,1,0:T(8,128)(2,1)}, bf16[8,6,12,192]{3,2,1,0:T(8,128)(2,1)S(1)}, u32[]{:S(2)}, u32[]{:S(2)}) collective-permute-start(bf16[8,6,12,192]{3,2,1,0:T(8,128)(2,1)} %get-tuple-element.19), channel_id=1, source_target_pairs={{15,0},{0,1},{1,2},{2,3},{3,4},{4,5},{5,6},{6,7},{7,8},{8,9},{9,10... | collective-permute-start | bytes 663560 | tf_op jit(solution)/shard_map/ppermute | solution.py:354
  (5 other events, 4.4 us)
where the time goes:
time: 104 us; the launch traced here: 103 us
  Pallas kernels  36.3 us (35%)
  waiting for transfers between devices  25.6 us (25%)
  local copies, waits for them, and re-layouts  24.3 us (23%)
  starting transfers between devices  11.3 us (11%)
  other arithmetic  4.82 us (5%)
    ppermute x3, waiting for transfers between devices, shift(): return lax.ppermute(array, ('lat', 'lon'), pairs)  21.2 us
    pallas_call x1, Pallas kernels, fine_stage(): pl.pallas_call(fine_kernel, grid=(levels // WIN_P,), in_specs=specs, out_...  18.7 us
    pallas_call x1, Pallas kernels, coarse_stage(): pl.pallas_call(coarse_kernel, in_specs=[smem] + [vmem] * (len(operands) -...  17.6 us
    ppermute x3, starting transfers between devices, shift(): lax.ppermute(array, 'lat', [((i + lat_by) % lats, i) for i in range(lats)])  6.99 us
    unnamed x44, local copies, waits for them, and re-layouts  5.46 us
    reshape x2, local copies, waits for them, and re-layouts, score_table(): main = turned[:, :, :MAIN].reshape(WIN, heads * MAIN)  4.92 us
    ppermute x3, waiting for transfers between devices, shift(): lax.ppermute(array, 'lat', [((i + lat_by) % lats, i) for i in range(lats)])  4.4 us
    ppermute x3, starting transfers between devices, shift(): lax.ppermute(array, 'lon', [((i + lon_by) % lons, i) for i in range(lons)])  3.38 us
  transfers between devices with their start and end apart: 9, of which 3 were waited for; matrix products, arithmetic and copies ran while one was open for 21% of the time, Pallas kernels for 0%

commit v1 on v0

v1 whole, which is shorter than its diff:
```python
import math

import jax
import jax.numpy as jnp
from jax import lax
from jax.experimental import pallas as pl
from jax.experimental.pallas import tpu as pltpu
from jax.sharding import PartitionSpec as P

WIN_P = 2
WIN_LAT = 6
WIN_LON = 12
WIN = WIN_P * WIN_LAT * WIN_LON
HALF_LAT = WIN_LAT // 2
HALF_LON = WIN_LON // 2
HEAD = 32
MAIN = 128
REST = WIN - MAIN
EPS = 1e-05
LOG2E = math.log2(math.e)
EXCLUDED = -1e30
PITCH = 32

F32 = jnp.float32
BF16 = jnp.bfloat16


def dot(a, b, contract=((1,), (0,))):
    return lax.dot_general(a, b, (contract, ((), ())), preferred_element_type=F32)


def layer_norm(values, gain):
    average = jnp.mean(values, axis=-1, keepdims=True)
    centred = values - average
    variance = jnp.mean(centred * centred, axis=-1, keepdims=True)
    return centred * lax.rsqrt(variance + EPS) * gain


def gelu(x):
    return 0.5 * x * (1.0 + lax.erf(x * (1.0 / math.sqrt(2.0))))


def token_index(shape, heads):
    key = lax.broadcasted_iota(jnp.int32, shape, 0)
    column = lax.broadcasted_iota(jnp.int32, shape, 1)
    rest = column - heads * MAIN
    query = jnp.where(rest < 0, jnp.bitwise_and(column, MAIN - 1), MAIN + jnp.bitwise_and(rest, REST - 1))
    return key, query


def level_mask(heads):
    key, query = token_index((WIN, heads * WIN), heads)
    half = WIN // 2
    return jnp.where((key >= half) != (query >= half), EXCLUDED, 0.0)


def lat_mask(heads):
    key, query = token_index((WIN, heads * WIN), heads)
    half, quarter = WIN // 2, WIN // 4

    def late(t):
        return jnp.where(t >= half, t - half, t) >= quarter

    return jnp.where(late(key) != late(query), EXCLUDED, 0.0)


def attend(q, k, vt, table, heads):
    width = heads * HEAD
    lane = lax.broadcasted_iota(jnp.int32, (1, MAIN), 1) // HEAD
    zero = jnp.zeros((), BF16)
    pieces = []
    rests = []
    for start in range(0, width, MAIN):
        stop = min(start + MAIN, width)
        span = stop - start
        qs = q[:, start:stop]
        here = span // HEAD
        masked = [jnp.where(lane[:, :span] == h, qs, zero) for h in range(here)]
        main = jnp.concatenate([m[:MAIN] for m in masked], axis=0)
        rest = jnp.concatenate([m[MAIN:] for m in masked], axis=0)
        ks = k[:, start:stop]
        pieces.append(dot(ks, main, ((1,), (1,))))
        rests.append(dot(ks, rest, ((1,), (1,))))
    outs = []
    base = 0
    for piece in pieces:
        span = piece.shape[1]
        s = piece + table[:, base : base + span]
        s = s - jnp.max(s, axis=0, keepdims=True)
        e = jnp.exp2(s)
        inv = 1.0 / jnp.sum(e, axis=0, keepdims=True)
        p = e.astype(BF16)
        for h in range(span // MAIN):
            row = base // MAIN + h
            cut = slice(h * MAIN, (h + 1) * MAIN)
            outs.append(dot(vt[row * HEAD : (row + 1) * HEAD], p[:, cut]) * inv[:, cut])
        base += span
    main_out = jnp.concatenate(outs, axis=0)
    s = jnp.concatenate(rests, axis=1) + table[:, base:]
    s = s - jnp.max(s, axis=0, keepdims=True)
    e = jnp.exp2(s)
    inv = 1.0 / jnp.sum(e, axis=0, keepdims=True)
    full = dot(vt, e.astype(BF16)) * inv
    row = lax.broadcasted_iota(jnp.int32, full.shape, 0) // HEAD
    column = lax.broadcasted_iota(jnp.int32, full.shape, 1) // REST
    full = jnp.where(row == column, full, 0.0).astype(BF16)
    fold_row = lax.broadcasted_iota(jnp.int32, (heads * REST, REST), 0)
    fold_column = lax.broadcasted_iota(jnp.int32, (heads * REST, REST), 1)
    fold = jnp.where(jnp.bitwise_and(fold_row, REST - 1) == fold_column, 1.0, 0.0).astype(BF16)
    rest_out = dot(full, fold)
    return jnp.concatenate([main_out.astype(BF16), rest_out.astype(BF16)], axis=1)


def block_rows(x_ref, count, table_ref, heads, gain_one, wq, wk, wvt, wo, gain_two, w1, w2, w2_dims, out_ref):
    x = x_ref[...]
    xn = layer_norm(x, gain_one[...][None, :]).astype(BF16)
    q = (dot(xn, wq) * (LOG2E / math.sqrt(HEAD))).astype(BF16)
    k = dot(xn, wk).astype(BF16)
    mixed = []
    for w in range(count):
        rows = slice(w * WIN, (w + 1) * WIN)
        vt = dot(wvt, xn[rows], ((1,), (1,))).astype(BF16)
        table = table_ref.at[1 if w == count - 1 else 0]
        attended = attend(q[rows], k[rows], vt, table, heads)
        mixed.append(dot(attended, wo[...], ((0,), (0,))))
    after = (x + jnp.concatenate(mixed, axis=0)).astype(BF16).astype(F32)
    normed = layer_norm(after, gain_two[...][None, :]).astype(BF16)
    hidden = gelu(dot(normed, w1[...])).astype(BF16)
    out_ref[...] = (after + dot(hidden, w2[...], w2_dims)).astype(BF16).astype(F32)


class Packed:
    def __init__(self, low_ref, high_ref, rows):
        self.low, self.high, self.rows = low_ref, high_ref, rows
        self.pairs = low_ref.shape[0]

    def put(self, p, at, value):
        n = value.shape[0]
        self.low[p, at : at + n, :] = value[:, :MAIN]
        self.high[p, at : at + n, : value.shape[1] - MAIN] = value[:, MAIN:]

    def get(self, p, at, n):
        return jnp.concatenate([self.low[p, at : at + n, :], self.high[p, at : at + n, : MAIN // 2]], axis=1)

    def store(self, out_ref):
        half = self.pairs // 2
        rows = slice(0, self.rows)
        for p in range(self.pairs):
            out_ref[p] = self.low[p, rows, :].astype(BF16)
        for p in range(half):
            sides = [self.high[p + s * half, rows, : MAIN // 2] for s in range(2)]
            out_ref[self.pairs + p] = jnp.concatenate(sides, axis=1).astype(BF16)

    def load(self, in_ref):
        half = self.pairs // 2
        rows = slice(0, self.rows)
        for p in range(self.pairs):
            self.low[p, rows, :] = in_ref[p].astype(F32)
        for p in range(half):
            both = in_ref[self.pairs + p].astype(F32)
            for s in range(2):
                self.high[p + s * half, rows, : MAIN // 2] = both[:, s * MAIN // 2 : (s + 1) * MAIN // 2]
        return self


def packed_rows(tokens):
    return -(-tokens // 16) * 16


def pair_levels(p, levels):
    return [(WIN_P * p + WIN_P // 2 + lev) % levels for lev in range(WIN_P)]


def start_kernel(field, lat_ref, lon_ref, diag_ref, line_ref, low_ref, high_ref):
    levels, rows, columns, _ = field.shape
    packs = [Packed(low_ref.at[n], high_ref.at[n], ref.shape[1]) for n, ref in enumerate((lat_ref, lon_ref, diag_ref))]
    lat, lon, diag = packs
    for p in range(levels // WIN_P):
        for lev, level in enumerate(pair_levels(p, levels)):
            for r in range(rows):
                line = field[level, r].astype(F32)
                if r < HALF_LAT:
                    slot = level * HALF_LAT + r
                    line_ref[slot] = line
                    diag.put(p, (lev * HALF_LAT + r) * HALF_LON, line[:HALF_LON])
                    span = columns - HALF_LON
                    lat.put(p, (lev * HALF_LAT + r) * span, line_ref[slot, HALF_LON:, :])
                else:
                    lon.put(p, (lev * (rows - HALF_LAT) + r - HALF_LAT) * HALF_LON, line[:HALF_LON])
    for pack, ref in zip(packs, (lat_ref, lon_ref, diag_ref)):
        pack.store(ref)


def table_kernel(edge_ref, a_bias, b_bias, project, plain_ref, late_ref, coarse_ref, wq_ref, wk_ref, wvt_ref):
    edge = edge_ref[0].astype(F32)
    for bias, out in ((a_bias, plain_ref), (b_bias, coarse_ref)):
        heads = bias.shape[0]
        for h in range(heads):
            turned = (bias[h] * LOG2E).T
            out[0, :, h * MAIN : (h + 1) * MAIN] = turned[:, :MAIN]
            out[0, :, heads * MAIN + h * REST : heads * MAIN + (h + 1) * REST] = turned[:, MAIN:]
        level = level_mask(heads)
        late = lat_mask(heads) * edge
        if out is coarse_ref:
            out[0] = out[0] + late
        else:
            late_ref[0] = out[0] + late
            late_ref[1] = late_ref[0] + level
        out[1] = out[0] + level
    width = wq_ref.shape[0]
    wq_ref[...] = project[:, :width]
    wk_ref[...] = project[:, width : 2 * width]
    wvt_ref[...] = project[:, 2 * width :].astype(F32).T.astype(BF16)


def fine_kernel(i, j, *refs):
    refs = list(refs)
    field = refs.pop(0)
    lat_in = refs.pop(0) if i else None
    lon_in = refs.pop(0) if j else None
    diag_in = refs.pop(0) if i and j else None
    first = refs.pop(0) if i != j else None
    table_ref, gain_one, wq, wk, wvt, wo, gain_two, w1, w2t, out_ref = refs[:10]
    refs = refs[10:]
    send_ref = None if i and j else refs.pop(0)
    line_ref, x_ref, low_ref, high_ref = refs
    levels, rows, columns, _ = field.shape
    pairs = levels // WIN_P
    lat, lon, diag = [
        Packed(low_ref.at[n], high_ref.at[n], ref.shape[1]).load(ref) if ref is not None else None
        for n, ref in enumerate((lat_in, lon_in, diag_in))
    ]
    at = 0
    slot = 0
    for p in range(pairs):
        for lev, level in enumerate(pair_levels(p, levels)):
            for row in range(i * WIN_LAT, (i + 1) * WIN_LAT):
                start = HALF_LON + j * WIN_LON
                own = min(columns - start, WIN_LON)
                if row + HALF_LAT < rows:
                    line_ref[slot] = field[level, row + HALF_LAT].astype(F32)
                    x_ref[at : at + own, :] = line_ref[slot, start : start + own, :]
                    slot += 1
                    if own < WIN_LON:
                        x_ref[at + own : at + WIN_LON, :] = lon.get(p, (lev * (rows - HALF_LAT) + row) * HALF_LON, HALF_LON)
                else:
                    below = lev * HALF_LAT + row + HALF_LAT - rows
                    x_ref[at : at + own, :] = lat.get(p, below * (columns - HALF_LON) + j * WIN_LON, own)
                    if own < WIN_LON:
                        x_ref[at + own : at + WIN_LON, :] = diag.get(p, below * HALF_LON, HALF_LON)
                at += WIN_LON
    block_rows(
        x_ref, pairs, table_ref, 6, gain_one, wq[...], wk[...], wvt[...], wo, gain_two, w1, w2t, ((1,), (1,)), out_ref
    )
    if send_ref is None:
        return
    send = Packed(low_ref.at[3], high_ref.at[3], send_ref.shape[1])
    for p in range(pairs):
        at = 0
        for lev in range(WIN_P):
            base = (p * WIN_P + lev) * WIN_LAT * WIN_LON
            if not i:
                for row in range(HALF_LAT):
                    here = base + row * WIN_LON
                    if j:
                        send.put(p, at, first[here + HALF_LON : here + WIN_LON, :])
                        send.put(p, at + HALF_LON, out_ref[here : here + WIN_LON, :])
                        at += WIN_LON + HALF_LON
                    else:
                        send.put(p, at, out_ref[here : here + HALF_LON, :])
                        at += HALF_LON
            else:
                for row in range(HALF_LAT, rows):
                    source, here = (first, row) if row < WIN_LAT else (out_ref, row - WIN_LAT)
                    here = base + here * WIN_LON
                    send.put(p, at, source[here : here + HALF_LON, :])
                    at += HALF_LON
    send.store(send_ref)


def coarse_kernel(
    w00, w01, w10, w11, lat_in, lon_in, diag_in, table_ref,
    merge_gain, merge_weight,
    gain_one, project, wo, gain_two, w1, w2,
    up_first, up_norm, up_second,
    stay_ref, to_lat_ref, to_lon_ref, to_diag_ref,
    low_ref, high_ref, grid_low, grid_high, quad_low, quad_high, parts_ref, x_ref, y_ref,
):
    heads = 12
    width = w00.shape[1]
    rows, columns = 2 * WIN_LAT, 2 * WIN_LON
    pairs = w00.shape[0] // WIN
    levels = pairs * WIN_P
    windows = ((w00, w01), (w10, w11))
    lat, lon, diag = [
        Packed(low_ref.at[n], high_ref.at[n], ref.shape[1]).load(ref) for n, ref in enumerate((lat_in, lon_in, diag_in))
    ]

    def put(at, value):
        grid_low[at : at + value.shape[0], :] = value[:, :MAIN]
        grid_high[at : at + value.shape[0], : width - MAIN] = value[:, MAIN:]

    for p in range(pairs):
        for lev in range(WIN_P):
            for row in range(rows):
                at = ((p * WIN_P + lev) * rows + row) * PITCH
                if row + HALF_LAT < rows:
                    left, right = windows[(row + HALF_LAT) // WIN_LAT]
                    here = ((p * WIN_P + lev) * WIN_LAT + (row + HALF_LAT) % WIN_LAT) * WIN_LON
                    put(at + HALF_LON, left[here + HALF_LON : here + WIN_LON, :])
                    put(at + WIN_LON, right[here : here + WIN_LON, :])
                    put(at + columns, lon.get(p, (lev * (rows - HALF_LAT) + row) * HALF_LON, HALF_LON))
                else:
                    below = lev * HALF_LAT + row + HALF_LAT - rows
                    span = columns - HALF_LON
                    put(at + HALF_LON, lat.get(p, below * span, span))
                    put(at + columns, diag.get(p, below * HALF_LON, HALF_LON))
    for r in range(2):
        for t in range(2):
            n = 2 * r + t
            at = 0
            for level in range(levels):
                for a in range(rows // 2):
                    start = (level * rows + 2 * a + r) * PITCH + HALF_LON + t
                    parts_ref[n, at : at + WIN_LON, :MAIN] = grid_low[pl.ds(start, WIN_LON, stride=2), :]
                    parts_ref[n, at : at + WIN_LON, MAIN:] = grid_high[pl.ds(start, WIN_LON, stride=2), :]
                    at += WIN_LON
    parts = [parts_ref[n, :, :width] for n in range(4)]
    average = jnp.sum(parts[0] + parts[1] + parts[2] + parts[3], axis=-1, keepdims=True) * (1.0 / (4 * width))
    centred = [part - average for part in parts]
    squares = centred[0] * centred[0]
    for c in centred[1:]:
        squares += c * c
    scale = lax.rsqrt(jnp.sum(squares, axis=-1, keepdims=True) * (1.0 / (4 * width)) + EPS)
    total = None
    for n in range(4):
        gain = merge_gain[n * width : (n + 1) * width][None, :]
        normed = (centred[n] * scale * gain).astype(BF16)
        term = dot(normed, merge_weight[n * width : (n + 1) * width, :])
        total = term if total is None else total + term
    x_ref[...] = total.astype(BF16).astype(F32)
    double = 2 * width
    wvt = project[:, 2 * double :].astype(F32).T.astype(BF16)
    block_rows(
        x_ref, pairs, table_ref, heads, gain_one, project[:, :double], project[:, double : 2 * double], wvt,
        wo, gain_two, w1, w2, ((1,), (0,)), y_ref,
    )
    coarse = y_ref[...].astype(BF16)
    half = rows // 2
    for r in range(2):
        for t in range(2):
            n = 2 * r + t
            raised = dot(coarse, up_first[:, n * width : (n + 1) * width]).astype(BF16).astype(F32)
            normed = layer_norm(raised, up_norm[...][None, :]).astype(BF16)
            parts_ref[n, :, :width] = parts_ref[n, :, :width] + dot(normed, up_second[...])
            for level in range(levels):
                for a in range(half):
                    row = 2 * a + r
                    for side in range(2):
                        at = (level * half + a) * WIN_LON + side * HALF_LON
                        quad, p = 2 * (row // half) + side, level // WIN_P
                        start = (level % WIN_P * half + row % half) * WIN_LON + t
                        to = pl.ds(start, HALF_LON, stride=2)
                        quad_low[quad, p, to, :] = parts_ref[n, at : at + HALF_LON, :MAIN]
                        quad_high[quad, p, to, :] = parts_ref[n, at : at + HALF_LON, MAIN:]
    for quad, ref in enumerate((stay_ref, to_lon_ref, to_lat_ref, to_diag_ref)):
        Packed(quad_low.at[quad], quad_high.at[quad], WIN).store(ref)


def finish_kernel(upper_left, upper_right, lower_left, lower_right, out_ref, low_ref, high_ref, line_low, line_high):
    levels, rows, columns, width = out_ref.shape
    half = rows // 2
    for quad, ref in enumerate((upper_left, upper_right, lower_left, lower_right)):
        pack = Packed(low_ref.at[quad], high_ref.at[quad], WIN).load(ref)
        for p in range(levels // WIN_P):
            for lev, level in enumerate(pair_levels(p, levels)):
                for row in range(half):
                    at = (level * rows + (quad // 2) * half + row) * columns + quad % 2 * WIN_LON
                    here = (lev * half + row) * WIN_LON
                    line_low[at : at + WIN_LON, :] = pack.low[p, here : here + WIN_LON, :]
                    line_high[at : at + WIN_LON, :] = pack.high[p, here : here + WIN_LON, :]
    for level in range(levels):
        for row in range(rows):
            at = (level * rows + row) * columns
            out_ref[level, row, :, :MAIN] = line_low[at : at + columns, :].astype(BF16)
            out_ref[level, row, :, MAIN:] = line_high[at : at + columns, : width - MAIN].astype(BF16)


MIB = 1024 * 1024


def call(kernel, name, operands, outs, scratch, limit, flops=0, scalars=0):
    vmem = pl.BlockSpec(memory_space=pltpu.VMEM)
    smem = pl.BlockSpec(memory_space=pltpu.SMEM)
    moved = sum(x.size * x.dtype.itemsize for x in operands) + sum(math.prod(s) * jnp.dtype(d).itemsize for s, d in outs)
    return pl.pallas_call(
        kernel,
        in_specs=[smem] * scalars + [vmem] * (len(operands) - scalars),
        out_specs=[vmem] * len(outs),
        out_shape=[jax.ShapeDtypeStruct(s, d) for s, d in outs],
        scratch_shapes=[pltpu.VMEM(s, F32) for s in scratch],
        compiler_params=pltpu.CompilerParams(vmem_limit_bytes=limit * MIB),
        cost_estimate=pl.CostEstimate(flops=flops, bytes_accessed=moved, transcendentals=0),
        name=name,
    )(*operands)


def packed_shape(tokens, pairs):
    return (pairs * 3 // 2, packed_rows(tokens), MAIN)


def shift(array, lat_by, lon_by):
    lats, lons = lax.axis_size("lat"), lax.axis_size("lon")
    if lat_by and lon_by:
        pairs = [
            (((a + lat_by) % lats) * lons + (b + lon_by) % lons, a * lons + b)
            for a in range(lats)
            for b in range(lons)
        ]
        return lax.ppermute(array, ("lat", "lon"), pairs)
    if lat_by:
        return lax.ppermute(array, "lat", [((i + lat_by) % lats, i) for i in range(lats)])
    return lax.ppermute(array, "lon", [((i + lon_by) % lons, i) for i in range(lons)])


def body(
    field, a_norm_one, a_project, a_bias, a_output, a_norm_two, a_raise, a_lower,
    merge_norm_gain, merge_weight,
    b_norm_one, b_project, b_bias, b_output, b_norm_two, b_raise, b_lower,
    up_first, up_norm, up_second,
):
    levels, rows, columns, width = field.shape
    pairs = levels // WIN_P
    lat_tokens = WIN_P * HALF_LAT * (columns - HALF_LON)
    lon_tokens = WIN_P * (rows - HALF_LAT) * HALF_LON
    diag_tokens = WIN_P * HALF_LAT * HALF_LON
    lat_shape, lon_shape, diag_shape = [packed_shape(n, pairs) for n in (lat_tokens, lon_tokens, diag_tokens)]
    halo_rows = max(lat_shape[1], lon_shape[1])
    tokens = pairs * WIN

    edge = (lax.axis_index("lat") == lax.axis_size("lat") - 1).astype(jnp.int32).reshape(1)
    staging = (3, pairs, halo_rows, MAIN)
    lat, lon, diag = call(
        start_kernel, "start", [field],
        [(lat_shape, BF16), (lon_shape, BF16), (diag_shape, BF16)],
        [(levels * HALF_LAT, columns, width), staging, staging], 16,
    )
    lon = shift(lon, 0, 1)
    lat = shift(lat, 1, 0)
    diag = shift(diag, 1, 1)
    a_heads, b_heads = a_bias.shape[0], b_bias.shape[0]
    square = ((width, width), BF16)
    plain, late, coarse_table, wq, wk, wvt = call(
        table_kernel, "tables", [edge, a_bias, b_bias, a_project],
        [((2, WIN, a_heads * WIN), F32)] * 2 + [((2, WIN, b_heads * WIN), F32)] + [square] * 3,
        [], 24, scalars=1,
    )
    weights = [a_norm_one, wq, wk, wvt, a_output, a_norm_two, a_raise, a_lower.T]
    staging = (4, pairs, halo_rows, MAIN)
    scratch = [(levels * WIN_LAT, columns, width), (tokens, width), staging, staging]
    out = ((tokens, width), F32)
    work = 2 * tokens * width * (4 * width + 8 * width)

    def fine(i, j, halos, outs):
        def kernel(*refs):
            fine_kernel(i, j, *refs)

        operands = [field, *halos, late if i else plain, *weights]
        return call(kernel, f"fine_{i}{j}", operands, [out] + outs, scratch, 24, work)

    w00, diag_two = fine(0, 0, [], [(diag_shape, BF16)])
    diag_two = shift(diag_two, 1, 1)
    w01, lat_two = fine(0, 1, [lon, w00], [(lat_shape, BF16)])
    lat_two = shift(lat_two, 1, 0)
    w10, lon_two = fine(1, 0, [lat, w00], [(lon_shape, BF16)])
    lon_two = shift(lon_two, 0, 1)
    (w11,) = fine(1, 1, [lat, lon, diag], [])

    quarter = packed_shape(WIN, pairs)
    halos = (3, pairs, halo_rows, MAIN)
    quads = (4, pairs, WIN, MAIN)
    lines = (levels * rows * PITCH, MAIN)
    stay, lat, lon, diag = call(
        coarse_kernel, "coarse",
        [
            w00, w01, w10, w11, lat_two, lon_two, diag_two, coarse_table, merge_norm_gain, merge_weight,
            b_norm_one, b_project, b_output, b_norm_two, b_raise, b_lower, up_first, up_norm, up_second,
        ],
        [(quarter, BF16)] * 4,
        [halos, halos, lines, lines, quads, quads, (4, tokens, 2 * MAIN), (tokens, 2 * width), (tokens, 2 * width)],
        48, 8 * work,
    )
    diag = shift(diag, -1, -1)
    lat = shift(lat, -1, 0)
    lon = shift(lon, 0, -1)
    lines = (levels * rows * columns, MAIN)
    (fine_out,) = call(
        finish_kernel, "finish", [diag, lat, lon, stay], [(field.shape, BF16)], [quads, quads, lines, lines], 24
    )
    return fine_out


def solution(mesh):
    in_specs = (P(None, "lat", "lon", None),) + (P(),) * 19
    out_specs = P(None, "lat", "lon", None)
    return jax.shard_map(body, mesh=mesh, in_specs=in_specs, out_specs=out_specs, check_vma=False)
```

time: 104 us -> 72.2 us (0.69); the launches traced: 103 us -> 72 us
  local copies, waits for them, and re-layouts: 24.3 us -> 2.83 us
  waiting for transfers between devices: 25.6 us -> 18.5 us
  other arithmetic: 4.82 us -> 0 us
  starting transfers between devices: 11.3 us -> 13.5 us
    reshape x8 -> x0, local copies, waits for them, and re-layouts: 9.69 us -> none  [the longest x2 4.92 us: score_table(): main = turned[:, :, :MAIN].reshape(WIN, heads * MAIN)]
    slice x9 -> x0, local copies, waits for them, and re-layouts: 9.15 us -> none  [the longest x2 2.27 us: score_table(): main = turned[:, :, :MAIN].reshape(WIN, heads * MAIN)]
    ppermute x3, waiting for transfers between devices: 21.2 us -> 14.8 us  [shift(): return lax.ppermute(array, ('lat', 'lon'), pairs)]
    concatenate x3 -> x0, other arithmetic: 4.58 us -> none  [the longest x1 2.48 us: body(): return jnp.roll(jnp.concatenate([upper, lower], axis=1), WIN_P // 2, axis=0)]
    unnamed x44 -> x40, local copies, waits for them, and re-layouts: 5.46 us -> 2.83 us
    ppermute x3, starting transfers between devices: 3.38 us -> 4.9 us  [shift(): lax.ppermute(array, 'lon', [((i + lon_by) % lons, i) for i in range(lons)])]
    ppermute x3, starting transfers between devices: 0.93 us -> 2.42 us  [shift(): return lax.ppermute(array, ('lat', 'lon'), pairs)]
    ppermute x3, waiting for transfers between devices: 4.4 us -> 2.93 us  [shift(): lax.ppermute(array, 'lat', [((i + lat_by) % lats, i) for i in range(lats)])]
  transfers between devices with their start and end apart: 9 -> 9, of which waited for: 3 -> 4; matrix products, arithmetic and copies ran while one was open for 21% -> 0% of each run, Pallas kernels for 0% -> 27%
where the time goes in v1:
time: 72.2 us; the launch traced here: 72 us
  Pallas kernels  37 us (51%)
  waiting for transfers between devices  18.5 us (26%)
  starting transfers between devices  13.5 us (19%)
  local copies, waits for them, and re-layouts  2.83 us (4%)
    pallas_call x8, Pallas kernels, call(): pl.pallas_call(kernel, in_specs=[smem] * scalars + [vmem] * (len(operands...  37 us
    ppermute x3, waiting for transfers between devices, shift(): return lax.ppermute(array, ('lat', 'lon'), pairs)  14.8 us
    ppermute x3, starting transfers between devices, shift(): lax.ppermute(array, 'lat', [((i + lat_by) % lats, i) for i in range(lats)])  6.17 us
    ppermute x3, starting transfers between devices, shift(): lax.ppermute(array, 'lon', [((i + lon_by) % lons, i) for i in range(lons)])  4.9 us
    ppermute x3, waiting for transfers between devices, shift(): lax.ppermute(array, 'lat', [((i + lat_by) % lats, i) for i in range(lats)])  2.93 us
    unnamed x40, local copies, waits for them, and re-layouts  2.83 us
    ppermute x3, starting transfers between devices, shift(): return lax.ppermute(array, ('lat', 'lon'), pairs)  2.42 us
  transfers between devices with their start and end apart: 9, of which 4 were waited for; matrix products, arithmetic and copies ran while one was open for 0% of the time, Pallas kernels for 27%

profile of v1, /device:TPU:0, one launch (start us, length us, event | category | flops | bytes accessed | tf_op | source)
XLA Modules:
  0.0 72.0 jit_solution(3944190288407912591)
XLA Ops:
  0.0 1.3 %copy-done = bf16[8,12,24,192]{3,2,1,0:T(8,128)(2,1)S(1)} copy-done((bf16[8,12,24,192]{3,2,1,0:T(8,128)(2,1)S(1)}, bf16[8,12,24,192]{3,2,1,0:T(8,128)(2,1)}, u32[]{:S(2)}) %copy-start) | copy-done | bytes 884760
  1.3 0.2 start.1
  1.5 4.6 %collective-permute-start = (bf16[6,112,128]{2,1,0:T(8,128)(2,1)S(1)}, bf16[6,112,128]{2,1,0:T(8,128)(2,1)S(1)}, u32[]{:S(2)}, u32[]{:S(2)}) collective-permute-start(bf16[6,112,128]{2,1,0:T(8,128)(2,1)S(1)} %get-tuple-element.29), channel_id=1, source_target_pairs={{1,0},{2,1},{3,2},{4,3},{5,4},{6,5},{7,6},{8,7},{9,8},{10,9},{11,1... | collective-permute-start | bytes 516104 | tf_op jit(solution)/shard_map/ppermute | solution.py:423
  6.1 5.1 %collective-permute-start.1 = (bf16[6,112,128]{2,1,0:T(8,128)(2,1)S(1)}, bf16[6,112,128]{2,1,0:T(8,128)(2,1)S(1)}, u32[]{:S(2)}, u32[]{:S(2)}) collective-permute-start(bf16[6,112,128]{2,1,0:T(8,128)(2,1)S(1)} %get-tuple-element.31), channel_id=1, source_target_pairs={{16,0},{32,16},{48,32},{64,48},{80,64},{96,80},{112,96},{0,112},{1... | collective-permute-start | bytes 516104 | tf_op jit(solution)/shard_map/ppermute | solution.py:422
  11.2 1.5 %copy-done.4 = f32[12,144,144]{2,1,0:T(8,128)S(1)} copy-done((f32[12,144,144]{2,1,0:T(8,128)S(1)}, f32[12,144,144]{2,1,0:T(8,128)}, u32[]{:S(2)}) %copy-start.4) | copy-done | bytes 995352
  12.7 0.0 copy-start.9
  12.8 1.5 %tables.1 = (f32[2,144,864]{2,1,0:T(8,128)S(1)}, f32[2,144,864]{2,1,0:T(8,128)S(1)}, f32[2,144,1728]{2,1,0:T(8,128)S(1)}, bf16[192,192]{1,0:T(8,128)(2,1)S(1)}, ...) custom-call(s32[1]{0:T(128)} %bitcast.edge_ref, f32[6,144,144]{2,1,0:T(8,128)S(1)} %copy-done.6, ...), custom_call_target="tpu_custom_call" | custom-call | bytes 5916676 | tf_op jit(solution)/shard_map/tables/pallas_call | solution.py:396
  14.4 4.4 %fine_00.1 = (f32[576,192]{1,0:T(8,128)S(1)}, bf16[6,48,128]{2,1,0:T(8,128)(2,1)S(1)}) custom-call(bf16[8,12,24,192]{3,2,1,0:T(8,128)(2,1)S(1)} %copy-done.1, f32[2,144,864]{2,1,0:T(8,128)S(1)} %get-tuple-element.24.refs_1_.refs_3_, f32[192]{0:T(256)S(1)} %copy-done.8, bf16[192,192]{1,0:T(8,128)(2,1)S(1)} %get-tuple-element.25.refs_3_.refs_5_.refs_6_, ...), custom_call_target="tpu_custom_call" | custom-call | flops 509607936 | bytes 3282432 | tf_op jit(solution)/shard_map/fine_00/pallas_call | solution.py:396
  18.8 4.5 %fine_01.1 = (f32[576,192]{1,0:T(8,128)S(1)}, bf16[6,112,128]{2,1,0:T(8,128)(2,1)S(1)}) custom-call(bf16[8,12,24,192]{3,2,1,0:T(8,128)(2,1)S(1)} %copy-done.1, bf16[6,112,128]{2,1,0:T(8,128)(2,1)S(1)} %collective-permute-done.refs_1_.refs_2_, f32[576,192]{1,0:T(8,128)S(1)} %get-tuple-element.28.refs_2_.w00, ...), custom_call_target="tpu_custom_call" | custom-call | flops 509607936 | bytes 3995136 | tf_op jit(solution)/shard_map/fine_01/pallas_call | solution.py:396
  23.3 1.1 %collective-permute-start.3 = (bf16[6,112,128]{2,1,0:T(8,128)(2,1)S(1)}, bf16[6,112,128]{2,1,0:T(8,128)(2,1)S(1)}, u32[]{:S(2)}, u32[]{:S(2)}) collective-permute-start(bf16[6,112,128]{2,1,0:T(8,128)(2,1)S(1)} %get-tuple-element.35), channel_id=1, source_target_pairs={{16,0},{32,16},{48,32},{64,48},{80,64},{96,80},{112,96},{0,112},{1... | collective-permute-start | bytes 516104 | tf_op jit(solution)/shard_map/ppermute | solution.py:422
  24.4 4.5 %fine_10.1 = (f32[576,192]{1,0:T(8,128)S(1)}, bf16[6,112,128]{2,1,0:T(8,128)(2,1)S(1)}) custom-call(bf16[8,12,24,192]{3,2,1,0:T(8,128)(2,1)S(1)} %copy-done.1, bf16[6,112,128]{2,1,0:T(8,128)(2,1)S(1)} %collective-permute-done.1.refs_1_, f32[576,192]{1,0:T(8,128)S(1)} %get-tuple-element.28.refs_2_.w00, f32[2,144,864]{2,1,0:T(8,128)S(1)} %get-tuple-element.32.refs_3_.refs_4_, ...), custom_call_target="tpu_custom_call" | custom-call | flops 509607936 | bytes 3995136 | tf_op jit(solution)/shard_map/fine_10/pallas_call | solution.py:396
  28.9 0.1 collective-permute-start.4
  29.0 0.1 collective-permute-start.2
  29.1 0.0 copy-start.15
  29.2 0.3 collective-permute-start.5
  29.5 4.1 %collective-permute-done.2.refs_3_ = bf16[6,48,128]{2,1,0:T(8,128)(2,1)S(1)} collective-permute-done((bf16[6,48,128]{2,1,0:T(8,128)(2,1)S(1)}, bf16[6,48,128]{2,1,0:T(8,128)(2,1)S(1)}, u32[]{:S(2)}, u32[]{:S(2)}) %collective-permute-start.2) | collective-permute-done | bytes 73760 | tf_op jit(solution)/shard_map/ppermute | solution.py:420
  33.6 4.5 %fine_11.1.w11 = f32[576,192]{1,0:T(8,128)S(1)} custom-call(bf16[8,12,24,192]{3,2,1,0:T(8,128)(2,1)S(1)} %copy-done.1, bf16[6,112,128]{2,1,0:T(8,128)(2,1)S(1)} %collective-permute-done.1.refs_1_, bf16[6,112,128]{2,1,0:T(8,128)(2,1)S(1)} %collective-permute-done.refs_1_.refs_2_, bf16[6,48,128]{2,1,0:T(8,128)(2,1)S(1)} %collective-permute-done.2.refs_3_, ...), custom_call_target="tpu_custom_call" | custom-call | flops 509607936 | bytes 3626496 | tf_op jit(solution)/shard_map/fine_11/pallas_call | solution.py:396
  38.2 15.7 %coarse.1 = (bf16[6,144,128]{2,1,0:T(8,128)(2,1)S(1)}, bf16[6,144,128]{2,1,0:T(8,128)(2,1)S(1)}, bf16[6,144,128]{2,1,0:T(8,128)(2,1)S(1)}, bf16[6,144,128]{2,1,0:T(8,128)(2,1)S(1)}) custom-call(f32[576,192]{1,0:T(8,128)S(1)} %get-tuple-element.28.refs_2_.w00, f32[576,192]{1,0:T(8,128)S(1)} %get-tuple-element.30.w01, f32[576,192]{1,0:T(8,128)S(1)} %get-tuple-element.33.w10, ...), custom_call_target="tpu_custom_call" | custom-call | flops 4076863488 | bytes 9861888 | tf_op jit(solution)/shard_map/coarse/pallas_call | solution.py:396
  53.8 2.0 %collective-permute-start.6 = (bf16[6,144,128]{2,1,0:T(8,128)(2,1)S(1)}, bf16[6,144,128]{2,1,0:T(8,128)(2,1)S(1)}, u32[]{:S(2)}, u32[]{:S(2)}) collective-permute-start(bf16[6,144,128]{2,1,0:T(8,128)(2,1)S(1)} %get-tuple-element.39), channel_id=1, source_target_pairs={{127,0},{112,1},{113,2},{114,3},{115,4},{116,5},{117,6},{118,7},{1... | collective-permute-start | bytes 663560 | tf_op jit(solution)/shard_map/ppermute | solution.py:420
  55.9 0.2 collective-permute-start.8
  56.1 10.7 %collective-permute-done.6.upper_left = bf16[6,144,128]{2,1,0:T(8,128)(2,1)S(1)} collective-permute-done((bf16[6,144,128]{2,1,0:T(8,128)(2,1)S(1)}, bf16[6,144,128]{2,1,0:T(8,128)(2,1)S(1)}, u32[]{:S(2)}, u32[]{:S(2)}) %collective-permute-start.6) | collective-permute-done | bytes 221216 | tf_op jit(solution)/shard_map/ppermute | solution.py:420
  66.8 2.9 %collective-permute-done.7.upper_right = bf16[6,144,128]{2,1,0:T(8,128)(2,1)S(1)} collective-permute-done((bf16[6,144,128]{2,1,0:T(8,128)(2,1)S(1)}, bf16[6,144,128]{2,1,0:T(8,128)(2,1)S(1)}, u32[]{:S(2)}, u32[]{:S(2)}) %collective-permute-start.7) | collective-permute-done | bytes 221216 | tf_op jit(solution)/shard_map/ppermute | solution.py:422
  69.7 0.7 %collective-permute-done.8.lower_left = bf16[6,144,128]{2,1,0:T(8,128)(2,1)S(1)} collective-permute-done((bf16[6,144,128]{2,1,0:T(8,128)(2,1)S(1)}, bf16[6,144,128]{2,1,0:T(8,128)(2,1)S(1)}, u32[]{:S(2)}, u32[]{:S(2)}) %collective-permute-start.8) | collective-permute-done | bytes 221216 | tf_op jit(solution)/shard_map/ppermute | solution.py:423
  70.4 1.6 %finish.1 = bf16[8,12,24,192]{3,2,1,0:T(8,128)(2,1)} custom-call(bf16[6,144,128]{2,1,0:T(8,128)(2,1)S(1)} %collective-permute-done.6.upper_left, bf16[6,144,128]{2,1,0:T(8,128)(2,1)S(1)} %collective-permute-done.7.upper_right, bf16[6,144,128]{2,1,0:T(8,128)(2,1)S(1)} %collective-permute-done.8.lower_left, bf16[6,144,128]{2,1,0:T(8,128)(2,1)S(1)} %get-tuple-element.42.lower_right), custom_call_target="tpu_custom_call" | custom-call | bytes 1769472 | tf_op jit(solution)/shard_map/finish/pallas_call | solution.py:396
  (42 shorter events, 0.1 us)
Async XLA Ops:
  1.3 10.0 %copy-start.6 = (f32[6,144,144]{2,1,0:T(8,128)S(1)}, f32[6,144,144]{2,1,0:T(8,128)}, u32[]{:S(2)}) copy-start(f32[6,144,144]{2,1,0:T(8,128)} %a_bias.1) | copy-start | bytes 1492996
  1.3 10.0 %copy-start.7 = (bf16[192,576]{1,0:T(8,128)(2,1)S(1)}, bf16[192,576]{1,0:T(8,128)(2,1)}, u32[]{:S(2)}) copy-start(bf16[192,576]{1,0:T(8,128)(2,1)} %project.2) | copy-start | bytes 663556
  1.5 17.3 %collective-permute-start = (bf16[6,112,128]{2,1,0:T(8,128)(2,1)S(1)}, bf16[6,112,128]{2,1,0:T(8,128)(2,1)S(1)}, u32[]{:S(2)}, u32[]{:S(2)}) collective-permute-start(bf16[6,112,128]{2,1,0:T(8,128)(2,1)S(1)} %get-tuple-element.29), channel_id=1, source_target_pairs={{1,0},{2,1},{3,2},{4,3},{5,4},{6,5},{7,6},{8,7},{9,8},{10,9},{11,1... | collective-permute-start | bytes 516104 | tf_op jit(solution)/shard_map/ppermute | solution.py:423
  6.1 18.3 %collective-permute-start.1 = (bf16[6,112,128]{2,1,0:T(8,128)(2,1)S(1)}, bf16[6,112,128]{2,1,0:T(8,128)(2,1)S(1)}, u32[]{:S(2)}, u32[]{:S(2)}) collective-permute-start(bf16[6,112,128]{2,1,0:T(8,128)(2,1)S(1)} %get-tuple-element.31), channel_id=1, source_target_pairs={{16,0},{32,16},{48,32},{64,48},{80,64},{96,80},{112,96},{0,112},{1... | collective-permute-start | bytes 516104 | tf_op jit(solution)/shard_map/ppermute | solution.py:422
  12.7 1.6 %copy-start.5 = (bf16[192,192]{1,0:T(8,128)(2,1)S(1)}, bf16[192,192]{1,0:T(8,128)(2,1)}, u32[]{:S(2)}) copy-start(bf16[192,192]{1,0:T(8,128)(2,1)} %refs_9_.5) | copy-start | bytes 221188
  12.7 1.6 %copy-start.8 = (f32[192]{0:T(256)S(1)}, f32[192]{0:T(256)}, u32[]{:S(2)}) copy-start(f32[192]{0:T(256)} %refs_5_.1) | copy-start | bytes 2308
  12.7 1.6 %copy-start.9 = (f32[192]{0:T(256)S(1)}, f32[192]{0:T(256)}, u32[]{:S(2)}) copy-start(f32[192]{0:T(256)} %refs_10_.5) | copy-start | bytes 2308
  14.3 4.5 %copy-start.10 = (f32[2,144,1728]{2,1,0:T(8,128)}, f32[2,144,1728]{2,1,0:T(8,128)S(1)}, u32[]{:S(2)}) copy-start(f32[2,144,1728]{2,1,0:T(8,128)S(1)} %get-tuple-element.38.table_ref) | copy-start | bytes 5971972
  23.3 14.7 %collective-permute-start.3 = (bf16[6,112,128]{2,1,0:T(8,128)(2,1)S(1)}, bf16[6,112,128]{2,1,0:T(8,128)(2,1)S(1)}, u32[]{:S(2)}, u32[]{:S(2)}) collective-permute-start(bf16[6,112,128]{2,1,0:T(8,128)(2,1)S(1)} %get-tuple-element.35), channel_id=1, source_target_pairs={{16,0},{32,16},{48,32},{64,48},{80,64},{96,80},{112,96},{0,112},{1... | collective-permute-start | bytes 516104 | tf_op jit(solution)/shard_map/ppermute | solution.py:422
  28.9 9.1 %collective-permute-start.4 = (bf16[6,112,128]{2,1,0:T(8,128)(2,1)S(1)}, bf16[6,112,128]{2,1,0:T(8,128)(2,1)S(1)}, u32[]{:S(2)}, u32[]{:S(2)}) collective-permute-start(bf16[6,112,128]{2,1,0:T(8,128)(2,1)S(1)} %get-tuple-element.36), channel_id=1, source_target_pairs={{1,0},{2,1},{3,2},{4,3},{5,4},{6,5},{7,6},{8,7},{9,8},{10,9},{11,1... | collective-permute-start | bytes 516104 | tf_op jit(solution)/shard_map/ppermute | solution.py:423
  29.0 4.5 %collective-permute-start.2 = (bf16[6,48,128]{2,1,0:T(8,128)(2,1)S(1)}, bf16[6,48,128]{2,1,0:T(8,128)(2,1)S(1)}, u32[]{:S(2)}, u32[]{:S(2)}) collective-permute-start(bf16[6,48,128]{2,1,0:T(8,128)(2,1)S(1)} %get-tuple-element.34), channel_id=1, source_target_pairs={{17,0},{18,1},{19,2},{20,3},{21,4},{22,5},{23,6},{24,7},{25,8},{26... | collective-permute-start | bytes 221192 | tf_op jit(solution)/shard_map/ppermute | solution.py:420
  29.1 8.9 %copy-start.11 = (bf16[384,1152]{1,0:T(8,128)(2,1)S(1)}, bf16[384,1152]{1,0:T(8,128)(2,1)}, u32[]{:S(2)}) copy-start(bf16[384,1152]{1,0:T(8,128)(2,1)} %project.3) | copy-start | bytes 2654212
  29.1 9.0 %copy-start.12 = (bf16[768,384]{1,0:T(8,128)(2,1)S(1)}, bf16[768,384]{1,0:T(8,128)(2,1)}, u32[]{:S(2)}) copy-start(bf16[768,384]{1,0:T(8,128)(2,1)} %merge_weight.1) | copy-start | bytes 1769476
  29.1 9.0 %copy-start.13 = (bf16[384,768]{1,0:T(8,128)(2,1)S(1)}, bf16[384,768]{1,0:T(8,128)(2,1)}, u32[]{:S(2)}) copy-start(bf16[384,768]{1,0:T(8,128)(2,1)} %up_first.1) | copy-start | bytes 1769476
  29.1 9.0 %copy-start.14 = (bf16[384,384]{1,0:T(8,128)(2,1)S(1)}, bf16[384,384]{1,0:T(8,128)(2,1)}, u32[]{:S(2)}) copy-start(bf16[384,384]{1,0:T(8,128)(2,1)} %wo.1) | copy-start | bytes 884740
  29.1 9.0 %copy-start.15 = (bf16[192,192]{1,0:T(8,128)(2,1)S(1)}, bf16[192,192]{1,0:T(8,128)(2,1)}, u32[]{:S(2)}) copy-start(bf16[192,192]{1,0:T(8,128)(2,1)} %up_second.1) | copy-start | bytes 221188
  29.2 9.0 %copy-start.16 = (f32[768]{0:T(1024)S(1)}, f32[768]{0:T(1024)}, u32[]{:S(2)}) copy-start(f32[768]{0:T(1024)} %merge_gain.1) | copy-start | bytes 9220
  29.2 9.0 %copy-start.17 = (f32[384]{0:T(512)S(1)}, f32[384]{0:T(512)}, u32[]{:S(2)}) copy-start(f32[384]{0:T(512)} %gain_one.1) | copy-start | bytes 4612
  29.2 9.0 %copy-start.18 = (f32[384]{0:T(512)S(1)}, f32[384]{0:T(512)}, u32[]{:S(2)}) copy-start(f32[384]{0:T(512)} %gain_two.1) | copy-start | bytes 4612
  29.2 9.0 %copy-start.19 = (f32[192]{0:T(256)S(1)}, f32[192]{0:T(256)}, u32[]{:S(2)}) copy-start(f32[192]{0:T(256)} %up_norm.1) | copy-start | bytes 2308
  29.2 8.8 %collective-permute-start.5 = (bf16[6,48,128]{2,1,0:T(8,128)(2,1)S(1)}, bf16[6,48,128]{2,1,0:T(8,128)(2,1)S(1)}, u32[]{:S(2)}, u32[]{:S(2)}) collective-permute-start(bf16[6,48,128]{2,1,0:T(8,128)(2,1)S(1)} %get-tuple-element.37), channel_id=1, source_target_pairs={{17,0},{18,1},{19,2},{20,3},{21,4},{22,5},{23,6},{24,7},{25,8},{26... | collective-permute-start | bytes 221192 | tf_op jit(solution)/shard_map/ppermute | solution.py:420
  53.8 12.9 %collective-permute-start.6 = (bf16[6,144,128]{2,1,0:T(8,128)(2,1)S(1)}, bf16[6,144,128]{2,1,0:T(8,128)(2,1)S(1)}, u32[]{:S(2)}, u32[]{:S(2)}) collective-permute-start(bf16[6,144,128]{2,1,0:T(8,128)(2,1)S(1)} %get-tuple-element.39), channel_id=1, source_target_pairs={{127,0},{112,1},{113,2},{114,3},{115,4},{116,5},{117,6},{118,7},{1... | collective-permute-start | bytes 663560 | tf_op jit(solution)/shard_map/ppermute | solution.py:420
  55.9 13.9 %collective-permute-start.7 = (bf16[6,144,128]{2,1,0:T(8,128)(2,1)S(1)}, bf16[6,144,128]{2,1,0:T(8,128)(2,1)S(1)}, u32[]{:S(2)}, u32[]{:S(2)}) collective-permute-start(bf16[6,144,128]{2,1,0:T(8,128)(2,1)S(1)} %get-tuple-element.40), channel_id=1, source_target_pairs={{112,0},{0,16},{16,32},{32,48},{48,64},{64,80},{80,96},{96,112},{1... | collective-permute-start | bytes 663560 | tf_op jit(solution)/shard_map/ppermute | solution.py:422
  55.9 14.6 %collective-permute-start.8 = (bf16[6,144,128]{2,1,0:T(8,128)(2,1)S(1)}, bf16[6,144,128]{2,1,0:T(8,128)(2,1)S(1)}, u32[]{:S(2)}, u32[]{:S(2)}) collective-permute-start(bf16[6,144,128]{2,1,0:T(8,128)(2,1)S(1)} %get-tuple-element.41), channel_id=1, source_target_pairs={{15,0},{0,1},{1,2},{2,3},{3,4},{4,5},{5,6},{6,7},{7,8},{8,9},{9,10... | collective-permute-start | bytes 663560 | tf_op jit(solution)/shard_map/ppermute | solution.py:423
  (5 other events, 7.5 us)

commit v2 on v1

--- a/solution.py
+++ b/solution.py
@@ -64,7 +64,7 @@
     return jnp.where(late(key) != late(query), EXCLUDED, 0.0)
 
 
-def attend(q, k, vt, table, heads):
+def attend(q, k, vt, table, heads, step):
     width = heads * HEAD
     lane = lax.broadcasted_iota(jnp.int32, (1, MAIN), 1) // HEAD
     zero = jnp.zeros((), BF16)
@@ -76,10 +76,11 @@
         qs = q[:, start:stop]
         here = span // HEAD
         masked = [jnp.where(lane[:, :span] == h, qs, zero) for h in range(here)]
-        main = jnp.concatenate([m[:MAIN] for m in masked], axis=0)
         rest = jnp.concatenate([m[MAIN:] for m in masked], axis=0)
         ks = k[:, start:stop]
-        pieces.append(dot(ks, main, ((1,), (1,))))
+        for h in range(0, here, step):
+            main = jnp.concatenate([m[:MAIN] for m in masked[h : h + step]], axis=0)
+            pieces.append(dot(ks, main, ((1,), (1,))))
         rests.append(dot(ks, rest, ((1,), (1,))))
     outs = []
     base = 0
@@ -121,7 +122,7 @@
         rows = slice(w * WIN, (w + 1) * WIN)
         vt = dot(wvt, xn[rows], ((1,), (1,))).astype(BF16)
         table = table_ref.at[1 if w == count - 1 else 0]
-        attended = attend(q[rows], k[rows], vt, table, heads)
+        attended = attend(q[rows], k[rows], vt, table, heads, 4 if heads == 6 else 2)
         mixed.append(dot(attended, wo[...], ((0,), (0,))))
     after = (x + jnp.concatenate(mixed, axis=0)).astype(BF16).astype(F32)
     normed = layer_norm(after, gain_two[...][None, :]).astype(BF16)
@@ -171,42 +172,65 @@
     return [(WIN_P * p + WIN_P // 2 + lev) % levels for lev in range(WIN_P)]
 
 
-def start_kernel(field, lat_ref, lon_ref, diag_ref, line_ref, low_ref, high_ref):
-    levels, rows, columns, _ = field.shape
-    packs = [Packed(low_ref.at[n], high_ref.at[n], ref.shape[1]) for n, ref in enumerate((lat_ref, lon_ref, diag_ref))]
-    lat, lon, diag = packs
+def pack_lon(field, out_ref, low_ref, high_ref):
+    levels, rows, _, _ = field.shape
+    send = Packed(low_ref, high_ref, out_ref.shape[1])
     for p in range(levels // WIN_P):
         for lev, level in enumerate(pair_levels(p, levels)):
             for r in range(rows):
-                line = field[level, r].astype(F32)
-                if r < HALF_LAT:
-                    slot = level * HALF_LAT + r
-                    line_ref[slot] = line
-                    diag.put(p, (lev * HALF_LAT + r) * HALF_LON, line[:HALF_LON])
-                    span = columns - HALF_LON
-                    lat.put(p, (lev * HALF_LAT + r) * span, line_ref[slot, HALF_LON:, :])
+                send.put(p, (lev * rows + r) * HALF_LON, field[level, r, :8].astype(F32)[:HALF_LON])
+    send.store(out_ref)
+
+
+def pack_lat(field, lon_in, out_ref, line_ref, low_ref, high_ref):
+    levels, rows, columns, _ = field.shape
+    lon = Packed(low_ref.at[0], high_ref.at[0], lon_in.shape[1]).load(lon_in)
+    send = Packed(low_ref.at[1], high_ref.at[1], out_ref.shape[1])
+    for p in range(levels // WIN_P):
+        for lev, level in enumerate(pair_levels(p, levels)):
+            for r in range(HALF_LAT):
+                slot = level * HALF_LAT + r
+                at = (lev * HALF_LAT + r) * columns
+                line_ref[slot] = field[level, r].astype(F32)
+                send.put(p, at, line_ref[slot, HALF_LON:, :])
+                send.put(p, at + columns - HALF_LON, lon.get(p, (lev * rows + r) * HALF_LON, HALF_LON))
+    send.store(out_ref)
+
+
+def pack_second(w00, w10, lat_in, out_ref, low_ref, high_ref):
+    rows, columns = 2 * WIN_LAT, 2 * WIN_LON
+    lat = Packed(low_ref.at[0], high_ref.at[0], lat_in.shape[1]).load(lat_in)
+    send = Packed(low_ref.at[1], high_ref.at[1], out_ref.shape[1])
+    for p in range(w00.shape[0] // WIN):
+        for lev in range(WIN_P):
+            for r in range(rows):
+                row = r + HALF_LAT
+                if row < rows:
+                    source = (w00, w10)[row // WIN_LAT]
+                    here = ((p * WIN_P + lev) * WIN_LAT + row % WIN_LAT) * WIN_LON
+                    value = source[here : here + HALF_LON, :]
                 else:
-                    lon.put(p, (lev * (rows - HALF_LAT) + r - HALF_LAT) * HALF_LON, line[:HALF_LON])
-    for pack, ref in zip(packs, (lat_ref, lon_ref, diag_ref)):
-        pack.store(ref)
-
-
-def table_kernel(edge_ref, a_bias, b_bias, project, plain_ref, late_ref, coarse_ref, wq_ref, wk_ref, wvt_ref):
-    edge = edge_ref[0].astype(F32)
-    for bias, out in ((a_bias, plain_ref), (b_bias, coarse_ref)):
-        heads = bias.shape[0]
-        for h in range(heads):
-            turned = (bias[h] * LOG2E).T
-            out[0, :, h * MAIN : (h + 1) * MAIN] = turned[:, :MAIN]
-            out[0, :, heads * MAIN + h * REST : heads * MAIN + (h + 1) * REST] = turned[:, MAIN:]
-        level = level_mask(heads)
-        late = lat_mask(heads) * edge
-        if out is coarse_ref:
-            out[0] = out[0] + late
-        else:
-            late_ref[0] = out[0] + late
-            late_ref[1] = late_ref[0] + level
-        out[1] = out[0] + level
+                    value = lat.get(p, (lev * HALF_LAT + row - rows) * columns, HALF_LON)
+                send.put(p, (lev * rows + r) * HALF_LON, value)
+    send.store(out_ref)
+
+
+def table_kernel(edge_ref, bias, *outs):
+    heads = bias.shape[0]
+    out = outs[0]
+    for h in range(heads):
+        turned = (bias[h] * LOG2E).T
+        out[0, :, h * MAIN : (h + 1) * MAIN] = turned[:, :MAIN]
+        out[0, :, heads * MAIN + h * REST : heads * MAIN + (h + 1) * REST] = turned[:, MAIN:]
+    level = level_mask(heads)
+    late = lat_mask(heads) * edge_ref[0].astype(F32)
+    outs[-1][0] = out[0] + late
+    for ref in outs:
+        ref[1] = ref[0] + level
+
+
+def fine_table_kernel(edge_ref, bias, project, plain_ref, late_ref, wq_ref, wk_ref, wvt_ref):
+    table_kernel(edge_ref, bias, plain_ref, late_ref)
     width = wq_ref.shape[0]
     wq_ref[...] = project[:, :width]
     wk_ref[...] = project[:, width : 2 * width]
@@ -218,68 +242,53 @@
     field = refs.pop(0)
     lat_in = refs.pop(0) if i else None
     lon_in = refs.pop(0) if j else None
-    diag_in = refs.pop(0) if i and j else None
-    first = refs.pop(0) if i != j else None
+    sends = j and not i
+    first = refs.pop(0) if sends else None
     table_ref, gain_one, wq, wk, wvt, wo, gain_two, w1, w2t, out_ref = refs[:10]
     refs = refs[10:]
-    send_ref = None if i and j else refs.pop(0)
+    send_ref = refs.pop(0) if sends else None
     line_ref, x_ref, low_ref, high_ref = refs
     levels, rows, columns, _ = field.shape
     pairs = levels // WIN_P
-    lat, lon, diag = [
+    lat, lon = [
         Packed(low_ref.at[n], high_ref.at[n], ref.shape[1]).load(ref) if ref is not None else None
-        for n, ref in enumerate((lat_in, lon_in, diag_in))
+        for n, ref in enumerate((lat_in, lon_in))
     ]
     at = 0
     slot = 0
+    start = HALF_LON + j * WIN_LON
+    own = min(columns - start, WIN_LON)
     for p in range(pairs):
         for lev, level in enumerate(pair_levels(p, levels)):
-            for row in range(i * WIN_LAT, (i + 1) * WIN_LAT):
-                start = HALF_LON + j * WIN_LON
-                own = min(columns - start, WIN_LON)
-                if row + HALF_LAT < rows:
-                    line_ref[slot] = field[level, row + HALF_LAT].astype(F32)
+            for row in range(i * WIN_LAT + HALF_LAT, (i + 1) * WIN_LAT + HALF_LAT):
+                if row < rows:
+                    line_ref[slot] = field[level, row].astype(F32)
                     x_ref[at : at + own, :] = line_ref[slot, start : start + own, :]
                     slot += 1
                     if own < WIN_LON:
-                        x_ref[at + own : at + WIN_LON, :] = lon.get(p, (lev * (rows - HALF_LAT) + row) * HALF_LON, HALF_LON)
+                        x_ref[at + own : at + WIN_LON, :] = lon.get(p, (lev * rows + row) * HALF_LON, HALF_LON)
                 else:
-                    below = lev * HALF_LAT + row + HALF_LAT - rows
-                    x_ref[at : at + own, :] = lat.get(p, below * (columns - HALF_LON) + j * WIN_LON, own)
-                    if own < WIN_LON:
-                        x_ref[at + own : at + WIN_LON, :] = diag.get(p, below * HALF_LON, HALF_LON)
+                    below = lev * HALF_LAT + row - rows
+                    x_ref[at : at + WIN_LON, :] = lat.get(p, below * columns + j * WIN_LON, WIN_LON)
                 at += WIN_LON
     block_rows(
         x_ref, pairs, table_ref, 6, gain_one, wq[...], wk[...], wvt[...], wo, gain_two, w1, w2t, ((1,), (1,)), out_ref
     )
-    if send_ref is None:
+    if not sends:
         return
-    send = Packed(low_ref.at[3], high_ref.at[3], send_ref.shape[1])
+    send = Packed(low_ref.at[0], high_ref.at[0], send_ref.shape[1])
     for p in range(pairs):
-        at = 0
         for lev in range(WIN_P):
-            base = (p * WIN_P + lev) * WIN_LAT * WIN_LON
-            if not i:
-                for row in range(HALF_LAT):
-                    here = base + row * WIN_LON
-                    if j:
-                        send.put(p, at, first[here + HALF_LON : here + WIN_LON, :])
-                        send.put(p, at + HALF_LON, out_ref[here : here + WIN_LON, :])
-                        at += WIN_LON + HALF_LON
-                    else:
-                        send.put(p, at, out_ref[here : here + HALF_LON, :])
-                        at += HALF_LON
-            else:
-                for row in range(HALF_LAT, rows):
-                    source, here = (first, row) if row < WIN_LAT else (out_ref, row - WIN_LAT)
-                    here = base + here * WIN_LON
-                    send.put(p, at, source[here : here + HALF_LON, :])
-                    at += HALF_LON
+            for row in range(HALF_LAT):
+                at = (lev * HALF_LAT + row) * columns
+                here = ((p * WIN_P + lev) * WIN_LAT + row) * WIN_LON
+                send.put(p, at, first[here : here + WIN_LON, :])
+                send.put(p, at + WIN_LON, out_ref[here : here + WIN_LON, :])
     send.store(send_ref)
 
 
 def coarse_kernel(
-    w00, w01, w10, w11, lat_in, lon_in, diag_in, table_ref,
+    w00, w01, w10, w11, lat_in, lon_in, table_ref,
     merge_gain, merge_weight,
     gain_one, project, wo, gain_two, w1, w2,
     up_first, up_norm, up_second,
@@ -292,9 +301,7 @@
     pairs = w00.shape[0] // WIN
     levels = pairs * WIN_P
     windows = ((w00, w01), (w10, w11))
-    lat, lon, diag = [
-        Packed(low_ref.at[n], high_ref.at[n], ref.shape[1]).load(ref) for n, ref in enumerate((lat_in, lon_in, diag_in))
-    ]
+    lat, lon = [Packed(low_ref.at[n], high_ref.at[n], ref.shape[1]).load(ref) for n, ref in enumerate((lat_in, lon_in))]
 
     def put(at, value):
         grid_low[at : at + value.shape[0], :] = value[:, :MAIN]
@@ -309,12 +316,10 @@
                     here = ((p * WIN_P + lev) * WIN_LAT + (row + HALF_LAT) % WIN_LAT) * WIN_LON
                     put(at + HALF_LON, left[here + HALF_LON : here + WIN_LON, :])
                     put(at + WIN_LON, right[here : here + WIN_LON, :])
-                    put(at + columns, lon.get(p, (lev * (rows - HALF_LAT) + row) * HALF_LON, HALF_LON))
                 else:
                     below = lev * HALF_LAT + row + HALF_LAT - rows
-                    span = columns - HALF_LON
-                    put(at + HALF_LON, lat.get(p, below * span, span))
-                    put(at + columns, diag.get(p, below * HALF_LON, HALF_LON))
+                    put(at + HALF_LON, lat.get(p, below * columns + HALF_LON, columns - HALF_LON))
+                put(at + columns, lon.get(p, (lev * rows + row) * HALF_LON, HALF_LON))
     for r in range(2):
         for t in range(2):
             n = 2 * r + t
@@ -389,10 +394,9 @@
 MIB = 1024 * 1024
 
 
-def call(kernel, name, operands, outs, scratch, limit, flops=0, scalars=0):
+def call(kernel, name, operands, outs, scratch, limit, scalars=0):
     vmem = pl.BlockSpec(memory_space=pltpu.VMEM)
     smem = pl.BlockSpec(memory_space=pltpu.SMEM)
-    moved = sum(x.size * x.dtype.itemsize for x in operands) + sum(math.prod(s) * jnp.dtype(d).itemsize for s, d in outs)
     return pl.pallas_call(
         kernel,
         in_specs=[smem] * scalars + [vmem] * (len(operands) - scalars),
@@ -400,7 +404,7 @@
         out_shape=[jax.ShapeDtypeStruct(s, d) for s, d in outs],
         scratch_shapes=[pltpu.VMEM(s, F32) for s in scratch],
         compiler_params=pltpu.CompilerParams(vmem_limit_bytes=limit * MIB),
-        cost_estimate=pl.CostEstimate(flops=flops, bytes_accessed=moved, transcendentals=0),
+        cost_estimate=pl.CostEstimate(flops=0, bytes_accessed=0, transcendentals=0),
         name=name,
     )(*operands)
 
@@ -431,64 +435,62 @@
 ):
     levels, rows, columns, width = field.shape
     pairs = levels // WIN_P
-    lat_tokens = WIN_P * HALF_LAT * (columns - HALF_LON)
-    lon_tokens = WIN_P * (rows - HALF_LAT) * HALF_LON
-    diag_tokens = WIN_P * HALF_LAT * HALF_LON
-    lat_shape, lon_shape, diag_shape = [packed_shape(n, pairs) for n in (lat_tokens, lon_tokens, diag_tokens)]
-    halo_rows = max(lat_shape[1], lon_shape[1])
+    halo = packed_shape(WIN, pairs)
+    staging = (pairs, WIN, MAIN)
+    both = (2,) + staging
     tokens = pairs * WIN
 
     edge = (lax.axis_index("lat") == lax.axis_size("lat") - 1).astype(jnp.int32).reshape(1)
-    staging = (3, pairs, halo_rows, MAIN)
-    lat, lon, diag = call(
-        start_kernel, "start", [field],
-        [(lat_shape, BF16), (lon_shape, BF16), (diag_shape, BF16)],
-        [(levels * HALF_LAT, columns, width), staging, staging], 16,
-    )
+    (lon,) = call(pack_lon, "pack_lon", [field], [(halo, BF16)], [staging, staging], 16)
     lon = shift(lon, 0, 1)
-    lat = shift(lat, 1, 0)
-    diag = shift(diag, 1, 1)
     a_heads, b_heads = a_bias.shape[0], b_bias.shape[0]
     square = ((width, width), BF16)
-    plain, late, coarse_table, wq, wk, wvt = call(
-        table_kernel, "tables", [edge, a_bias, b_bias, a_project],
-        [((2, WIN, a_heads * WIN), F32)] * 2 + [((2, WIN, b_heads * WIN), F32)] + [square] * 3,
-        [], 24, scalars=1,
+    plain, late, wq, wk, wvt = call(
+        fine_table_kernel, "fine_tables", [edge, a_bias, a_project],
+        [((2, WIN, a_heads * WIN), F32)] * 2 + [square] * 3, [], 16, scalars=1,
     )
     weights = [a_norm_one, wq, wk, wvt, a_output, a_norm_two, a_raise, a_lower.T]
-    staging = (4, pairs, halo_rows, MAIN)
-    scratch = [(levels * WIN_LAT, columns, width), (tokens, width), staging, staging]
+    scratch = [(levels * WIN_LAT, columns, width), (tokens, width), both, both]
     out = ((tokens, width), F32)
-    work = 2 * tokens * width * (4 * width + 8 * width)
 
     def fine(i, j, halos, outs):
         def kernel(*refs):
             fine_kernel(i, j, *refs)
 
         operands = [field, *halos, late if i else plain, *weights]
-        return call(kernel, f"fine_{i}{j}", operands, [out] + outs, scratch, 24, work)
-
-    w00, diag_two = fine(0, 0, [], [(diag_shape, BF16)])
-    diag_two = shift(diag_two, 1, 1)
-    w01, lat_two = fine(0, 1, [lon, w00], [(lat_shape, BF16)])
+        return call(kernel, f"fine_{i}{j}", operands, [out] + outs, scratch, 20)
+
+    (w00,) = fine(0, 0, [], [])
+    lon, w00 = lax.optimization_barrier((lon, w00))
+    lines = (levels * HALF_LAT, columns, width)
+    (lat,) = call(pack_lat, "pack_lat", [field, lon], [(halo, BF16)], [lines, both, both], 16)
+    lon, lat = lax.optimization_barrier((lon, lat))
+    lat = shift(lat, 1, 0)
+    w01, lat_two = fine(0, 1, [lon, w00], [(halo, BF16)])
+    lat, lat_two = lax.optimization_barrier((lat, lat_two))
     lat_two = shift(lat_two, 1, 0)
-    w10, lon_two = fine(1, 0, [lat, w00], [(lon_shape, BF16)])
+    (w10,) = fine(1, 0, [lat], [])
+    lat_two, w10 = lax.optimization_barrier((lat_two, w10))
+    (lon_two,) = call(pack_second, "pack_second", [w00, w10, lat_two], [(halo, BF16)], [both, both], 16)
+    lon, lon_two = lax.optimization_barrier((lon, lon_two))
     lon_two = shift(lon_two, 0, 1)
-    (w11,) = fine(1, 1, [lat, lon, diag], [])
-
-    quarter = packed_shape(WIN, pairs)
-    halos = (3, pairs, halo_rows, MAIN)
-    quads = (4, pairs, WIN, MAIN)
+    (w11,) = fine(1, 1, [lat, lon], [])
+    late_bias, w11 = lax.optimization_barrier((b_bias, w11))
+    (coarse_table,) = call(
+        table_kernel, "coarse_table", [edge, late_bias], [((2, WIN, b_heads * WIN), F32)], [], 16, scalars=1
+    )
+
+    quads = (4,) + staging
     lines = (levels * rows * PITCH, MAIN)
     stay, lat, lon, diag = call(
         coarse_kernel, "coarse",
         [
-            w00, w01, w10, w11, lat_two, lon_two, diag_two, coarse_table, merge_norm_gain, merge_weight,
+            w00, w01, w10, w11, lat_two, lon_two, coarse_table, merge_norm_gain, merge_weight,
             b_norm_one, b_project, b_output, b_norm_two, b_raise, b_lower, up_first, up_norm, up_second,
         ],
-        [(quarter, BF16)] * 4,
-        [halos, halos, lines, lines, quads, quads, (4, tokens, 2 * MAIN), (tokens, 2 * width), (tokens, 2 * width)],
-        48, 8 * work,
+        [(halo, BF16)] * 4,
+        [both, both, lines, lines, quads, quads, (4, tokens, 2 * MAIN), (tokens, 2 * width), (tokens, 2 * width)],
+        32,
     )
     diag = shift(diag, -1, -1)
     lat = shift(lat, -1, 0)

time: 72.2 us -> 70.7 us (0.979)
  Pallas kernels: 37 us -> 33.4 us
  waiting for transfers between devices: 18.5 us -> 15.1 us
  local copies, waits for them, and re-layouts: 2.83 us -> 5.74 us
  starting transfers between devices: 13.5 us -> 15.9 us
    ppermute x3, starting transfers between devices: 6.17 us -> 10.3 us  [shift(): lax.ppermute(array, 'lat', [((i + lat_by) % lats, i) for i in range(lats)])]
    pallas_call x8 -> x11, Pallas kernels: 37 us -> 33.4 us  [call(): pl.pallas_call(kernel, in_specs=[smem] * scalars + [vmem] * (len(operands...]
    unnamed x40 -> x42, local copies, waits for them, and re-layouts: 2.83 us -> 5.74 us
    ppermute x3 -> x1, starting transfers between devices: 2.42 us -> 0.07 us  [shift(): return lax.ppermute(array, ('lat', 'lon'), pairs)]
    ppermute x3 -> x1, waiting for transfers between devices: 14.8 us -> 13.1 us  [shift(): return lax.ppermute(array, ('lat', 'lon'), pairs)]
    ppermute x3, waiting for transfers between devices: 2.93 us -> 1.97 us  [shift(): lax.ppermute(array, 'lat', [((i + lat_by) % lats, i) for i in range(lats)])]
  transfers between devices with their start and end apart: 9 -> 7, of which waited for: 4 -> 2; matrix products, arithmetic and copies ran while one was open for 0% -> 0% of each run, Pallas kernels for 27% -> 27%
where the time goes in v2:
time: 70.7 us; the launch traced here: 70.5 us
  Pallas kernels  33.4 us (47%)
  starting transfers between devices  15.9 us (22%)
  waiting for transfers between devices  15.1 us (21%)
  local copies, waits for them, and re-layouts  5.74 us (8%)
    pallas_call x11, Pallas kernels, call(): pl.pallas_call(kernel, in_specs=[smem] * scalars + [vmem] * (len(operands...  33.4 us
    ppermute x1, waiting for transfers between devices, shift(): return lax.ppermute(array, ('lat', 'lon'), pairs)  13.1 us
    ppermute x3, starting transfers between devices, shift(): lax.ppermute(array, 'lat', [((i + lat_by) % lats, i) for i in range(lats)])  10.3 us
    unnamed x42, local copies, waits for them, and re-layouts  5.74 us
    ppermute x3, starting transfers between devices, shift(): lax.ppermute(array, 'lon', [((i + lon_by) % lons, i) for i in range(lons)])  5.54 us
    ppermute x3, waiting for transfers between devices, shift(): lax.ppermute(array, 'lat', [((i + lat_by) % lats, i) for i in range(lats)])  1.97 us
  transfers between devices with their start and end apart: 7, of which 2 were waited for; matrix products, arithmetic and copies ran while one was open for 0% of the time, Pallas kernels for 27%

profile of v2, /device:TPU:0, one launch (start us, length us, event | category | flops | bytes accessed | tf_op | source)
XLA Modules:
  0.0 70.5 jit_solution(15782475176839937842)
XLA Ops:
  0.0 1.3 %copy-done = bf16[8,12,24,192]{3,2,1,0:T(8,128)(2,1)S(1)} copy-done((bf16[8,12,24,192]{3,2,1,0:T(8,128)(2,1)S(1)}, bf16[8,12,24,192]{3,2,1,0:T(8,128)(2,1)}, u32[]{:S(2)}) %copy-start) | copy-done | bytes 884760
  1.4 4.6 %collective-permute-start = (bf16[6,144,128]{2,1,0:T(8,128)(2,1)S(1)}, bf16[6,144,128]{2,1,0:T(8,128)(2,1)S(1)}, u32[]{:S(2)}, u32[]{:S(2)}) collective-permute-start(bf16[6,144,128]{2,1,0:T(8,128)(2,1)S(1)} %pack_lon.1), channel_id=1, source_target_pairs={{1,0},{2,1},{3,2},{4,3},{5,4},{6,5},{7,6},{8,7},{9,8},{10,9},{11,1... | collective-permute-start | bytes 663560 | tf_op jit(solution)/shard_map/ppermute | solution.py:427
  6.1 1.2 %copy-done.9 = f32[6,144,144]{2,1,0:T(8,128)S(1)} copy-done((f32[6,144,144]{2,1,0:T(8,128)S(1)}, f32[6,144,144]{2,1,0:T(8,128)}, u32[]{:S(2)}) %copy-start.9) | copy-done | bytes 497688
  7.2 0.9 %copy-done.13 = bf16[192,576]{1,0:T(8,128)(2,1)S(1)} copy-done((bf16[192,576]{1,0:T(8,128)(2,1)S(1)}, bf16[192,576]{1,0:T(8,128)(2,1)}, u32[]{:S(2)}) %copy-start.13) | copy-done | bytes 221208
  8.2 0.6 fine_tables.1
  8.9 0.7 copy-done.15
  9.5 0.7 copy-done.16
  10.2 4.3 %fine_00.1.refs_2_.w00 = f32[576,192]{1,0:T(8,128)S(1)} custom-call(bf16[8,12,24,192]{3,2,1,0:T(8,128)(2,1)S(1)} %copy-done.1, f32[2,144,864]{2,1,0:T(8,128)S(1)} %get-tuple-element.28.refs_1_.refs_3_, f32[192]{0:T(256)S(1)} %copy-done.15, bf16[192,192]{1,0:T(8,128)(2,1)S(1)} %get-tuple-element.29.refs_3_.refs_5_.refs_4_, ...), custom_call_target="tpu_custom_call" | custom-call | tf_op jit(solution)/shard_map/fine_00/pallas_call | solution.py:400
  14.5 0.2 pack_lat.1
  14.8 5.2 %collective-permute-start.1 = (bf16[6,144,128]{2,1,0:T(8,128)(2,1)S(1)}, bf16[6,144,128]{2,1,0:T(8,128)(2,1)S(1)}, u32[]{:S(2)}, u32[]{:S(2)}) collective-permute-start(bf16[6,144,128]{2,1,0:T(8,128)(2,1)S(1)} %pack_lat.1), channel_id=1, source_target_pairs={{16,0},{32,16},{48,32},{64,48},{80,64},{96,80},{112,96},{0,112},{1... | collective-permute-start | bytes 663560 | tf_op jit(solution)/shard_map/ppermute | solution.py:426
  19.9 4.4 %fine_01.1 = (f32[576,192]{1,0:T(8,128)S(1)}, bf16[6,144,128]{2,1,0:T(8,128)(2,1)S(1)}) custom-call(bf16[8,12,24,192]{3,2,1,0:T(8,128)(2,1)S(1)} %copy-done.1, bf16[6,144,128]{2,1,0:T(8,128)(2,1)S(1)} %collective-permute-done.lon_in.refs_1_.refs_2_, f32[576,192]{1,0:T(8,128)S(1)} %fine_00.1.refs_2_.w00, ...), custom_call_target="tpu_custom_call" | custom-call | tf_op jit(solution)/shard_map/fine_01/pallas_call | solution.py:400
  24.4 5.1 %collective-permute-start.2 = (bf16[6,144,128]{2,1,0:T(8,128)(2,1)S(1)}, bf16[6,144,128]{2,1,0:T(8,128)(2,1)S(1)}, u32[]{:S(2)}, u32[]{:S(2)}) collective-permute-start(bf16[6,144,128]{2,1,0:T(8,128)(2,1)S(1)} %get-tuple-element.38), channel_id=1, source_target_pairs={{16,0},{32,16},{48,32},{64,48},{80,64},{96,80},{112,96},{0,112},{1... | collective-permute-start | bytes 663560 | tf_op jit(solution)/shard_map/ppermute | solution.py:426
  29.5 4.4 %fine_10.1.w10 = f32[576,192]{1,0:T(8,128)S(1)} custom-call(bf16[8,12,24,192]{3,2,1,0:T(8,128)(2,1)S(1)} %copy-done.1, bf16[6,144,128]{2,1,0:T(8,128)(2,1)S(1)} %collective-permute-done.1.refs_1_, f32[2,144,864]{2,1,0:T(8,128)S(1)} %get-tuple-element.40.refs_2_.refs_3_, f32[192]{0:T(256)S(1)} %copy-done.15, ...), custom_call_target="tpu_custom_call" | custom-call | tf_op jit(solution)/shard_map/fine_10/pallas_call | solution.py:400
  33.9 0.2 pack_second.1
  34.1 0.8 %collective-permute-start.3 = (bf16[6,144,128]{2,1,0:T(8,128)(2,1)S(1)}, bf16[6,144,128]{2,1,0:T(8,128)(2,1)S(1)}, u32[]{:S(2)}, u32[]{:S(2)}) collective-permute-start(bf16[6,144,128]{2,1,0:T(8,128)(2,1)S(1)} %pack_second.1), channel_id=1, source_target_pairs={{1,0},{2,1},{3,2},{4,3},{5,4},{6,5},{7,6},{8,7},{9,8},{10,9},{11,1... | collective-permute-start | bytes 663560 | tf_op jit(solution)/shard_map/ppermute | solution.py:427
  34.9 4.5 %fine_11.1.w11 = f32[576,192]{1,0:T(8,128)S(1)} custom-call(bf16[8,12,24,192]{3,2,1,0:T(8,128)(2,1)S(1)} %copy-done.1, bf16[6,144,128]{2,1,0:T(8,128)(2,1)S(1)} %collective-permute-done.1.refs_1_, bf16[6,144,128]{2,1,0:T(8,128)(2,1)S(1)} %collective-permute-done.lon_in.refs_1_.refs_2_, f32[2,144,864]{2,1,0:T(8,128)S(1)} %get-tuple-element.40.refs_2_.refs_3_, ...), custom_call_target="tpu_custom_call" | custom-call | tf_op jit(solution)/shard_map/fine_11/pallas_call | solution.py:400
  39.5 1.0 %coarse_table.1.table_ref = f32[2,144,1728]{2,1,0:T(8,128)S(1)} custom-call(s32[1]{0:T(128)} %bitcast.edge_ref, f32[12,144,144]{2,1,0:T(8,128)S(1)} %copy-done.4), custom_call_target="tpu_custom_call" | custom-call | tf_op jit(solution)/shard_map/coarse_table/pallas_call | solution.py:400
  40.5 0.2 copy-done.6
  40.7 0.4 copy-done.7
  41.1 0.3 copy-done.8
  41.5 12.1 %coarse.1 = (bf16[6,144,128]{2,1,0:T(8,128)(2,1)S(1)}, bf16[6,144,128]{2,1,0:T(8,128)(2,1)S(1)}, bf16[6,144,128]{2,1,0:T(8,128)(2,1)S(1)}, bf16[6,144,128]{2,1,0:T(8,128)(2,1)S(1)}) custom-call(f32[576,192]{1,0:T(8,128)S(1)} %fine_00.1.refs_2_.w00, f32[576,192]{1,0:T(8,128)S(1)} %get-tuple-element.35.w01, f32[576,192]{1,0:T(8,128)S(1)} %fine_10.1.w10, ...), custom_call_target="tpu_custom_call" | custom-call | tf_op jit(solution)/shard_map/coarse/pallas_call | solution.py:400
  53.8 13.1 %collective-permute-done.4.upper_left = bf16[6,144,128]{2,1,0:T(8,128)(2,1)S(1)} collective-permute-done((bf16[6,144,128]{2,1,0:T(8,128)(2,1)S(1)}, bf16[6,144,128]{2,1,0:T(8,128)(2,1)S(1)}, u32[]{:S(2)}, u32[]{:S(2)}) %collective-permute-start.4) | collective-permute-done | bytes 221216 | tf_op jit(solution)/shard_map/ppermute | solution.py:424
  66.9 2.0 %collective-permute-done.5.upper_right = bf16[6,144,128]{2,1,0:T(8,128)(2,1)S(1)} collective-permute-done((bf16[6,144,128]{2,1,0:T(8,128)(2,1)S(1)}, bf16[6,144,128]{2,1,0:T(8,128)(2,1)S(1)}, u32[]{:S(2)}, u32[]{:S(2)}) %collective-permute-start.5) | collective-permute-done | bytes 221216 | tf_op jit(solution)/shard_map/ppermute | solution.py:426
  68.9 1.6 %finish.1 = bf16[8,12,24,192]{3,2,1,0:T(8,128)(2,1)} custom-call(bf16[6,144,128]{2,1,0:T(8,128)(2,1)S(1)} %collective-permute-done.4.upper_left, bf16[6,144,128]{2,1,0:T(8,128)(2,1)S(1)} %collective-permute-done.5.upper_right, bf16[6,144,128]{2,1,0:T(8,128)(2,1)S(1)} %collective-permute-done.6.lower_left, bf16[6,144,128]{2,1,0:T(8,128)(2,1)S(1)} %get-tuple-element.50.lower_right), custom_call_target="tpu_custom_call" | custom-call | tf_op jit(solution)/shard_map/finish/pallas_call | solution.py:400
  (43 shorter events, 0.6 us)
Async XLA Ops:
  0.0 1.3 %copy-start = (bf16[8,12,24,192]{3,2,1,0:T(8,128)(2,1)S(1)}, bf16[8,12,24,192]{3,2,1,0:T(8,128)(2,1)}, u32[]{:S(2)}) copy-start(bf16[8,12,24,192]{3,2,1,0:T(8,128)(2,1)} %refs_0_.7) | copy-start | bytes 2654212
  1.3 7.5 %copy-start.1 = (bf16[8,12,24,192]{3,2,1,0:T(8,128)(2,1)S(1)}, bf16[8,12,24,192]{3,2,1,0:T(8,128)(2,1)}, u32[]{:S(2)}) copy-start(bf16[8,12,24,192]{3,2,1,0:T(8,128)(2,1)} %refs_0_.7) | copy-start | bytes 2654212
  1.3 7.5 %copy-start.2 = (bf16[192,768]{1,0:T(8,128)(2,1)S(1)}, bf16[192,768]{1,0:T(8,128)(2,1)}, u32[]{:S(2)}) copy-start(bf16[192,768]{1,0:T(8,128)(2,1)} %refs_10_.3) | copy-start | bytes 884740
  1.3 7.6 %copy-start.3 = (bf16[768,192]{0,1:T(8,128)(2,1)S(1)}, bf16[768,192]{0,1:T(8,128)(2,1)}, u32[]{:S(2)}) copy-start(bf16[768,192]{0,1:T(8,128)(2,1)} %param.27) | copy-start | bytes 884740
  1.3 7.6 %copy-start.5 = (bf16[192,192]{1,0:T(8,128)(2,1)S(1)}, bf16[192,192]{1,0:T(8,128)(2,1)}, u32[]{:S(2)}) copy-start(bf16[192,192]{1,0:T(8,128)(2,1)} %refs_8_.7) | copy-start | bytes 221188
  1.4 13.1 %collective-permute-start = (bf16[6,144,128]{2,1,0:T(8,128)(2,1)S(1)}, bf16[6,144,128]{2,1,0:T(8,128)(2,1)S(1)}, u32[]{:S(2)}, u32[]{:S(2)}) collective-permute-start(bf16[6,144,128]{2,1,0:T(8,128)(2,1)S(1)} %pack_lon.1), channel_id=1, source_target_pairs={{1,0},{2,1},{3,2},{4,3},{5,4},{6,5},{7,6},{8,7},{9,8},{10,9},{11,1... | collective-permute-start | bytes 663560 | tf_op jit(solution)/shard_map/ppermute | solution.py:427
  14.8 9.6 %collective-permute-start.1 = (bf16[6,144,128]{2,1,0:T(8,128)(2,1)S(1)}, bf16[6,144,128]{2,1,0:T(8,128)(2,1)S(1)}, u32[]{:S(2)}, u32[]{:S(2)}) collective-permute-start(bf16[6,144,128]{2,1,0:T(8,128)(2,1)S(1)} %pack_lat.1), channel_id=1, source_target_pairs={{16,0},{32,16},{48,32},{64,48},{80,64},{96,80},{112,96},{0,112},{1... | collective-permute-start | bytes 663560 | tf_op jit(solution)/shard_map/ppermute | solution.py:426
  24.4 9.5 %collective-permute-start.2 = (bf16[6,144,128]{2,1,0:T(8,128)(2,1)S(1)}, bf16[6,144,128]{2,1,0:T(8,128)(2,1)S(1)}, u32[]{:S(2)}, u32[]{:S(2)}) collective-permute-start(bf16[6,144,128]{2,1,0:T(8,128)(2,1)S(1)} %get-tuple-element.38), channel_id=1, source_target_pairs={{16,0},{32,16},{48,32},{64,48},{80,64},{96,80},{112,96},{0,112},{1... | collective-permute-start | bytes 663560 | tf_op jit(solution)/shard_map/ppermute | solution.py:426
  34.1 5.3 %copy-start.4 = (f32[12,144,144]{2,1,0:T(8,128)S(1)}, f32[12,144,144]{2,1,0:T(8,128)}, u32[]{:S(2)}) copy-start(f32[12,144,144]{2,1,0:T(8,128)} %bias.2) | copy-start | bytes 2985988
  34.1 6.4 %collective-permute-start.3 = (bf16[6,144,128]{2,1,0:T(8,128)(2,1)S(1)}, bf16[6,144,128]{2,1,0:T(8,128)(2,1)S(1)}, u32[]{:S(2)}, u32[]{:S(2)}) collective-permute-start(bf16[6,144,128]{2,1,0:T(8,128)(2,1)S(1)} %pack_second.1), channel_id=1, source_target_pairs={{1,0},{2,1},{3,2},{4,3},{5,4},{6,5},{7,6},{8,7},{9,8},{10,9},{11,1... | collective-permute-start | bytes 663560 | tf_op jit(solution)/shard_map/ppermute | solution.py:427
  34.9 5.6 %copy-start.11 = (bf16[384,768]{1,0:T(8,128)(2,1)S(1)}, bf16[384,768]{1,0:T(8,128)(2,1)}, u32[]{:S(2)}) copy-start(bf16[384,768]{1,0:T(8,128)(2,1)} %up_first.1) | copy-start | bytes 1769476
  34.9 5.6 %copy-start.12 = (bf16[384,384]{1,0:T(8,128)(2,1)S(1)}, bf16[384,384]{1,0:T(8,128)(2,1)}, u32[]{:S(2)}) copy-start(bf16[384,384]{1,0:T(8,128)(2,1)} %wo.1) | copy-start | bytes 884740
  34.9 5.6 %copy-start.14 = (bf16[192,192]{1,0:T(8,128)(2,1)S(1)}, bf16[192,192]{1,0:T(8,128)(2,1)}, u32[]{:S(2)}) copy-start(bf16[192,192]{1,0:T(8,128)(2,1)} %up_second.1) | copy-start | bytes 221188
  34.9 5.6 %copy-start.17 = (f32[768]{0:T(1024)S(1)}, f32[768]{0:T(1024)}, u32[]{:S(2)}) copy-start(f32[768]{0:T(1024)} %merge_gain.1) | copy-start | bytes 9220
  34.9 5.6 %copy-start.19 = (f32[384]{0:T(512)S(1)}, f32[384]{0:T(512)}, u32[]{:S(2)}) copy-start(f32[384]{0:T(512)} %gain_two.1) | copy-start | bytes 4612
  34.9 5.6 %copy-start.20 = (f32[192]{0:T(256)S(1)}, f32[192]{0:T(256)}, u32[]{:S(2)}) copy-start(f32[192]{0:T(256)} %up_norm.1) | copy-start | bytes 2308
  39.4 1.3 %copy-start.6 = (bf16[384,1536]{1,0:T(8,128)(2,1)S(1)}, bf16[384,1536]{1,0:T(8,128)(2,1)}, u32[]{:S(2)}) copy-start(bf16[384,1536]{1,0:T(8,128)(2,1)} %w1.1) | copy-start | bytes 3538948
  39.4 1.6 %copy-start.7 = (bf16[1536,384]{1,0:T(8,128)(2,1)S(1)}, bf16[1536,384]{1,0:T(8,128)(2,1)}, u32[]{:S(2)}) copy-start(bf16[1536,384]{1,0:T(8,128)(2,1)} %w2.1) | copy-start | bytes 3538948
  39.5 1.9 %copy-start.8 = (bf16[384,1152]{1,0:T(8,128)(2,1)S(1)}, bf16[384,1152]{1,0:T(8,128)(2,1)}, u32[]{:S(2)}) copy-start(bf16[384,1152]{1,0:T(8,128)(2,1)} %project.3) | copy-start | bytes 2654212
  39.5 2.0 %copy-start.10 = (bf16[768,384]{1,0:T(8,128)(2,1)S(1)}, bf16[768,384]{1,0:T(8,128)(2,1)}, u32[]{:S(2)}) copy-start(bf16[768,384]{1,0:T(8,128)(2,1)} %merge_weight.1) | copy-start | bytes 1769476
  39.5 2.0 %copy-start.18 = (f32[384]{0:T(512)S(1)}, f32[384]{0:T(512)}, u32[]{:S(2)}) copy-start(f32[384]{0:T(512)} %gain_one.1) | copy-start | bytes 4612
  53.6 13.3 %collective-permute-start.4 = (bf16[6,144,128]{2,1,0:T(8,128)(2,1)S(1)}, bf16[6,144,128]{2,1,0:T(8,128)(2,1)S(1)}, u32[]{:S(2)}, u32[]{:S(2)}) collective-permute-start(bf16[6,144,128]{2,1,0:T(8,128)(2,1)S(1)} %get-tuple-element.47), channel_id=1, source_target_pairs={{127,0},{112,1},{113,2},{114,3},{115,4},{116,5},{117,6},{118,7},{1... | collective-permute-start | bytes 663560 | tf_op jit(solution)/shard_map/ppermute | solution.py:424
  53.6 15.2 %collective-permute-start.5 = (bf16[6,144,128]{2,1,0:T(8,128)(2,1)S(1)}, bf16[6,144,128]{2,1,0:T(8,128)(2,1)S(1)}, u32[]{:S(2)}, u32[]{:S(2)}) collective-permute-start(bf16[6,144,128]{2,1,0:T(8,128)(2,1)S(1)} %get-tuple-element.48), channel_id=1, source_target_pairs={{112,0},{0,16},{16,32},{32,48},{48,64},{64,80},{80,96},{96,112},{1... | collective-permute-start | bytes 663560 | tf_op jit(solution)/shard_map/ppermute | solution.py:426
  53.7 15.1 %collective-permute-start.6 = (bf16[6,144,128]{2,1,0:T(8,128)(2,1)S(1)}, bf16[6,144,128]{2,1,0:T(8,128)(2,1)S(1)}, u32[]{:S(2)}, u32[]{:S(2)}) collective-permute-start(bf16[6,144,128]{2,1,0:T(8,128)(2,1)S(1)} %get-tuple-element.49), channel_id=1, source_target_pairs={{15,0},{0,1},{1,2},{2,3},{3,4},{4,5},{5,6},{6,7},{7,8},{8,9},{9,10... | collective-permute-start | bytes 663560 | tf_op jit(solution)/shard_map/ppermute | solution.py:427
  (4 other events, 3.5 us)

commit v3 on v2

--- a/solution.py
+++ b/solution.py
@@ -172,29 +172,24 @@
     return [(WIN_P * p + WIN_P // 2 + lev) % levels for lev in range(WIN_P)]
 
 
-def pack_lon(field, out_ref, low_ref, high_ref):
-    levels, rows, _, _ = field.shape
-    send = Packed(low_ref, high_ref, out_ref.shape[1])
+def start_kernel(field, lat_ref, lon_ref, diag_ref, line_ref, low_ref, high_ref):
+    levels, rows, columns, _ = field.shape
+    packs = [Packed(low_ref.at[n], high_ref.at[n], ref.shape[1]) for n, ref in enumerate((lat_ref, lon_ref, diag_ref))]
+    lat, lon, diag = packs
     for p in range(levels // WIN_P):
         for lev, level in enumerate(pair_levels(p, levels)):
             for r in range(rows):
-                send.put(p, (lev * rows + r) * HALF_LON, field[level, r, :8].astype(F32)[:HALF_LON])
-    send.store(out_ref)
-
-
-def pack_lat(field, lon_in, out_ref, line_ref, low_ref, high_ref):
-    levels, rows, columns, _ = field.shape
-    lon = Packed(low_ref.at[0], high_ref.at[0], lon_in.shape[1]).load(lon_in)
-    send = Packed(low_ref.at[1], high_ref.at[1], out_ref.shape[1])
-    for p in range(levels // WIN_P):
-        for lev, level in enumerate(pair_levels(p, levels)):
-            for r in range(HALF_LAT):
-                slot = level * HALF_LAT + r
-                at = (lev * HALF_LAT + r) * columns
-                line_ref[slot] = field[level, r].astype(F32)
-                send.put(p, at, line_ref[slot, HALF_LON:, :])
-                send.put(p, at + columns - HALF_LON, lon.get(p, (lev * rows + r) * HALF_LON, HALF_LON))
-    send.store(out_ref)
+                line = field[level, r].astype(F32)
+                if r < HALF_LAT:
+                    slot = level * HALF_LAT + r
+                    line_ref[slot] = line
+                    diag.put(p, (lev * HALF_LAT + r) * HALF_LON, line[:HALF_LON])
+                    span = columns - HALF_LON
+                    lat.put(p, (lev * HALF_LAT + r) * span, line_ref[slot, HALF_LON:, :])
+                else:
+                    lon.put(p, (lev * (rows - HALF_LAT) + r - HALF_LAT) * HALF_LON, line[:HALF_LON])
+    for pack, ref in zip(packs, (lat_ref, lon_ref, diag_ref)):
+        pack.store(ref)
 
 
 def pack_second(w00, w10, lat_in, out_ref, low_ref, high_ref):
@@ -242,6 +237,7 @@
     field = refs.pop(0)
     lat_in = refs.pop(0) if i else None
     lon_in = refs.pop(0) if j else None
+    diag_in = refs.pop(0) if i and j else None
     sends = j and not i
     first = refs.pop(0) if sends else None
     table_ref, gain_one, wq, wk, wvt, wo, gain_two, w1, w2t, out_ref = refs[:10]
@@ -250,9 +246,9 @@
     line_ref, x_ref, low_ref, high_ref = refs
     levels, rows, columns, _ = field.shape
     pairs = levels // WIN_P
-    lat, lon = [
+    lat, lon, diag = [
         Packed(low_ref.at[n], high_ref.at[n], ref.shape[1]).load(ref) if ref is not None else None
-        for n, ref in enumerate((lat_in, lon_in))
+        for n, ref in enumerate((lat_in, lon_in, diag_in))
     ]
     at = 0
     slot = 0
@@ -266,10 +262,13 @@
                     x_ref[at : at + own, :] = line_ref[slot, start : start + own, :]
                     slot += 1
                     if own < WIN_LON:
-                        x_ref[at + own : at + WIN_LON, :] = lon.get(p, (lev * rows + row) * HALF_LON, HALF_LON)
+                        late = lev * (rows - HALF_LAT) + row - HALF_LAT
+                        x_ref[at + own : at + WIN_LON, :] = lon.get(p, late * HALF_LON, HALF_LON)
                 else:
                     below = lev * HALF_LAT + row - rows
-                    x_ref[at : at + WIN_LON, :] = lat.get(p, below * columns + j * WIN_LON, WIN_LON)
+                    x_ref[at : at + own, :] = lat.get(p, below * (columns - HALF_LON) + j * WIN_LON, own)
+                    if own < WIN_LON:
+                        x_ref[at + own : at + WIN_LON, :] = diag.get(p, below * HALF_LON, HALF_LON)
                 at += WIN_LON
     block_rows(
         x_ref, pairs, table_ref, 6, gain_one, wq[...], wk[...], wvt[...], wo, gain_two, w1, w2t, ((1,), (1,)), out_ref
@@ -394,9 +393,10 @@
 MIB = 1024 * 1024
 
 
-def call(kernel, name, operands, outs, scratch, limit, scalars=0):
+def call(kernel, name, operands, outs, scratch, limit, scalars=0, us=1):
     vmem = pl.BlockSpec(memory_space=pltpu.VMEM)
     smem = pl.BlockSpec(memory_space=pltpu.SMEM)
+    moved = sum(x.size * x.dtype.itemsize for x in operands) + sum(math.prod(s) * jnp.dtype(d).itemsize for s, d in outs)
     return pl.pallas_call(
         kernel,
         in_specs=[smem] * scalars + [vmem] * (len(operands) - scalars),
@@ -404,7 +404,7 @@
         out_shape=[jax.ShapeDtypeStruct(s, d) for s, d in outs],
         scratch_shapes=[pltpu.VMEM(s, F32) for s in scratch],
         compiler_params=pltpu.CompilerParams(vmem_limit_bytes=limit * MIB),
-        cost_estimate=pl.CostEstimate(flops=0, bytes_accessed=0, transcendentals=0),
+        cost_estimate=pl.CostEstimate(flops=us * 1000 * MIB, bytes_accessed=moved, transcendentals=0),
         name=name,
     )(*operands)
 
@@ -441,16 +441,24 @@
     tokens = pairs * WIN
 
     edge = (lax.axis_index("lat") == lax.axis_size("lat") - 1).astype(jnp.int32).reshape(1)
-    (lon,) = call(pack_lon, "pack_lon", [field], [(halo, BF16)], [staging, staging], 16)
+    lat_shape = packed_shape(WIN_P * HALF_LAT * (columns - HALF_LON), pairs)
+    lon_shape = packed_shape(WIN_P * (rows - HALF_LAT) * HALF_LON, pairs)
+    diag_shape = packed_shape(WIN_P * HALF_LAT * HALF_LON, pairs)
+    lat, lon, diag = call(
+        start_kernel, "start", [field], [(lat_shape, BF16), (lon_shape, BF16), (diag_shape, BF16)],
+        [(levels * HALF_LAT, columns, width), (3,) + staging, (3,) + staging], 16, us=3,
+    )
     lon = shift(lon, 0, 1)
+    lat = shift(lat, 1, 0)
+    diag = shift(diag, 1, 1)
     a_heads, b_heads = a_bias.shape[0], b_bias.shape[0]
     square = ((width, width), BF16)
     plain, late, wq, wk, wvt = call(
         fine_table_kernel, "fine_tables", [edge, a_bias, a_project],
-        [((2, WIN, a_heads * WIN), F32)] * 2 + [square] * 3, [], 16, scalars=1,
+        [((2, WIN, a_heads * WIN), F32)] * 2 + [square] * 3, [], 16, scalars=1, us=3,
     )
     weights = [a_norm_one, wq, wk, wvt, a_output, a_norm_two, a_raise, a_lower.T]
-    scratch = [(levels * WIN_LAT, columns, width), (tokens, width), both, both]
+    scratch = [(levels * WIN_LAT, columns, width), (tokens, width), (3,) + staging, (3,) + staging]
     out = ((tokens, width), F32)
 
     def fine(i, j, halos, outs):
@@ -458,23 +466,19 @@
             fine_kernel(i, j, *refs)
 
         operands = [field, *halos, late if i else plain, *weights]
-        return call(kernel, f"fine_{i}{j}", operands, [out] + outs, scratch, 20)
+        return call(kernel, f"fine_{i}{j}", operands, [out] + outs, scratch, 20, us=5)
 
     (w00,) = fine(0, 0, [], [])
-    lon, w00 = lax.optimization_barrier((lon, w00))
-    lines = (levels * HALF_LAT, columns, width)
-    (lat,) = call(pack_lat, "pack_lat", [field, lon], [(halo, BF16)], [lines, both, both], 16)
-    lon, lat = lax.optimization_barrier((lon, lat))
-    lat = shift(lat, 1, 0)
+    lon, lat, diag, w00 = lax.optimization_barrier((lon, lat, diag, w00))
     w01, lat_two = fine(0, 1, [lon, w00], [(halo, BF16)])
-    lat, lat_two = lax.optimization_barrier((lat, lat_two))
     lat_two = shift(lat_two, 1, 0)
+    lat, w01 = lax.optimization_barrier((lat, w01))
     (w10,) = fine(1, 0, [lat], [])
     lat_two, w10 = lax.optimization_barrier((lat_two, w10))
     (lon_two,) = call(pack_second, "pack_second", [w00, w10, lat_two], [(halo, BF16)], [both, both], 16)
-    lon, lon_two = lax.optimization_barrier((lon, lon_two))
+    diag, lon_two = lax.optimization_barrier((diag, lon_two))
     lon_two = shift(lon_two, 0, 1)
-    (w11,) = fine(1, 1, [lat, lon], [])
+    (w11,) = fine(1, 1, [lat, lon, diag], [])
     late_bias, w11 = lax.optimization_barrier((b_bias, w11))
     (coarse_table,) = call(
         table_kernel, "coarse_table", [edge, late_bias], [((2, WIN, b_heads * WIN), F32)], [], 16, scalars=1
@@ -490,7 +494,7 @@
         ],
         [(halo, BF16)] * 4,
         [both, both, lines, lines, quads, quads, (4, tokens, 2 * MAIN), (tokens, 2 * width), (tokens, 2 * width)],
-        32,
+        32, us=12,
     )
     diag = shift(diag, -1, -1)
     lat = shift(lat, -1, 0)

time: 70.7 us -> 68 us (0.962)
  local copies, waits for them, and re-layouts: 5.74 us -> 3.02 us
    ppermute x1 -> x2, starting transfers between devices: 0.07 us -> 8.35 us  [shift(): return lax.ppermute(array, ('lat', 'lon'), pairs)]
    ppermute x3, starting transfers between devices: 10.3 us -> 5.5 us  [shift(): lax.ppermute(array, 'lat', [((i + lat_by) % lats, i) for i in range(lats)])]
    ppermute x3, starting transfers between devices: 5.54 us -> 1.79 us  [shift(): lax.ppermute(array, 'lon', [((i + lon_by) % lons, i) for i in range(lons)])]
    unnamed x42, local copies, waits for them, and re-layouts: 5.74 us -> 3.02 us
    ppermute x1 -> x2, waiting for transfers between devices: 13.1 us -> 13 us  [shift(): return lax.ppermute(array, ('lat', 'lon'), pairs)]
    pallas_call x11 -> x10, Pallas kernels: 33.4 us -> 33.4 us  [call(): pl.pallas_call(kernel, in_specs=[smem] * scalars + [vmem] * (len(operands...]
  transfers between devices with their start and end apart: 7 -> 8, of which waited for: 2 -> 2; matrix products, arithmetic and copies ran while one was open for 0% -> 0% of each run, Pallas kernels for 27% -> 22%
where the time goes in v3:
time: 68 us; the launch traced here: 67.8 us
  Pallas kernels  33.4 us (49%)
  starting transfers between devices  15.6 us (23%)
  waiting for transfers between devices  15.5 us (23%)
  local copies, waits for them, and re-layouts  3.02 us (4%)
    pallas_call x10, Pallas kernels, call(): pl.pallas_call(kernel, in_specs=[smem] * scalars + [vmem] * (len(operands...  33.4 us
    ppermute x2, waiting for transfers between devices, shift(): return lax.ppermute(array, ('lat', 'lon'), pairs)  13 us
    ppermute x2, starting transfers between devices, shift(): return lax.ppermute(array, ('lat', 'lon'), pairs)  8.35 us
    ppermute x3, starting transfers between devices, shift(): lax.ppermute(array, 'lat', [((i + lat_by) % lats, i) for i in range(lats)])  5.5 us
    unnamed x42, local copies, waits for them, and re-layouts  3.02 us
    ppermute x3, waiting for transfers between devices, shift(): lax.ppermute(array, 'lat', [((i + lat_by) % lats, i) for i in range(lats)])  2.5 us
    ppermute x3, starting transfers between devices, shift(): lax.ppermute(array, 'lon', [((i + lon_by) % lons, i) for i in range(lons)])  1.79 us
  transfers between devices with their start and end apart: 8, of which 2 were waited for; matrix products, arithmetic and copies ran while one was open for 0% of the time, Pallas kernels for 22%

profile of v3, /device:TPU:0, one launch (start us, length us, event | category | flops | bytes accessed | tf_op | source)
XLA Modules:
  0.0 67.8 jit_solution(10086472075696321250)
XLA Ops:
  0.0 1.3 %copy-done.1 = bf16[8,12,24,192]{3,2,1,0:T(8,128)(2,1)S(1)} copy-done((bf16[8,12,24,192]{3,2,1,0:T(8,128)(2,1)S(1)}, bf16[8,12,24,192]{3,2,1,0:T(8,128)(2,1)}, u32[]{:S(2)}) %copy-start.1) | copy-done | bytes 884760
  1.3 0.2 start.1
  1.5 8.3 %collective-permute-start.2 = (bf16[6,48,128]{2,1,0:T(8,128)(2,1)S(1)}, bf16[6,48,128]{2,1,0:T(8,128)(2,1)S(1)}, u32[]{:S(2)}, u32[]{:S(2)}) collective-permute-start(bf16[6,48,128]{2,1,0:T(8,128)(2,1)S(1)} %get-tuple-element.33), channel_id=1, source_target_pairs={{17,0},{18,1},{19,2},{20,3},{21,4},{22,5},{23,6},{24,7},{25,8},{26... | collective-permute-start | bytes 221192 | tf_op jit(solution)/shard_map/ppermute | solution.py:424
  9.8 1.1 %collective-permute-start = (bf16[6,112,128]{2,1,0:T(8,128)(2,1)S(1)}, bf16[6,112,128]{2,1,0:T(8,128)(2,1)S(1)}, u32[]{:S(2)}, u32[]{:S(2)}) collective-permute-start(bf16[6,112,128]{2,1,0:T(8,128)(2,1)S(1)} %get-tuple-element.31), channel_id=1, source_target_pairs={{1,0},{2,1},{3,2},{4,3},{5,4},{6,5},{7,6},{8,7},{9,8},{10,9},{11,1... | collective-permute-start | bytes 516104 | tf_op jit(solution)/shard_map/ppermute | solution.py:427
  10.9 1.4 %collective-permute-start.1 = (bf16[6,112,128]{2,1,0:T(8,128)(2,1)S(1)}, bf16[6,112,128]{2,1,0:T(8,128)(2,1)S(1)}, u32[]{:S(2)}, u32[]{:S(2)}) collective-permute-start(bf16[6,112,128]{2,1,0:T(8,128)(2,1)S(1)} %get-tuple-element.32), channel_id=1, source_target_pairs={{16,0},{32,16},{48,32},{64,48},{80,64},{96,80},{112,96},{0,112},{1... | collective-permute-start | bytes 516104 | tf_op jit(solution)/shard_map/ppermute | solution.py:426
  12.4 0.6 fine_tables.1
  13.0 0.6 copy-done.2
  13.8 4.3 %fine_00.1.refs_2_.w00 = f32[576,192]{1,0:T(8,128)S(1)} custom-call(bf16[8,12,24,192]{3,2,1,0:T(8,128)(2,1)S(1)} %copy-done.2, f32[2,144,864]{2,1,0:T(8,128)S(1)} %get-tuple-element.34.refs_1_.refs_3_, f32[192]{0:T(256)S(1)} %copy-done.18, bf16[192,192]{1,0:T(8,128)(2,1)S(1)} %get-tuple-element.35.refs_3_.refs_5_.refs_4_.refs_6_, ...), custom_call_target="tpu_custom_call" | custom-call | flops 5242880000 | bytes 3208704 | tf_op jit(solution)/shard_map/fine_00/pallas_call | solution.py:400
  18.1 4.5 %fine_01.1 = (f32[576,192]{1,0:T(8,128)S(1)}, bf16[6,144,128]{2,1,0:T(8,128)(2,1)S(1)}) custom-call(bf16[8,12,24,192]{3,2,1,0:T(8,128)(2,1)S(1)} %copy-done.2, bf16[6,112,128]{2,1,0:T(8,128)(2,1)S(1)} %collective-permute-done.refs_1_.refs_2_, f32[576,192]{1,0:T(8,128)S(1)} %fine_00.1.refs_2_.w00, f32[2,144,864]{2,1,0:T(8,128)S(1)} %get-tuple-element.34.refs_1_.refs_3_, ...), custom_call_target="tpu_custom_call" | custom-call | flops 5242880000 | bytes 4044288 | tf_op jit(solution)/shard_map/fine_01/pallas_call | solution.py:400
  22.7 4.0 %collective-permute-start.3 = (bf16[6,144,128]{2,1,0:T(8,128)(2,1)S(1)}, bf16[6,144,128]{2,1,0:T(8,128)(2,1)S(1)}, u32[]{:S(2)}, u32[]{:S(2)}) collective-permute-start(bf16[6,144,128]{2,1,0:T(8,128)(2,1)S(1)} %get-tuple-element.43), channel_id=1, source_target_pairs={{16,0},{32,16},{48,32},{64,48},{80,64},{96,80},{112,96},{0,112},{1... | collective-permute-start | bytes 663560 | tf_op jit(solution)/shard_map/ppermute | solution.py:426
  26.7 4.4 %fine_10.1.w10 = f32[576,192]{1,0:T(8,128)S(1)} custom-call(bf16[8,12,24,192]{3,2,1,0:T(8,128)(2,1)S(1)} %copy-done.2, bf16[6,112,128]{2,1,0:T(8,128)(2,1)S(1)} %collective-permute-done.1.refs_1_, f32[2,144,864]{2,1,0:T(8,128)S(1)} %get-tuple-element.45.refs_2_.refs_4_, f32[192]{0:T(256)S(1)} %copy-done.18, ...), custom_call_target="tpu_custom_call" | custom-call | flops 5242880000 | bytes 3380736 | tf_op jit(solution)/shard_map/fine_10/pallas_call | solution.py:400
  31.1 0.2 pack_second.1
  31.3 0.5 collective-permute-start.4
  31.8 4.5 %fine_11.1.w11 = f32[576,192]{1,0:T(8,128)S(1)} custom-call(bf16[8,12,24,192]{3,2,1,0:T(8,128)(2,1)S(1)} %copy-done.2, bf16[6,112,128]{2,1,0:T(8,128)(2,1)S(1)} %collective-permute-done.1.refs_1_, bf16[6,112,128]{2,1,0:T(8,128)(2,1)S(1)} %collective-permute-done.refs_1_.refs_2_, bf16[6,48,128]{2,1,0:T(8,128)(2,1)S(1)} %collective-permute-done.2.refs_3_, ...), custom_call_target="tpu_custom_call" | custom-call | flops 5242880000 | bytes 3626496 | tf_op jit(solution)/shard_map/fine_11/pallas_call | solution.py:400
  36.4 1.0 %coarse_table.1.table_ref = f32[2,144,1728]{2,1,0:T(8,128)S(1)} custom-call(s32[1]{0:T(128)} %bitcast.edge_ref, f32[12,144,144]{2,1,0:T(8,128)S(1)} %copy-done), custom_call_target="tpu_custom_call" | custom-call | flops 1048576000 | bytes 2985988 | tf_op jit(solution)/shard_map/coarse_table/pallas_call | solution.py:400
  37.4 0.2 copy-done.3
  37.6 0.4 copy-done.4
  37.9 0.3 copy-done.6
  38.2 0.2 copy-done.7
  38.4 12.1 %coarse.1 = (bf16[6,144,128]{2,1,0:T(8,128)(2,1)S(1)}, bf16[6,144,128]{2,1,0:T(8,128)(2,1)S(1)}, bf16[6,144,128]{2,1,0:T(8,128)(2,1)S(1)}, bf16[6,144,128]{2,1,0:T(8,128)(2,1)S(1)}) custom-call(f32[576,192]{1,0:T(8,128)S(1)} %fine_00.1.refs_2_.w00, f32[576,192]{1,0:T(8,128)S(1)} %get-tuple-element.42.w01, f32[576,192]{1,0:T(8,128)S(1)} %fine_10.1.w10, ...), custom_call_target="tpu_custom_call" | custom-call | flops 12582912000 | bytes 9886464 | tf_op jit(solution)/shard_map/coarse/pallas_call | solution.py:400
  50.6 0.1 collective-permute-start.7
  50.8 13.0 %collective-permute-done.5.upper_left = bf16[6,144,128]{2,1,0:T(8,128)(2,1)S(1)} collective-permute-done((bf16[6,144,128]{2,1,0:T(8,128)(2,1)S(1)}, bf16[6,144,128]{2,1,0:T(8,128)(2,1)S(1)}, u32[]{:S(2)}, u32[]{:S(2)}) %collective-permute-start.5) | collective-permute-done | bytes 221216 | tf_op jit(solution)/shard_map/ppermute | solution.py:424
  63.7 2.5 %collective-permute-done.6.upper_right = bf16[6,144,128]{2,1,0:T(8,128)(2,1)S(1)} collective-permute-done((bf16[6,144,128]{2,1,0:T(8,128)(2,1)S(1)}, bf16[6,144,128]{2,1,0:T(8,128)(2,1)S(1)}, u32[]{:S(2)}, u32[]{:S(2)}) %collective-permute-start.6) | collective-permute-done | bytes 221216 | tf_op jit(solution)/shard_map/ppermute | solution.py:426
  66.2 1.6 %finish.1 = bf16[8,12,24,192]{3,2,1,0:T(8,128)(2,1)} custom-call(bf16[6,144,128]{2,1,0:T(8,128)(2,1)S(1)} %collective-permute-done.5.upper_left, bf16[6,144,128]{2,1,0:T(8,128)(2,1)S(1)} %collective-permute-done.6.upper_right, bf16[6,144,128]{2,1,0:T(8,128)(2,1)S(1)} %collective-permute-done.7.lower_left, bf16[6,144,128]{2,1,0:T(8,128)(2,1)S(1)} %get-tuple-element.56.lower_right), custom_call_target="tpu_custom_call" | custom-call | flops 1048576000 | bytes 1769472 | tf_op jit(solution)/shard_map/finish/pallas_call | solution.py:400
  (44 shorter events, 0.4 us)
Async XLA Ops:
  1.3 11.1 %copy-start.5 = (f32[6,144,144]{2,1,0:T(8,128)S(1)}, f32[6,144,144]{2,1,0:T(8,128)}, u32[]{:S(2)}) copy-start(f32[6,144,144]{2,1,0:T(8,128)} %bias.1) | copy-start | bytes 1492996
  1.3 11.1 %copy-start.12 = (bf16[192,576]{1,0:T(8,128)(2,1)S(1)}, bf16[192,576]{1,0:T(8,128)(2,1)}, u32[]{:S(2)}) copy-start(bf16[192,576]{1,0:T(8,128)(2,1)} %project.2) | copy-start | bytes 663556
  1.5 16.6 %collective-permute-start.2 = (bf16[6,48,128]{2,1,0:T(8,128)(2,1)S(1)}, bf16[6,48,128]{2,1,0:T(8,128)(2,1)S(1)}, u32[]{:S(2)}, u32[]{:S(2)}) collective-permute-start(bf16[6,48,128]{2,1,0:T(8,128)(2,1)S(1)} %get-tuple-element.33), channel_id=1, source_target_pairs={{17,0},{18,1},{19,2},{20,3},{21,4},{22,5},{23,6},{24,7},{25,8},{26... | collective-permute-start | bytes 221192 | tf_op jit(solution)/shard_map/ppermute | solution.py:424
  9.8 8.3 %collective-permute-start = (bf16[6,112,128]{2,1,0:T(8,128)(2,1)S(1)}, bf16[6,112,128]{2,1,0:T(8,128)(2,1)S(1)}, u32[]{:S(2)}, u32[]{:S(2)}) collective-permute-start(bf16[6,112,128]{2,1,0:T(8,128)(2,1)S(1)} %get-tuple-element.31), channel_id=1, source_target_pairs={{1,0},{2,1},{3,2},{4,3},{5,4},{6,5},{7,6},{8,7},{9,8},{10,9},{11,1... | collective-permute-start | bytes 516104 | tf_op jit(solution)/shard_map/ppermute | solution.py:427
  10.9 7.2 %collective-permute-start.1 = (bf16[6,112,128]{2,1,0:T(8,128)(2,1)S(1)}, bf16[6,112,128]{2,1,0:T(8,128)(2,1)S(1)}, u32[]{:S(2)}, u32[]{:S(2)}) collective-permute-start(bf16[6,112,128]{2,1,0:T(8,128)(2,1)S(1)} %get-tuple-element.32), channel_id=1, source_target_pairs={{16,0},{32,16},{48,32},{64,48},{80,64},{96,80},{112,96},{0,112},{1... | collective-permute-start | bytes 516104 | tf_op jit(solution)/shard_map/ppermute | solution.py:426
  12.4 1.4 %copy-start.10 = (bf16[768,192]{0,1:T(8,128)(2,1)S(1)}, bf16[768,192]{0,1:T(8,128)(2,1)}, u32[]{:S(2)}) copy-start(bf16[768,192]{0,1:T(8,128)(2,1)} %param.27) | copy-start | bytes 884740
  12.4 1.4 %copy-start.13 = (bf16[192,192]{1,0:T(8,128)(2,1)S(1)}, bf16[192,192]{1,0:T(8,128)(2,1)}, u32[]{:S(2)}) copy-start(bf16[192,192]{1,0:T(8,128)(2,1)} %refs_9_.5) | copy-start | bytes 221188
  12.4 1.4 %copy-start.18 = (f32[192]{0:T(256)S(1)}, f32[192]{0:T(256)}, u32[]{:S(2)}) copy-start(f32[192]{0:T(256)} %refs_5_.1) | copy-start | bytes 2308
  22.7 8.4 %collective-permute-start.3 = (bf16[6,144,128]{2,1,0:T(8,128)(2,1)S(1)}, bf16[6,144,128]{2,1,0:T(8,128)(2,1)S(1)}, u32[]{:S(2)}, u32[]{:S(2)}) collective-permute-start(bf16[6,144,128]{2,1,0:T(8,128)(2,1)S(1)} %get-tuple-element.43), channel_id=1, source_target_pairs={{16,0},{32,16},{48,32},{64,48},{80,64},{96,80},{112,96},{0,112},{1... | collective-permute-start | bytes 663560 | tf_op jit(solution)/shard_map/ppermute | solution.py:426
  31.3 5.0 %copy-start = (f32[12,144,144]{2,1,0:T(8,128)S(1)}, f32[12,144,144]{2,1,0:T(8,128)}, u32[]{:S(2)}) copy-start(f32[12,144,144]{2,1,0:T(8,128)} %bias.2) | copy-start | bytes 2985988
  31.3 6.1 %collective-permute-start.4 = (bf16[6,144,128]{2,1,0:T(8,128)(2,1)S(1)}, bf16[6,144,128]{2,1,0:T(8,128)(2,1)S(1)}, u32[]{:S(2)}, u32[]{:S(2)}) collective-permute-start(bf16[6,144,128]{2,1,0:T(8,128)(2,1)S(1)} %pack_second.1), channel_id=1, source_target_pairs={{1,0},{2,1},{3,2},{4,3},{5,4},{6,5},{7,6},{8,7},{9,8},{10,9},{11,1... | collective-permute-start | bytes 663560 | tf_op jit(solution)/shard_map/ppermute | solution.py:427
  31.8 5.6 %copy-start.8 = (bf16[384,768]{1,0:T(8,128)(2,1)S(1)}, bf16[384,768]{1,0:T(8,128)(2,1)}, u32[]{:S(2)}) copy-start(bf16[384,768]{1,0:T(8,128)(2,1)} %up_first.1) | copy-start | bytes 1769476
  31.8 5.6 %copy-start.11 = (bf16[384,384]{1,0:T(8,128)(2,1)S(1)}, bf16[384,384]{1,0:T(8,128)(2,1)}, u32[]{:S(2)}) copy-start(bf16[384,384]{1,0:T(8,128)(2,1)} %wo.1) | copy-start | bytes 884740
  31.8 5.6 %copy-start.14 = (bf16[192,192]{1,0:T(8,128)(2,1)S(1)}, bf16[192,192]{1,0:T(8,128)(2,1)}, u32[]{:S(2)}) copy-start(bf16[192,192]{1,0:T(8,128)(2,1)} %up_second.1) | copy-start | bytes 221188
  36.3 1.6 %copy-start.4 = (bf16[1536,384]{1,0:T(8,128)(2,1)S(1)}, bf16[1536,384]{1,0:T(8,128)(2,1)}, u32[]{:S(2)}) copy-start(bf16[1536,384]{1,0:T(8,128)(2,1)} %w2.1) | copy-start | bytes 3538948
  36.3 1.9 %copy-start.6 = (bf16[384,1152]{1,0:T(8,128)(2,1)S(1)}, bf16[384,1152]{1,0:T(8,128)(2,1)}, u32[]{:S(2)}) copy-start(bf16[384,1152]{1,0:T(8,128)(2,1)} %project.3) | copy-start | bytes 2654212
  36.4 2.0 %copy-start.7 = (bf16[768,384]{1,0:T(8,128)(2,1)S(1)}, bf16[768,384]{1,0:T(8,128)(2,1)}, u32[]{:S(2)}) copy-start(bf16[768,384]{1,0:T(8,128)(2,1)} %merge_weight.1) | copy-start | bytes 1769476
  36.4 2.0 %copy-start.15 = (f32[768]{0:T(1024)S(1)}, f32[768]{0:T(1024)}, u32[]{:S(2)}) copy-start(f32[768]{0:T(1024)} %merge_gain.1) | copy-start | bytes 9220
  36.4 2.0 %copy-start.16 = (f32[384]{0:T(512)S(1)}, f32[384]{0:T(512)}, u32[]{:S(2)}) copy-start(f32[384]{0:T(512)} %gain_one.1) | copy-start | bytes 4612
  36.4 2.0 %copy-start.17 = (f32[384]{0:T(512)S(1)}, f32[384]{0:T(512)}, u32[]{:S(2)}) copy-start(f32[384]{0:T(512)} %gain_two.1) | copy-start | bytes 4612
  36.4 2.0 %copy-start.20 = (f32[192]{0:T(256)S(1)}, f32[192]{0:T(256)}, u32[]{:S(2)}) copy-start(f32[192]{0:T(256)} %up_norm.1) | copy-start | bytes 2308
  50.5 13.3 %collective-permute-start.5 = (bf16[6,144,128]{2,1,0:T(8,128)(2,1)S(1)}, bf16[6,144,128]{2,1,0:T(8,128)(2,1)S(1)}, u32[]{:S(2)}, u32[]{:S(2)}) collective-permute-start(bf16[6,144,128]{2,1,0:T(8,128)(2,1)S(1)} %get-tuple-element.53), channel_id=1, source_target_pairs={{127,0},{112,1},{113,2},{114,3},{115,4},{116,5},{117,6},{118,7},{1... | collective-permute-start | bytes 663560 | tf_op jit(solution)/shard_map/ppermute | solution.py:424
  50.6 15.7 %collective-permute-start.6 = (bf16[6,144,128]{2,1,0:T(8,128)(2,1)S(1)}, bf16[6,144,128]{2,1,0:T(8,128)(2,1)S(1)}, u32[]{:S(2)}, u32[]{:S(2)}) collective-permute-start(bf16[6,144,128]{2,1,0:T(8,128)(2,1)S(1)} %get-tuple-element.54), channel_id=1, source_target_pairs={{112,0},{0,16},{16,32},{32,48},{48,64},{64,80},{80,96},{96,112},{1... | collective-permute-start | bytes 663560 | tf_op jit(solution)/shard_map/ppermute | solution.py:426
  50.6 15.6 %collective-permute-start.7 = (bf16[6,144,128]{2,1,0:T(8,128)(2,1)S(1)}, bf16[6,144,128]{2,1,0:T(8,128)(2,1)S(1)}, u32[]{:S(2)}, u32[]{:S(2)}) collective-permute-start(bf16[6,144,128]{2,1,0:T(8,128)(2,1)S(1)} %get-tuple-element.55), channel_id=1, source_target_pairs={{15,0},{0,1},{1,2},{2,3},{3,4},{4,5},{5,6},{6,7},{7,8},{8,9},{9,10... | collective-permute-start | bytes 663560 | tf_op jit(solution)/shard_map/ppermute | solution.py:427
  (5 other events, 6.5 us)

commit v4 on v3

--- a/solution.py
+++ b/solution.py
@@ -112,7 +112,7 @@
     return jnp.concatenate([main_out.astype(BF16), rest_out.astype(BF16)], axis=1)
 
 
-def block_rows(x_ref, count, table_ref, heads, gain_one, wq, wk, wvt, wo, gain_two, w1, w2, w2_dims, out_ref):
+def block_rows(x_ref, count, table_ref, heads, gain_one, wq, wk, wvt, wo, gain_two, w1, w2, w2_dims, out_ref, ends=True):
     x = x_ref[...]
     xn = layer_norm(x, gain_one[...][None, :]).astype(BF16)
     q = (dot(xn, wq) * (LOG2E / math.sqrt(HEAD))).astype(BF16)
@@ -121,7 +121,7 @@
     for w in range(count):
         rows = slice(w * WIN, (w + 1) * WIN)
         vt = dot(wvt, xn[rows], ((1,), (1,))).astype(BF16)
-        table = table_ref.at[1 if w == count - 1 else 0]
+        table = table_ref.at[1 if ends and w == count - 1 else 0]
         attended = attend(q[rows], k[rows], vt, table, heads, 4 if heads == 6 else 2)
         mixed.append(dot(attended, wo[...], ((0,), (0,))))
     after = (x + jnp.concatenate(mixed, axis=0)).astype(BF16).astype(F32)
@@ -152,15 +152,15 @@
             sides = [self.high[p + s * half, rows, : MAIN // 2] for s in range(2)]
             out_ref[self.pairs + p] = jnp.concatenate(sides, axis=1).astype(BF16)
 
-    def load(self, in_ref):
-        half = self.pairs // 2
+    def load(self, in_ref, first=0):
+        pairs = in_ref.shape[0] * 2 // 3
+        half = pairs // 2
         rows = slice(0, self.rows)
         for p in range(self.pairs):
-            self.low[p, rows, :] = in_ref[p].astype(F32)
-        for p in range(half):
-            both = in_ref[self.pairs + p].astype(F32)
-            for s in range(2):
-                self.high[p + s * half, rows, : MAIN // 2] = both[:, s * MAIN // 2 : (s + 1) * MAIN // 2]
+            self.low[p, rows, :] = in_ref[first + p].astype(F32)
+            side, row = divmod(first + p, half)
+            both = in_ref[pairs + row].astype(F32)
+            self.high[p, rows, : MAIN // 2] = both[:, side * MAIN // 2 : (side + 1) * MAIN // 2]
         return self
 
 
@@ -287,7 +287,7 @@
 
 
 def coarse_kernel(
-    w00, w01, w10, w11, lat_in, lon_in, table_ref,
+    first, w00, w01, w10, w11, lat_in, lon_in, table_ref,
     merge_gain, merge_weight,
     gain_one, project, wo, gain_two, w1, w2,
     up_first, up_norm, up_second,
@@ -297,10 +297,12 @@
     heads = 12
     width = w00.shape[1]
     rows, columns = 2 * WIN_LAT, 2 * WIN_LON
-    pairs = w00.shape[0] // WIN
+    pairs = x_ref.shape[0] // WIN
     levels = pairs * WIN_P
     windows = ((w00, w01), (w10, w11))
-    lat, lon = [Packed(low_ref.at[n], high_ref.at[n], ref.shape[1]).load(ref) for n, ref in enumerate((lat_in, lon_in))]
+    lat, lon = [
+        Packed(low_ref.at[n], high_ref.at[n], ref.shape[1]).load(ref, first) for n, ref in enumerate((lat_in, lon_in))
+    ]
 
     def put(at, value):
         grid_low[at : at + value.shape[0], :] = value[:, :MAIN]
@@ -312,7 +314,7 @@
                 at = ((p * WIN_P + lev) * rows + row) * PITCH
                 if row + HALF_LAT < rows:
                     left, right = windows[(row + HALF_LAT) // WIN_LAT]
-                    here = ((p * WIN_P + lev) * WIN_LAT + (row + HALF_LAT) % WIN_LAT) * WIN_LON
+                    here = (((first + p) * WIN_P + lev) * WIN_LAT + (row + HALF_LAT) % WIN_LAT) * WIN_LON
                     put(at + HALF_LON, left[here + HALF_LON : here + WIN_LON, :])
                     put(at + WIN_LON, right[here : here + WIN_LON, :])
                 else:
@@ -347,7 +349,7 @@
     wvt = project[:, 2 * double :].astype(F32).T.astype(BF16)
     block_rows(
         x_ref, pairs, table_ref, heads, gain_one, project[:, :double], project[:, double : 2 * double], wvt,
-        wo, gain_two, w1, w2, ((1,), (0,)), y_ref,
+        wo, gain_two, w1, w2, ((1,), (0,)), y_ref, first + pairs == w00.shape[0] // WIN,
     )
     coarse = y_ref[...].astype(BF16)
     half = rows // 2
@@ -371,13 +373,17 @@
         Packed(quad_low.at[quad], quad_high.at[quad], WIN).store(ref)
 
 
-def finish_kernel(upper_left, upper_right, lower_left, lower_right, out_ref, low_ref, high_ref, line_low, line_high):
+def finish_kernel(*refs):
+    quarters = refs[:-5]
+    out_ref, low_ref, high_ref, line_low, line_high = refs[-5:]
     levels, rows, columns, width = out_ref.shape
     half = rows // 2
-    for quad, ref in enumerate((upper_left, upper_right, lower_left, lower_right)):
-        pack = Packed(low_ref.at[quad], high_ref.at[quad], WIN).load(ref)
-        for p in range(levels // WIN_P):
-            for lev, level in enumerate(pair_levels(p, levels)):
+    pairs = low_ref.shape[1]
+    for n, ref in enumerate(quarters):
+        part, quad = divmod(n, 4)
+        pack = Packed(low_ref.at[n], high_ref.at[n], WIN).load(ref)
+        for p in range(pairs):
+            for lev, level in enumerate(pair_levels(part * pairs + p, levels)):
                 for row in range(half):
                     at = (level * rows + (quad // 2) * half + row) * columns + quad % 2 * WIN_LON
                     here = (lev * half + row) * WIN_LON
@@ -484,25 +490,33 @@
         table_kernel, "coarse_table", [edge, late_bias], [((2, WIN, b_heads * WIN), F32)], [], 16, scalars=1
     )
 
-    quads = (4,) + staging
-    lines = (levels * rows * PITCH, MAIN)
-    stay, lat, lon, diag = call(
-        coarse_kernel, "coarse",
-        [
-            w00, w01, w10, w11, lat_two, lon_two, coarse_table, merge_norm_gain, merge_weight,
-            b_norm_one, b_project, b_output, b_norm_two, b_raise, b_lower, up_first, up_norm, up_second,
-        ],
-        [(halo, BF16)] * 4,
-        [both, both, lines, lines, quads, quads, (4, tokens, 2 * MAIN), (tokens, 2 * width), (tokens, 2 * width)],
-        32, us=12,
-    )
-    diag = shift(diag, -1, -1)
-    lat = shift(lat, -1, 0)
-    lon = shift(lon, 0, -1)
+    part = pairs // 2
+    part_halo = (2, part, WIN, MAIN)
+    quads = (4, part, WIN, MAIN)
+    lines = (part * WIN_P * rows * PITCH, MAIN)
+
+    def coarse(first):
+        def kernel(*refs):
+            coarse_kernel(first, *refs)
+
+        return call(
+            kernel, f"coarse_{first}",
+            [
+                w00, w01, w10, w11, lat_two, lon_two, coarse_table, merge_norm_gain, merge_weight,
+                b_norm_one, b_project, b_output, b_norm_two, b_raise, b_lower, up_first, up_norm, up_second,
+            ],
+            [(packed_shape(WIN, part), BF16)] * 4,
+            [part_halo, part_halo, lines, lines, quads, quads, (4, part * WIN, 2 * MAIN)] + [(part * WIN, 2 * width)] * 2,
+            32, us=7,
+        )
+
+    quarters = []
+    for first in range(0, pairs, part):
+        stay, lat, lon, diag = coarse(first)
+        quarters += [shift(diag, -1, -1), shift(lat, -1, 0), shift(lon, 0, -1), stay]
+    quads = (8, part, WIN, MAIN)
     lines = (levels * rows * columns, MAIN)
-    (fine_out,) = call(
-        finish_kernel, "finish", [diag, lat, lon, stay], [(field.shape, BF16)], [quads, quads, lines, lines], 24
-    )
+    (fine_out,) = call(finish_kernel, "finish", quarters, [(field.shape, BF16)], [quads, quads, lines, lines], 24)
     return fine_out
 
 

time: 68 us -> 69.1 us (1.016)
  waiting for transfers between devices: 15.5 us -> 9.26 us
  starting transfers between devices: 15.6 us -> 20.8 us
  Pallas kernels: 33.4 us -> 35.3 us
    ppermute x2 -> x3, starting transfers between devices: 8.35 us -> 1.4 us  [shift(): return lax.ppermute(array, ('lat', 'lon'), pairs)]
    ppermute x3 -> x4, starting transfers between devices: 1.79 us -> 8.55 us  [shift(): lax.ppermute(array, 'lon', [((i + lon_by) % lons, i) for i in range(lons)])]
    ppermute x3 -> x4, starting transfers between devices: 5.5 us -> 10.9 us  [shift(): lax.ppermute(array, 'lat', [((i + lat_by) % lats, i) for i in range(lats)])]
    ppermute x2 -> x3, waiting for transfers between devices: 13 us -> 8.4 us  [shift(): return lax.ppermute(array, ('lat', 'lon'), pairs)]
    ppermute x3 -> x4, waiting for transfers between devices: 2.5 us -> 0.01 us  [shift(): lax.ppermute(array, 'lat', [((i + lat_by) % lats, i) for i in range(lats)])]
    pallas_call x10 -> x11, Pallas kernels: 33.4 us -> 35.3 us  [call(): pl.pallas_call(kernel, in_specs=[smem] * scalars + [vmem] * (len(operands...]
    ppermute x3 -> x4, waiting for transfers between devices: 0.01 us -> 0.85 us  [shift(): lax.ppermute(array, 'lon', [((i + lon_by) % lons, i) for i in range(lons)])]
  transfers between devices with their start and end apart: 8 -> 11, of which waited for: 2 -> 3; matrix products, arithmetic and copies ran while one was open for 0% -> 0% of each run, Pallas kernels for 22% -> 32%
where the time goes in v4:
time: 69.1 us; the launch traced here: 68.7 us
  Pallas kernels  35.3 us (51%)
  starting transfers between devices  20.8 us (30%)
  waiting for transfers between devices  9.26 us (13%)
  local copies, waits for them, and re-layouts  3.01 us (4%)
    pallas_call x11, Pallas kernels, call(): pl.pallas_call(kernel, in_specs=[smem] * scalars + [vmem] * (len(operands...  35.3 us
    ppermute x4, starting transfers between devices, shift(): lax.ppermute(array, 'lat', [((i + lat_by) % lats, i) for i in range(lats)])  10.9 us
    ppermute x4, starting transfers between devices, shift(): lax.ppermute(array, 'lon', [((i + lon_by) % lons, i) for i in range(lons)])  8.55 us
    ppermute x3, waiting for transfers between devices, shift(): return lax.ppermute(array, ('lat', 'lon'), pairs)  8.4 us
    unnamed x42, local copies, waits for them, and re-layouts  3.01 us
    ppermute x3, starting transfers between devices, shift(): return lax.ppermute(array, ('lat', 'lon'), pairs)  1.4 us
  transfers between devices with their start and end apart: 11, of which 3 were waited for; matrix products, arithmetic and copies ran while one was open for 0% of the time, Pallas kernels for 32%

profile of v4, /device:TPU:0, one launch (start us, length us, event | category | flops | bytes accessed | tf_op | source)
XLA Modules:
  0.0 68.7 jit_solution(2536444683689416450)
XLA Ops:
  0.0 1.3 %copy-done.1 = bf16[8,12,24,192]{3,2,1,0:T(8,128)(2,1)S(1)} copy-done((bf16[8,12,24,192]{3,2,1,0:T(8,128)(2,1)S(1)}, bf16[8,12,24,192]{3,2,1,0:T(8,128)(2,1)}, u32[]{:S(2)}) %copy-start.1) | copy-done | bytes 884760
  1.5 4.6 %collective-permute-start = (bf16[6,112,128]{2,1,0:T(8,128)(2,1)S(1)}, bf16[6,112,128]{2,1,0:T(8,128)(2,1)S(1)}, u32[]{:S(2)}, u32[]{:S(2)}) collective-permute-start(bf16[6,112,128]{2,1,0:T(8,128)(2,1)S(1)} %get-tuple-element.35), channel_id=1, source_target_pairs={{1,0},{2,1},{3,2},{4,3},{5,4},{6,5},{7,6},{8,7},{9,8},{10,9},{11,1... | collective-permute-start | bytes 516104 | tf_op jit(solution)/shard_map/ppermute | solution.py:433
  6.1 5.1 %collective-permute-start.1 = (bf16[6,112,128]{2,1,0:T(8,128)(2,1)S(1)}, bf16[6,112,128]{2,1,0:T(8,128)(2,1)S(1)}, u32[]{:S(2)}, u32[]{:S(2)}) collective-permute-start(bf16[6,112,128]{2,1,0:T(8,128)(2,1)S(1)} %get-tuple-element.36), channel_id=1, source_target_pairs={{16,0},{32,16},{48,32},{64,48},{80,64},{96,80},{112,96},{0,112},{1... | collective-permute-start | bytes 516104 | tf_op jit(solution)/shard_map/ppermute | solution.py:432
  11.3 0.6 fine_tables.1
  12.0 0.6 copy-done.2
  12.7 4.3 %fine_00.1.refs_2_.w00.refs_0_ = f32[576,192]{1,0:T(8,128)S(1)} custom-call(bf16[8,12,24,192]{3,2,1,0:T(8,128)(2,1)S(1)} %copy-done.2, f32[2,144,864]{2,1,0:T(8,128)S(1)} %get-tuple-element.38.refs_1_.refs_3_, f32[192]{0:T(256)S(1)} %copy-done.18, bf16[192,192]{1,0:T(8,128)(2,1)S(1)} %get-tuple-element.39.refs_3_.refs_5_.refs_4_.refs_6_, ...), custom_call_target="tpu_custom_call" | custom-call | flops 5242880000 | bytes 3208704 | tf_op jit(solution)/shard_map/fine_00/pallas_call | solution.py:406
  17.0 4.5 %fine_01.1 = (f32[576,192]{1,0:T(8,128)S(1)}, bf16[6,144,128]{2,1,0:T(8,128)(2,1)S(1)}) custom-call(bf16[8,12,24,192]{3,2,1,0:T(8,128)(2,1)S(1)} %copy-done.2, bf16[6,112,128]{2,1,0:T(8,128)(2,1)S(1)} %collective-permute-done.refs_1_.refs_2_, f32[576,192]{1,0:T(8,128)S(1)} %fine_00.1.refs_2_.w00.refs_0_, ...), custom_call_target="tpu_custom_call" | custom-call | flops 5242880000 | bytes 4044288 | tf_op jit(solution)/shard_map/fine_01/pallas_call | solution.py:406
  21.6 5.0 %collective-permute-start.3 = (bf16[6,144,128]{2,1,0:T(8,128)(2,1)S(1)}, bf16[6,144,128]{2,1,0:T(8,128)(2,1)S(1)}, u32[]{:S(2)}, u32[]{:S(2)}) collective-permute-start(bf16[6,144,128]{2,1,0:T(8,128)(2,1)S(1)} %get-tuple-element.47), channel_id=1, source_target_pairs={{16,0},{32,16},{48,32},{64,48},{80,64},{96,80},{112,96},{0,112},{1... | collective-permute-start | bytes 663560 | tf_op jit(solution)/shard_map/ppermute | solution.py:432
  26.6 4.4 %fine_10.1.w10.refs_2_ = f32[576,192]{1,0:T(8,128)S(1)} custom-call(bf16[8,12,24,192]{3,2,1,0:T(8,128)(2,1)S(1)} %copy-done.2, bf16[6,112,128]{2,1,0:T(8,128)(2,1)S(1)} %collective-permute-done.1.refs_1_, f32[2,144,864]{2,1,0:T(8,128)S(1)} %get-tuple-element.49.refs_2_.refs_4_, f32[192]{0:T(256)S(1)} %copy-done.18, ...), custom_call_target="tpu_custom_call" | custom-call | flops 5242880000 | bytes 3380736 | tf_op jit(solution)/shard_map/fine_10/pallas_call | solution.py:406
  31.2 2.1 %collective-permute-start.4 = (bf16[6,144,128]{2,1,0:T(8,128)(2,1)S(1)}, bf16[6,144,128]{2,1,0:T(8,128)(2,1)S(1)}, u32[]{:S(2)}, u32[]{:S(2)}) collective-permute-start(bf16[6,144,128]{2,1,0:T(8,128)(2,1)S(1)} %pack_second.1), channel_id=1, source_target_pairs={{1,0},{2,1},{3,2},{4,3},{5,4},{6,5},{7,6},{8,7},{9,8},{10,9},{11,1... | collective-permute-start | bytes 663560 | tf_op jit(solution)/shard_map/ppermute | solution.py:433
  33.3 4.5 %fine_11.1.refs_3_ = f32[576,192]{1,0:T(8,128)S(1)} custom-call(bf16[8,12,24,192]{3,2,1,0:T(8,128)(2,1)S(1)} %copy-done.2, bf16[6,112,128]{2,1,0:T(8,128)(2,1)S(1)} %collective-permute-done.1.refs_1_, bf16[6,112,128]{2,1,0:T(8,128)(2,1)S(1)} %collective-permute-done.refs_1_.refs_2_, bf16[6,48,128]{2,1,0:T(8,128)(2,1)S(1)} %collective-permute-done.2.refs_3_, ...), custom_call_target="tpu_custom_call" | custom-call | flops 5242880000 | bytes 3626496 | tf_op jit(solution)/shard_map/fine_11/pallas_call | solution.py:406
  37.9 1.0 %coarse_table.1.refs_6_ = f32[2,144,1728]{2,1,0:T(8,128)S(1)} custom-call(s32[1]{0:T(128)} %bitcast.edge_ref, f32[12,144,144]{2,1,0:T(8,128)S(1)} %copy-done), custom_call_target="tpu_custom_call" | custom-call | flops 1048576000 | bytes 2985988 | tf_op jit(solution)/shard_map/coarse_table/pallas_call | solution.py:406
  39.1 0.4 copy-done.4
  39.5 0.3 copy-done.6
  39.9 7.0 %coarse_2.1 = (bf16[3,144,128]{2,1,0:T(8,128)(2,1)S(1)}, bf16[3,144,128]{2,1,0:T(8,128)(2,1)S(1)}, bf16[3,144,128]{2,1,0:T(8,128)(2,1)S(1)}, bf16[3,144,128]{2,1,0:T(8,128)(2,1)S(1)}) custom-call(f32[576,192]{1,0:T(8,128)S(1)} %fine_00.1.refs_2_.w00.refs_0_, f32[576,192]{1,0:T(8,128)S(1)} %get-tuple-element.46.refs_1_, f32[576,192]{1,0:T(8,128)S(1)} %fine_10.1.w10.refs_2_, ...), custom_call_target="tpu_custom_call" | custom-call | flops 7340032000 | bytes 9444096 | tf_op jit(solution)/shard_map/coarse_2/pallas_call | solution.py:406
  47.0 0.3 collective-permute-start.9
  47.3 7.0 %coarse_0.1 = (bf16[3,144,128]{2,1,0:T(8,128)(2,1)S(1)}, bf16[3,144,128]{2,1,0:T(8,128)(2,1)S(1)}, bf16[3,144,128]{2,1,0:T(8,128)(2,1)S(1)}, bf16[3,144,128]{2,1,0:T(8,128)(2,1)S(1)}) custom-call(f32[576,192]{1,0:T(8,128)S(1)} %fine_00.1.refs_2_.w00.refs_0_, f32[576,192]{1,0:T(8,128)S(1)} %get-tuple-element.46.refs_1_, f32[576,192]{1,0:T(8,128)S(1)} %fine_10.1.w10.refs_2_, ...), custom_call_target="tpu_custom_call" | custom-call | flops 7340032000 | bytes 9444096 | tf_op jit(solution)/shard_map/coarse_0/pallas_call | solution.py:406
  54.3 1.3 %collective-permute-start.5 = (bf16[3,144,128]{2,1,0:T(8,128)(2,1)S(1)}, bf16[3,144,128]{2,1,0:T(8,128)(2,1)S(1)}, u32[]{:S(2)}, u32[]{:S(2)}) collective-permute-start(bf16[3,144,128]{2,1,0:T(8,128)(2,1)S(1)} %get-tuple-element.57), channel_id=1, source_target_pairs={{127,0},{112,1},{113,2},{114,3},{115,4},{116,5},{117,6},{118,7},{1... | collective-permute-start | bytes 331784 | tf_op jit(solution)/shard_map/ppermute | solution.py:430
  55.6 0.4 collective-permute-start.6
  56.0 1.8 %collective-permute-start.7 = (bf16[3,144,128]{2,1,0:T(8,128)(2,1)S(1)}, bf16[3,144,128]{2,1,0:T(8,128)(2,1)S(1)}, u32[]{:S(2)}, u32[]{:S(2)}) collective-permute-start(bf16[3,144,128]{2,1,0:T(8,128)(2,1)S(1)} %get-tuple-element.59), channel_id=1, source_target_pairs={{15,0},{0,1},{1,2},{2,3},{3,4},{4,5},{5,6},{6,7},{7,8},{8,9},{9,10... | collective-permute-start | bytes 331784 | tf_op jit(solution)/shard_map/ppermute | solution.py:433
  57.8 1.4 %collective-permute-done.8.refs_4_ = bf16[3,144,128]{2,1,0:T(8,128)(2,1)S(1)} collective-permute-done((bf16[3,144,128]{2,1,0:T(8,128)(2,1)S(1)}, bf16[3,144,128]{2,1,0:T(8,128)(2,1)S(1)}, u32[]{:S(2)}, u32[]{:S(2)}) %collective-permute-start.8) | collective-permute-done | bytes 110624 | tf_op jit(solution)/shard_map/ppermute | solution.py:430
  59.2 7.0 %collective-permute-done.5.refs_0_ = bf16[3,144,128]{2,1,0:T(8,128)(2,1)S(1)} collective-permute-done((bf16[3,144,128]{2,1,0:T(8,128)(2,1)S(1)}, bf16[3,144,128]{2,1,0:T(8,128)(2,1)S(1)}, u32[]{:S(2)}, u32[]{:S(2)}) %collective-permute-start.5) | collective-permute-done | bytes 110624 | tf_op jit(solution)/shard_map/ppermute | solution.py:430
  66.2 0.8 %collective-permute-done.7.refs_2_ = bf16[3,144,128]{2,1,0:T(8,128)(2,1)S(1)} collective-permute-done((bf16[3,144,128]{2,1,0:T(8,128)(2,1)S(1)}, bf16[3,144,128]{2,1,0:T(8,128)(2,1)S(1)}, u32[]{:S(2)}, u32[]{:S(2)}) %collective-permute-start.7) | collective-permute-done | bytes 110624 | tf_op jit(solution)/shard_map/ppermute | solution.py:433
  67.1 1.7 %finish.1 = bf16[8,12,24,192]{3,2,1,0:T(8,128)(2,1)} custom-call(bf16[3,144,128]{2,1,0:T(8,128)(2,1)S(1)} %collective-permute-done.5.refs_0_, bf16[3,144,128]{2,1,0:T(8,128)(2,1)S(1)} %collective-permute-done.6.refs_1_, bf16[3,144,128]{2,1,0:T(8,128)(2,1)S(1)} %collective-permute-done.7.refs_2_, bf16[3,144,128]{2,1,0:T(8,128)(2,1)S(1)} %get-tuple-element.60.refs_3_, ...), custom_call_target="tpu_custom_call" | custom-call | flops 1048576000 | bytes 1769472 | tf_op jit(solution)/shard_map/finish/pallas_call | solution.py:406
  (51 shorter events, 1.2 us)
Async XLA Ops:
  1.3 10.0 %copy-start.5 = (f32[6,144,144]{2,1,0:T(8,128)S(1)}, f32[6,144,144]{2,1,0:T(8,128)}, u32[]{:S(2)}) copy-start(f32[6,144,144]{2,1,0:T(8,128)} %bias.1) | copy-start | bytes 1492996
  1.3 10.0 %copy-start.12 = (bf16[192,576]{1,0:T(8,128)(2,1)S(1)}, bf16[192,576]{1,0:T(8,128)(2,1)}, u32[]{:S(2)}) copy-start(bf16[192,576]{1,0:T(8,128)(2,1)} %project.1) | copy-start | bytes 663556
  1.5 15.5 %collective-permute-start = (bf16[6,112,128]{2,1,0:T(8,128)(2,1)S(1)}, bf16[6,112,128]{2,1,0:T(8,128)(2,1)S(1)}, u32[]{:S(2)}, u32[]{:S(2)}) collective-permute-start(bf16[6,112,128]{2,1,0:T(8,128)(2,1)S(1)} %get-tuple-element.35), channel_id=1, source_target_pairs={{1,0},{2,1},{3,2},{4,3},{5,4},{6,5},{7,6},{8,7},{9,8},{10,9},{11,1... | collective-permute-start | bytes 516104 | tf_op jit(solution)/shard_map/ppermute | solution.py:433
  6.1 10.9 %collective-permute-start.1 = (bf16[6,112,128]{2,1,0:T(8,128)(2,1)S(1)}, bf16[6,112,128]{2,1,0:T(8,128)(2,1)S(1)}, u32[]{:S(2)}, u32[]{:S(2)}) collective-permute-start(bf16[6,112,128]{2,1,0:T(8,128)(2,1)S(1)} %get-tuple-element.36), channel_id=1, source_target_pairs={{16,0},{32,16},{48,32},{64,48},{80,64},{96,80},{112,96},{0,112},{1... | collective-permute-start | bytes 516104 | tf_op jit(solution)/shard_map/ppermute | solution.py:432
  11.2 5.8 %collective-permute-start.2 = (bf16[6,48,128]{2,1,0:T(8,128)(2,1)S(1)}, bf16[6,48,128]{2,1,0:T(8,128)(2,1)S(1)}, u32[]{:S(2)}, u32[]{:S(2)}) collective-permute-start(bf16[6,48,128]{2,1,0:T(8,128)(2,1)S(1)} %get-tuple-element.37), channel_id=1, source_target_pairs={{17,0},{18,1},{19,2},{20,3},{21,4},{22,5},{23,6},{24,7},{25,8},{26... | collective-permute-start | bytes 221192 | tf_op jit(solution)/shard_map/ppermute | solution.py:430
  21.6 9.4 %collective-permute-start.3 = (bf16[6,144,128]{2,1,0:T(8,128)(2,1)S(1)}, bf16[6,144,128]{2,1,0:T(8,128)(2,1)S(1)}, u32[]{:S(2)}, u32[]{:S(2)}) collective-permute-start(bf16[6,144,128]{2,1,0:T(8,128)(2,1)S(1)} %get-tuple-element.47), channel_id=1, source_target_pairs={{16,0},{32,16},{48,32},{64,48},{80,64},{96,80},{112,96},{0,112},{1... | collective-permute-start | bytes 663560 | tf_op jit(solution)/shard_map/ppermute | solution.py:432
  31.2 6.6 %copy-start = (f32[12,144,144]{2,1,0:T(8,128)S(1)}, f32[12,144,144]{2,1,0:T(8,128)}, u32[]{:S(2)}) copy-start(f32[12,144,144]{2,1,0:T(8,128)} %bias.2) | copy-start | bytes 2985988
  31.2 7.7 %collective-permute-start.4 = (bf16[6,144,128]{2,1,0:T(8,128)(2,1)S(1)}, bf16[6,144,128]{2,1,0:T(8,128)(2,1)S(1)}, u32[]{:S(2)}, u32[]{:S(2)}) collective-permute-start(bf16[6,144,128]{2,1,0:T(8,128)(2,1)S(1)} %pack_second.1), channel_id=1, source_target_pairs={{1,0},{2,1},{3,2},{4,3},{5,4},{6,5},{7,6},{8,7},{9,8},{10,9},{11,1... | collective-permute-start | bytes 663560 | tf_op jit(solution)/shard_map/ppermute | solution.py:433
  33.3 5.6 %copy-start.8 = (bf16[384,768]{1,0:T(8,128)(2,1)S(1)}, bf16[384,768]{1,0:T(8,128)(2,1)}, u32[]{:S(2)}) copy-start(bf16[384,768]{1,0:T(8,128)(2,1)} %refs_15_.3) | copy-start | bytes 1769476
  33.3 5.6 %copy-start.11 = (bf16[384,384]{1,0:T(8,128)(2,1)S(1)}, bf16[384,384]{1,0:T(8,128)(2,1)}, u32[]{:S(2)}) copy-start(bf16[384,384]{1,0:T(8,128)(2,1)} %refs_11_.5) | copy-start | bytes 884740
  33.3 5.6 %copy-start.14 = (bf16[192,192]{1,0:T(8,128)(2,1)S(1)}, bf16[192,192]{1,0:T(8,128)(2,1)}, u32[]{:S(2)}) copy-start(bf16[192,192]{1,0:T(8,128)(2,1)} %refs_17_.3) | copy-start | bytes 221188
  37.8 1.6 %copy-start.4 = (bf16[1536,384]{1,0:T(8,128)(2,1)S(1)}, bf16[1536,384]{1,0:T(8,128)(2,1)}, u32[]{:S(2)}) copy-start(bf16[1536,384]{1,0:T(8,128)(2,1)} %refs_14_.3) | copy-start | bytes 3538948
  37.8 1.9 %copy-start.6 = (bf16[384,1152]{1,0:T(8,128)(2,1)S(1)}, bf16[384,1152]{1,0:T(8,128)(2,1)}, u32[]{:S(2)}) copy-start(bf16[384,1152]{1,0:T(8,128)(2,1)} %refs_10_.7) | copy-start | bytes 2654212
  37.9 2.0 %copy-start.7 = (bf16[768,384]{1,0:T(8,128)(2,1)S(1)}, bf16[768,384]{1,0:T(8,128)(2,1)}, u32[]{:S(2)}) copy-start(bf16[768,384]{1,0:T(8,128)(2,1)} %refs_8_.9) | copy-start | bytes 1769476
  37.9 2.0 %copy-start.15 = (f32[768]{0:T(1024)S(1)}, f32[768]{0:T(1024)}, u32[]{:S(2)}) copy-start(f32[768]{0:T(1024)} %refs_7_.7) | copy-start | bytes 9220
  37.9 2.0 %copy-start.16 = (f32[384]{0:T(512)S(1)}, f32[384]{0:T(512)}, u32[]{:S(2)}) copy-start(f32[384]{0:T(512)} %refs_9_.9) | copy-start | bytes 4612
  37.9 2.0 %copy-start.17 = (f32[384]{0:T(512)S(1)}, f32[384]{0:T(512)}, u32[]{:S(2)}) copy-start(f32[384]{0:T(512)} %refs_12_.3) | copy-start | bytes 4612
  37.9 2.0 %copy-start.20 = (f32[192]{0:T(256)S(1)}, f32[192]{0:T(256)}, u32[]{:S(2)}) copy-start(f32[192]{0:T(256)} %refs_16_.3) | copy-start | bytes 2308
  46.8 9.2 %collective-permute-start.10 = (bf16[3,144,128]{2,1,0:T(8,128)(2,1)S(1)}, bf16[3,144,128]{2,1,0:T(8,128)(2,1)S(1)}, u32[]{:S(2)}, u32[]{:S(2)}) collective-permute-start(bf16[3,144,128]{2,1,0:T(8,128)(2,1)S(1)} %get-tuple-element.63), channel_id=1, source_target_pairs={{15,0},{0,1},{1,2},{2,3},{3,4},{4,5},{5,6},{6,7},{7,8},{8,9},{9,10... | collective-permute-start | bytes 331784 | tf_op jit(solution)/shard_map/ppermute | solution.py:433
  46.9 12.3 %collective-permute-start.8 = (bf16[3,144,128]{2,1,0:T(8,128)(2,1)S(1)}, bf16[3,144,128]{2,1,0:T(8,128)(2,1)S(1)}, u32[]{:S(2)}, u32[]{:S(2)}) collective-permute-start(bf16[3,144,128]{2,1,0:T(8,128)(2,1)S(1)} %get-tuple-element.61), channel_id=1, source_target_pairs={{127,0},{112,1},{113,2},{114,3},{115,4},{116,5},{117,6},{118,7},{1... | collective-permute-start | bytes 331784 | tf_op jit(solution)/shard_map/ppermute | solution.py:430
  47.0 12.2 %collective-permute-start.9 = (bf16[3,144,128]{2,1,0:T(8,128)(2,1)S(1)}, bf16[3,144,128]{2,1,0:T(8,128)(2,1)S(1)}, u32[]{:S(2)}, u32[]{:S(2)}) collective-permute-start(bf16[3,144,128]{2,1,0:T(8,128)(2,1)S(1)} %get-tuple-element.62), channel_id=1, source_target_pairs={{112,0},{0,16},{16,32},{32,48},{48,64},{64,80},{80,96},{96,112},{1... | collective-permute-start | bytes 331784 | tf_op jit(solution)/shard_map/ppermute | solution.py:432
  54.3 11.9 %collective-permute-start.5 = (bf16[3,144,128]{2,1,0:T(8,128)(2,1)S(1)}, bf16[3,144,128]{2,1,0:T(8,128)(2,1)S(1)}, u32[]{:S(2)}, u32[]{:S(2)}) collective-permute-start(bf16[3,144,128]{2,1,0:T(8,128)(2,1)S(1)} %get-tuple-element.57), channel_id=1, source_target_pairs={{127,0},{112,1},{113,2},{114,3},{115,4},{116,5},{117,6},{118,7},{1... | collective-permute-start | bytes 331784 | tf_op jit(solution)/shard_map/ppermute | solution.py:430
  55.6 10.6 %collective-permute-start.6 = (bf16[3,144,128]{2,1,0:T(8,128)(2,1)S(1)}, bf16[3,144,128]{2,1,0:T(8,128)(2,1)S(1)}, u32[]{:S(2)}, u32[]{:S(2)}) collective-permute-start(bf16[3,144,128]{2,1,0:T(8,128)(2,1)S(1)} %get-tuple-element.58), channel_id=1, source_target_pairs={{112,0},{0,16},{16,32},{32,48},{48,64},{64,80},{80,96},{96,112},{1... | collective-permute-start | bytes 331784 | tf_op jit(solution)/shard_map/ppermute | solution.py:432
  56.0 11.0 %collective-permute-start.7 = (bf16[3,144,128]{2,1,0:T(8,128)(2,1)S(1)}, bf16[3,144,128]{2,1,0:T(8,128)(2,1)S(1)}, u32[]{:S(2)}, u32[]{:S(2)}) collective-permute-start(bf16[3,144,128]{2,1,0:T(8,128)(2,1)S(1)} %get-tuple-element.59), channel_id=1, source_target_pairs={{15,0},{0,1},{1,2},{2,3},{3,4},{4,5},{5,6},{6,7},{7,8},{8,9},{9,10... | collective-permute-start | bytes 331784 | tf_op jit(solution)/shard_map/ppermute | solution.py:433
  (8 other events, 10.7 us)

commit v5 on v3

--- a/solution.py
+++ b/solution.py
@@ -64,7 +64,7 @@
     return jnp.where(late(key) != late(query), EXCLUDED, 0.0)
 
 
-def attend(q, k, vt, table, heads, step):
+def attend(q, k, vt, table, heads, step, near):
     width = heads * HEAD
     lane = lax.broadcasted_iota(jnp.int32, (1, MAIN), 1) // HEAD
     zero = jnp.zeros((), BF16)
@@ -91,10 +91,12 @@
         e = jnp.exp2(s)
         inv = 1.0 / jnp.sum(e, axis=0, keepdims=True)
         p = e.astype(BF16)
-        for h in range(span // MAIN):
+        for h in range(0, span // MAIN, near):
             row = base // MAIN + h
-            cut = slice(h * MAIN, (h + 1) * MAIN)
-            outs.append(dot(vt[row * HEAD : (row + 1) * HEAD], p[:, cut]) * inv[:, cut])
+            both = dot(vt[row * HEAD : (row + near) * HEAD], p[:, h * MAIN : (h + near) * MAIN])
+            for n in range(near):
+                cut = slice(n * MAIN, (n + 1) * MAIN)
+                outs.append(both[n * HEAD : (n + 1) * HEAD, cut] * inv[:, (h + n) * MAIN : (h + n + 1) * MAIN])
         base += span
     main_out = jnp.concatenate(outs, axis=0)
     s = jnp.concatenate(rests, axis=1) + table[:, base:]
@@ -122,12 +124,16 @@
         rows = slice(w * WIN, (w + 1) * WIN)
         vt = dot(wvt, xn[rows], ((1,), (1,))).astype(BF16)
         table = table_ref.at[1 if w == count - 1 else 0]
-        attended = attend(q[rows], k[rows], vt, table, heads, 4 if heads == 6 else 2)
+        attended = attend(q[rows], k[rows], vt, table, heads, *((4, 2) if heads == 6 else (2, 1)))
         mixed.append(dot(attended, wo[...], ((0,), (0,))))
-    after = (x + jnp.concatenate(mixed, axis=0)).astype(BF16).astype(F32)
-    normed = layer_norm(after, gain_two[...][None, :]).astype(BF16)
-    hidden = gelu(dot(normed, w1[...])).astype(BF16)
-    out_ref[...] = (after + dot(hidden, w2[...], w2_dims)).astype(BF16).astype(F32)
+    half = count // 2
+    for first in range(0, count, half):
+        rows = slice(first * WIN, (first + half) * WIN)
+        after = x_ref[rows, :] + jnp.concatenate(mixed[first : first + half], axis=0)
+        after = after.astype(BF16).astype(F32)
+        normed = layer_norm(after, gain_two[...][None, :]).astype(BF16)
+        hidden = gelu(dot(normed, w1[...])).astype(BF16)
+        out_ref[rows, :] = (after + dot(hidden, w2[...], w2_dims)).astype(BF16).astype(F32)
 
 
 class Packed:
@@ -404,7 +410,7 @@
         out_shape=[jax.ShapeDtypeStruct(s, d) for s, d in outs],
         scratch_shapes=[pltpu.VMEM(s, F32) for s in scratch],
         compiler_params=pltpu.CompilerParams(vmem_limit_bytes=limit * MIB),
-        cost_estimate=pl.CostEstimate(flops=us * 1000 * MIB, bytes_accessed=moved, transcendentals=0),
+        cost_estimate=pl.CostEstimate(flops=us * 1000 * MIB, bytes_accessed=moved if us else 0, transcendentals=0),
         name=name,
     )(*operands)
 
@@ -455,7 +461,7 @@
     square = ((width, width), BF16)
     plain, late, wq, wk, wvt = call(
         fine_table_kernel, "fine_tables", [edge, a_bias, a_project],
-        [((2, WIN, a_heads * WIN), F32)] * 2 + [square] * 3, [], 16, scalars=1, us=3,
+        [((2, WIN, a_heads * WIN), F32)] * 2 + [square] * 3, [], 16, scalars=1, us=0,
     )
     weights = [a_norm_one, wq, wk, wvt, a_output, a_norm_two, a_raise, a_lower.T]
     scratch = [(levels * WIN_LAT, columns, width), (tokens, width), (3,) + staging, (3,) + staging]
@@ -476,13 +482,13 @@
     (w10,) = fine(1, 0, [lat], [])
     lat_two, w10 = lax.optimization_barrier((lat_two, w10))
     (lon_two,) = call(pack_second, "pack_second", [w00, w10, lat_two], [(halo, BF16)], [both, both], 16)
-    diag, lon_two = lax.optimization_barrier((diag, lon_two))
+    lon_two, late_bias = lax.optimization_barrier((lon_two, b_bias))
     lon_two = shift(lon_two, 0, 1)
+    (coarse_table,) = call(
+        table_kernel, "coarse_table", [edge, late_bias], [((2, WIN, b_heads * WIN), F32)], [], 16, scalars=1, us=0
+    )
+    diag, coarse_table = lax.optimization_barrier((diag, coarse_table))
     (w11,) = fine(1, 1, [lat, lon, diag], [])
-    late_bias, w11 = lax.optimization_barrier((b_bias, w11))
-    (coarse_table,) = call(
-        table_kernel, "coarse_table", [edge, late_bias], [((2, WIN, b_heads * WIN), F32)], [], 16, scalars=1
-    )
 
     quads = (4,) + staging
     lines = (levels * rows * PITCH, MAIN)

time: 68 us -> 67.9 us (level)
  starting transfers between devices: 15.6 us -> 17.2 us
  local copies, waits for them, and re-layouts: 3.02 us -> 1.62 us
    unnamed x42, local copies, waits for them, and re-layouts: 3.02 us -> 1.62 us
    ppermute x3, starting transfers between devices: 5.5 us -> 6.66 us  [shift(): lax.ppermute(array, 'lat', [((i + lat_by) % lats, i) for i in range(lats)])]
  transfers between devices with their start and end apart: 8 -> 8, of which waited for: 2 -> 2; matrix products, arithmetic and copies ran while one was open for 0% -> 0% of each run, Pallas kernels for 22% -> 21%
where the time goes in v5:
time: 67.9 us; the launch traced here: 67.7 us
  Pallas kernels  33.2 us (49%)
  starting transfers between devices  17.2 us (25%)
  waiting for transfers between devices  15.2 us (22%)
  local copies, waits for them, and re-layouts  1.62 us (2%)
    pallas_call x10, Pallas kernels, call(): pl.pallas_call(kernel, in_specs=[smem] * scalars + [vmem] * (len(operands...  33.2 us
    ppermute x2, waiting for transfers between devices, shift(): return lax.ppermute(array, ('lat', 'lon'), pairs)  13 us
    ppermute x2, starting transfers between devices, shift(): return lax.ppermute(array, ('lat', 'lon'), pairs)  8.28 us
    ppermute x3, starting transfers between devices, shift(): lax.ppermute(array, 'lat', [((i + lat_by) % lats, i) for i in range(lats)])  6.66 us
    ppermute x3, starting transfers between devices, shift(): lax.ppermute(array, 'lon', [((i + lon_by) % lons, i) for i in range(lons)])  2.31 us
    ppermute x3, waiting for transfers between devices, shift(): lax.ppermute(array, 'lat', [((i + lat_by) % lats, i) for i in range(lats)])  2.2 us
    unnamed x42, local copies, waits for them, and re-layouts  1.62 us
  transfers between devices with their start and end apart: 8, of which 2 were waited for; matrix products, arithmetic and copies ran while one was open for 0% of the time, Pallas kernels for 21%

profile of v5, /device:TPU:0, one launch (start us, length us, event | category | flops | bytes accessed | tf_op | source)
XLA Modules:
  0.0 67.7 jit_solution(17016523358696747390)
XLA Ops:
  0.0 1.4 %copy-done.3 = bf16[8,12,24,192]{3,2,1,0:T(8,128)(2,1)S(1)} copy-done((bf16[8,12,24,192]{3,2,1,0:T(8,128)(2,1)S(1)}, bf16[8,12,24,192]{3,2,1,0:T(8,128)(2,1)}, u32[]{:S(2)}) %copy-start.3) | copy-done | bytes 884760
  1.4 0.9 %start.1 = (bf16[6,112,128]{2,1,0:T(8,128)(2,1)S(1)}, bf16[6,112,128]{2,1,0:T(8,128)(2,1)}, bf16[6,48,128]{2,1,0:T(8,128)(2,1)}) custom-call(bf16[8,12,24,192]{3,2,1,0:T(8,128)(2,1)S(1)} %copy-done.3), custom_call_target="tpu_custom_call" | custom-call | flops 3145728000 | bytes 1302528 | tf_op jit(solution)/shard_map/start/pallas_call | solution.py:406
  2.3 8.2 %collective-permute-start.2 = (bf16[6,48,128]{2,1,0:T(8,128)(2,1)}, bf16[6,48,128]{2,1,0:T(8,128)(2,1)}, u32[]{:S(2)}, u32[]{:S(2)}) collective-permute-start(bf16[6,48,128]{2,1,0:T(8,128)(2,1)} %get-tuple-element.33), channel_id=1, source_target_pairs={{17,0},{18,1},{19,2},{20,3},{21,4},{22,5},{23,6},{24,7},{25,8},{26... | collective-permute-start | bytes 221192 | tf_op jit(solution)/shard_map/ppermute | solution.py:430
  10.5 1.1 %collective-permute-start = (bf16[6,112,128]{2,1,0:T(8,128)(2,1)}, bf16[6,112,128]{2,1,0:T(8,128)(2,1)S(1)}, u32[]{:S(2)}, u32[]{:S(2)}) collective-permute-start(bf16[6,112,128]{2,1,0:T(8,128)(2,1)} %get-tuple-element.31), channel_id=1, source_target_pairs={{1,0},{2,1},{3,2},{4,3},{5,4},{6,5},{7,6},{8,7},{9,8},{10,9},{11,1... | collective-permute-start | bytes 516104 | tf_op jit(solution)/shard_map/ppermute | solution.py:433
  11.7 1.4 %collective-permute-start.1 = (bf16[6,112,128]{2,1,0:T(8,128)(2,1)S(1)}, bf16[6,112,128]{2,1,0:T(8,128)(2,1)S(1)}, u32[]{:S(2)}, u32[]{:S(2)}) collective-permute-start(bf16[6,112,128]{2,1,0:T(8,128)(2,1)S(1)} %get-tuple-element.32), channel_id=1, source_target_pairs={{16,0},{32,16},{48,32},{64,48},{80,64},{96,80},{112,96},{0,112},{1... | collective-permute-start | bytes 516104 | tf_op jit(solution)/shard_map/ppermute | solution.py:432
  13.1 0.6 fine_tables.1
  13.8 3.9 %fine_00.1.refs_2_.w00 = f32[576,192]{1,0:T(8,128)S(1)} custom-call(bf16[8,12,24,192]{3,2,1,0:T(8,128)(2,1)S(1)} %copy-done.4, f32[2,144,864]{2,1,0:T(8,128)S(1)} %get-tuple-element.34.refs_1_.refs_3_, f32[192]{0:T(256)S(1)} %copy-done.18, bf16[192,192]{1,0:T(8,128)(2,1)S(1)} %get-tuple-element.35.refs_3_.refs_5_.refs_4_.refs_6_, ...), custom_call_target="tpu_custom_call" | custom-call | flops 5242880000 | bytes 3208704 | tf_op jit(solution)/shard_map/fine_00/pallas_call | solution.py:406
  17.7 4.1 %fine_01.1 = (f32[576,192]{1,0:T(8,128)S(1)}, bf16[6,144,128]{2,1,0:T(8,128)(2,1)S(1)}) custom-call(bf16[8,12,24,192]{3,2,1,0:T(8,128)(2,1)S(1)} %copy-done.4, bf16[6,112,128]{2,1,0:T(8,128)(2,1)S(1)} %collective-permute-done.refs_1_.refs_2_, f32[576,192]{1,0:T(8,128)S(1)} %fine_00.1.refs_2_.w00, f32[2,144,864]{2,1,0:T(8,128)S(1)} %get-tuple-element.34.refs_1_.refs_3_, ...), custom_call_target="tpu_custom_call" | custom-call | flops 5242880000 | bytes 4044288 | tf_op jit(solution)/shard_map/fine_01/pallas_call | solution.py:406
  21.8 5.1 %collective-permute-start.3 = (bf16[6,144,128]{2,1,0:T(8,128)(2,1)S(1)}, bf16[6,144,128]{2,1,0:T(8,128)(2,1)S(1)}, u32[]{:S(2)}, u32[]{:S(2)}) collective-permute-start(bf16[6,144,128]{2,1,0:T(8,128)(2,1)S(1)} %get-tuple-element.43), channel_id=1, source_target_pairs={{16,0},{32,16},{48,32},{64,48},{80,64},{96,80},{112,96},{0,112},{1... | collective-permute-start | bytes 663560 | tf_op jit(solution)/shard_map/ppermute | solution.py:432
  26.9 3.9 %fine_10.1.w10 = f32[576,192]{1,0:T(8,128)S(1)} custom-call(bf16[8,12,24,192]{3,2,1,0:T(8,128)(2,1)S(1)} %copy-done.4, bf16[6,112,128]{2,1,0:T(8,128)(2,1)S(1)} %collective-permute-done.1.refs_1_, f32[2,144,864]{2,1,0:T(8,128)S(1)} %get-tuple-element.45.refs_2_.refs_4_, f32[192]{0:T(256)S(1)} %copy-done.18, ...), custom_call_target="tpu_custom_call" | custom-call | flops 5242880000 | bytes 3380736 | tf_op jit(solution)/shard_map/fine_10/pallas_call | solution.py:406
  30.9 0.2 pack_second.1
  31.1 1.1 %collective-permute-start.4 = (bf16[6,144,128]{2,1,0:T(8,128)(2,1)S(1)}, bf16[6,144,128]{2,1,0:T(8,128)(2,1)S(1)}, u32[]{:S(2)}, u32[]{:S(2)}) collective-permute-start(bf16[6,144,128]{2,1,0:T(8,128)(2,1)S(1)} %pack_second.1), channel_id=1, source_target_pairs={{1,0},{2,1},{3,2},{4,3},{5,4},{6,5},{7,6},{8,7},{9,8},{10,9},{11,1... | collective-permute-start | bytes 663560 | tf_op jit(solution)/shard_map/ppermute | solution.py:433
  32.2 0.2 copy-done
  32.4 1.0 %coarse_table.1.table_ref = f32[2,144,1728]{2,1,0:T(8,128)S(1)} custom-call(s32[1]{0:T(128)} %bitcast.edge_ref, f32[12,144,144]{2,1,0:T(8,128)S(1)} %copy-done), custom_call_target="tpu_custom_call" | custom-call | tf_op jit(solution)/shard_map/coarse_table/pallas_call | solution.py:406
  33.3 0.0 copy-start.5
  33.4 0.0 copy-start.6
  33.5 5.1 %fine_11.1.w11 = f32[576,192]{1,0:T(8,128)S(1)} custom-call(bf16[8,12,24,192]{3,2,1,0:T(8,128)(2,1)S(1)} %copy-done.4, bf16[6,112,128]{2,1,0:T(8,128)(2,1)S(1)} %collective-permute-done.1.refs_1_, bf16[6,112,128]{2,1,0:T(8,128)(2,1)S(1)} %collective-permute-done.refs_1_.refs_2_, bf16[6,48,128]{2,1,0:T(8,128)(2,1)} %collective-permute-done.2.refs_3_, ...), custom_call_target="tpu_custom_call" | custom-call | flops 5242880000 | bytes 3626496 | tf_op jit(solution)/shard_map/fine_11/pallas_call | solution.py:406
  38.7 12.0 %coarse.1 = (bf16[6,144,128]{2,1,0:T(8,128)(2,1)S(1)}, bf16[6,144,128]{2,1,0:T(8,128)(2,1)S(1)}, bf16[6,144,128]{2,1,0:T(8,128)(2,1)S(1)}, bf16[6,144,128]{2,1,0:T(8,128)(2,1)S(1)}) custom-call(f32[576,192]{1,0:T(8,128)S(1)} %fine_00.1.refs_2_.w00, f32[576,192]{1,0:T(8,128)S(1)} %get-tuple-element.42.w01, f32[576,192]{1,0:T(8,128)S(1)} %fine_10.1.w10, ...), custom_call_target="tpu_custom_call" | custom-call | flops 12582912000 | bytes 9886464 | tf_op jit(solution)/shard_map/coarse/pallas_call | solution.py:406
  50.6 0.1 collective-permute-start.5
  50.7 0.1 collective-permute-start.6
  50.8 0.1 collective-permute-start.7
  50.9 13.0 %collective-permute-done.5.upper_left = bf16[6,144,128]{2,1,0:T(8,128)(2,1)S(1)} collective-permute-done((bf16[6,144,128]{2,1,0:T(8,128)(2,1)S(1)}, bf16[6,144,128]{2,1,0:T(8,128)(2,1)S(1)}, u32[]{:S(2)}, u32[]{:S(2)}) %collective-permute-start.5) | collective-permute-done | bytes 221216 | tf_op jit(solution)/shard_map/ppermute | solution.py:430
  63.9 2.2 %collective-permute-done.6.upper_right = bf16[6,144,128]{2,1,0:T(8,128)(2,1)S(1)} collective-permute-done((bf16[6,144,128]{2,1,0:T(8,128)(2,1)S(1)}, bf16[6,144,128]{2,1,0:T(8,128)(2,1)S(1)}, u32[]{:S(2)}, u32[]{:S(2)}) %collective-permute-start.6) | collective-permute-done | bytes 221216 | tf_op jit(solution)/shard_map/ppermute | solution.py:432
  66.1 1.6 %finish.1 = bf16[8,12,24,192]{3,2,1,0:T(8,128)(2,1)} custom-call(bf16[6,144,128]{2,1,0:T(8,128)(2,1)S(1)} %collective-permute-done.5.upper_left, bf16[6,144,128]{2,1,0:T(8,128)(2,1)S(1)} %collective-permute-done.6.upper_right, bf16[6,144,128]{2,1,0:T(8,128)(2,1)S(1)} %collective-permute-done.7.lower_left, bf16[6,144,128]{2,1,0:T(8,128)(2,1)S(1)} %get-tuple-element.56.lower_right), custom_call_target="tpu_custom_call" | custom-call | flops 1048576000 | bytes 1769472 | tf_op jit(solution)/shard_map/finish/pallas_call | solution.py:406
  (44 shorter events, 0.1 us)
Async XLA Ops:
  0.0 13.1 %copy-start.1 = (f32[6,144,144]{2,1,0:T(8,128)S(1)}, f32[6,144,144]{2,1,0:T(8,128)}, u32[]{:S(2)}) copy-start(f32[6,144,144]{2,1,0:T(8,128)} %bias.1) | copy-start | bytes 1492996
  0.0 13.1 %copy-start.2 = (bf16[192,576]{1,0:T(8,128)(2,1)S(1)}, bf16[192,576]{1,0:T(8,128)(2,1)}, u32[]{:S(2)}) copy-start(bf16[192,576]{1,0:T(8,128)(2,1)} %project.2) | copy-start | bytes 663556
  1.4 12.4 %copy-start.4 = (bf16[8,12,24,192]{3,2,1,0:T(8,128)(2,1)S(1)}, bf16[8,12,24,192]{3,2,1,0:T(8,128)(2,1)}, u32[]{:S(2)}) copy-start(bf16[8,12,24,192]{3,2,1,0:T(8,128)(2,1)} %refs_0_.7) | copy-start | bytes 2654212
  1.4 12.4 %copy-start.10 = (bf16[192,768]{1,0:T(8,128)(2,1)S(1)}, bf16[192,768]{1,0:T(8,128)(2,1)}, u32[]{:S(2)}) copy-start(bf16[192,768]{1,0:T(8,128)(2,1)} %refs_11_.1) | copy-start | bytes 884740
  1.4 12.4 %copy-start.11 = (bf16[768,192]{0,1:T(8,128)(2,1)S(1)}, bf16[768,192]{0,1:T(8,128)(2,1)}, u32[]{:S(2)}) copy-start(bf16[768,192]{0,1:T(8,128)(2,1)} %param.27) | copy-start | bytes 884740
  1.4 12.4 %copy-start.13 = (bf16[192,192]{1,0:T(8,128)(2,1)S(1)}, bf16[192,192]{1,0:T(8,128)(2,1)}, u32[]{:S(2)}) copy-start(bf16[192,192]{1,0:T(8,128)(2,1)} %refs_9_.5) | copy-start | bytes 221188
  1.4 12.4 %copy-start.18 = (f32[192]{0:T(256)S(1)}, f32[192]{0:T(256)}, u32[]{:S(2)}) copy-start(f32[192]{0:T(256)} %refs_5_.1) | copy-start | bytes 2308
  1.4 12.4 %copy-start.19 = (f32[192]{0:T(256)S(1)}, f32[192]{0:T(256)}, u32[]{:S(2)}) copy-start(f32[192]{0:T(256)} %refs_10_.3) | copy-start | bytes 2308
  2.3 15.4 %collective-permute-start.2 = (bf16[6,48,128]{2,1,0:T(8,128)(2,1)}, bf16[6,48,128]{2,1,0:T(8,128)(2,1)}, u32[]{:S(2)}, u32[]{:S(2)}) collective-permute-start(bf16[6,48,128]{2,1,0:T(8,128)(2,1)} %get-tuple-element.33), channel_id=1, source_target_pairs={{17,0},{18,1},{19,2},{20,3},{21,4},{22,5},{23,6},{24,7},{25,8},{26... | collective-permute-start | bytes 221192 | tf_op jit(solution)/shard_map/ppermute | solution.py:430
  10.5 7.2 %collective-permute-start = (bf16[6,112,128]{2,1,0:T(8,128)(2,1)}, bf16[6,112,128]{2,1,0:T(8,128)(2,1)S(1)}, u32[]{:S(2)}, u32[]{:S(2)}) collective-permute-start(bf16[6,112,128]{2,1,0:T(8,128)(2,1)} %get-tuple-element.31), channel_id=1, source_target_pairs={{1,0},{2,1},{3,2},{4,3},{5,4},{6,5},{7,6},{8,7},{9,8},{10,9},{11,1... | collective-permute-start | bytes 516104 | tf_op jit(solution)/shard_map/ppermute | solution.py:433
  11.7 6.1 %collective-permute-start.1 = (bf16[6,112,128]{2,1,0:T(8,128)(2,1)S(1)}, bf16[6,112,128]{2,1,0:T(8,128)(2,1)S(1)}, u32[]{:S(2)}, u32[]{:S(2)}) collective-permute-start(bf16[6,112,128]{2,1,0:T(8,128)(2,1)S(1)} %get-tuple-element.32), channel_id=1, source_target_pairs={{16,0},{32,16},{48,32},{64,48},{80,64},{96,80},{112,96},{0,112},{1... | collective-permute-start | bytes 516104 | tf_op jit(solution)/shard_map/ppermute | solution.py:432
  21.8 9.1 %collective-permute-start.3 = (bf16[6,144,128]{2,1,0:T(8,128)(2,1)S(1)}, bf16[6,144,128]{2,1,0:T(8,128)(2,1)S(1)}, u32[]{:S(2)}, u32[]{:S(2)}) collective-permute-start(bf16[6,144,128]{2,1,0:T(8,128)(2,1)S(1)} %get-tuple-element.43), channel_id=1, source_target_pairs={{16,0},{32,16},{48,32},{64,48},{80,64},{96,80},{112,96},{0,112},{1... | collective-permute-start | bytes 663560 | tf_op jit(solution)/shard_map/ppermute | solution.py:432
  31.1 7.4 %collective-permute-start.4 = (bf16[6,144,128]{2,1,0:T(8,128)(2,1)S(1)}, bf16[6,144,128]{2,1,0:T(8,128)(2,1)S(1)}, u32[]{:S(2)}, u32[]{:S(2)}) collective-permute-start(bf16[6,144,128]{2,1,0:T(8,128)(2,1)S(1)} %pack_second.1), channel_id=1, source_target_pairs={{1,0},{2,1},{3,2},{4,3},{5,4},{6,5},{7,6},{8,7},{9,8},{10,9},{11,1... | collective-permute-start | bytes 663560 | tf_op jit(solution)/shard_map/ppermute | solution.py:433
  33.3 5.2 %copy-start.5 = (bf16[384,1536]{1,0:T(8,128)(2,1)S(1)}, bf16[384,1536]{1,0:T(8,128)(2,1)}, u32[]{:S(2)}) copy-start(bf16[384,1536]{1,0:T(8,128)(2,1)} %w1.1) | copy-start | bytes 3538948
  33.4 5.2 %copy-start.6 = (bf16[1536,384]{1,0:T(8,128)(2,1)S(1)}, bf16[1536,384]{1,0:T(8,128)(2,1)}, u32[]{:S(2)}) copy-start(bf16[1536,384]{1,0:T(8,128)(2,1)} %w2.1) | copy-start | bytes 3538948
  33.4 5.2 %copy-start.7 = (bf16[384,1152]{1,0:T(8,128)(2,1)S(1)}, bf16[384,1152]{1,0:T(8,128)(2,1)}, u32[]{:S(2)}) copy-start(bf16[384,1152]{1,0:T(8,128)(2,1)} %project.3) | copy-start | bytes 2654212
  33.4 5.2 %copy-start.8 = (bf16[768,384]{1,0:T(8,128)(2,1)S(1)}, bf16[768,384]{1,0:T(8,128)(2,1)}, u32[]{:S(2)}) copy-start(bf16[768,384]{1,0:T(8,128)(2,1)} %merge_weight.1) | copy-start | bytes 1769476
  33.4 5.2 %copy-start.9 = (bf16[384,768]{1,0:T(8,128)(2,1)S(1)}, bf16[384,768]{1,0:T(8,128)(2,1)}, u32[]{:S(2)}) copy-start(bf16[384,768]{1,0:T(8,128)(2,1)} %up_first.1) | copy-start | bytes 1769476
  33.4 5.2 %copy-start.12 = (bf16[384,384]{1,0:T(8,128)(2,1)S(1)}, bf16[384,384]{1,0:T(8,128)(2,1)}, u32[]{:S(2)}) copy-start(bf16[384,384]{1,0:T(8,128)(2,1)} %wo.1) | copy-start | bytes 884740
  33.4 5.2 %copy-start.14 = (bf16[192,192]{1,0:T(8,128)(2,1)S(1)}, bf16[192,192]{1,0:T(8,128)(2,1)}, u32[]{:S(2)}) copy-start(bf16[192,192]{1,0:T(8,128)(2,1)} %up_second.1) | copy-start | bytes 221188
  33.4 5.2 %copy-start.15 = (f32[768]{0:T(1024)S(1)}, f32[768]{0:T(1024)}, u32[]{:S(2)}) copy-start(f32[768]{0:T(1024)} %merge_gain.1) | copy-start | bytes 9220
  50.6 13.3 %collective-permute-start.5 = (bf16[6,144,128]{2,1,0:T(8,128)(2,1)S(1)}, bf16[6,144,128]{2,1,0:T(8,128)(2,1)S(1)}, u32[]{:S(2)}, u32[]{:S(2)}) collective-permute-start(bf16[6,144,128]{2,1,0:T(8,128)(2,1)S(1)} %get-tuple-element.53), channel_id=1, source_target_pairs={{127,0},{112,1},{113,2},{114,3},{115,4},{116,5},{117,6},{118,7},{1... | collective-permute-start | bytes 663560 | tf_op jit(solution)/shard_map/ppermute | solution.py:430
  50.7 15.4 %collective-permute-start.6 = (bf16[6,144,128]{2,1,0:T(8,128)(2,1)S(1)}, bf16[6,144,128]{2,1,0:T(8,128)(2,1)S(1)}, u32[]{:S(2)}, u32[]{:S(2)}) collective-permute-start(bf16[6,144,128]{2,1,0:T(8,128)(2,1)S(1)} %get-tuple-element.54), channel_id=1, source_target_pairs={{112,0},{0,16},{16,32},{32,48},{48,64},{64,80},{80,96},{96,112},{1... | collective-permute-start | bytes 663560 | tf_op jit(solution)/shard_map/ppermute | solution.py:432
  50.8 15.3 %collective-permute-start.7 = (bf16[6,144,128]{2,1,0:T(8,128)(2,1)S(1)}, bf16[6,144,128]{2,1,0:T(8,128)(2,1)S(1)}, u32[]{:S(2)}, u32[]{:S(2)}) collective-permute-start(bf16[6,144,128]{2,1,0:T(8,128)(2,1)S(1)} %get-tuple-element.55), channel_id=1, source_target_pairs={{15,0},{0,1},{1,2},{2,3},{3,4},{4,5},{5,6},{6,7},{7,8},{8,9},{9,10... | collective-permute-start | bytes 663560 | tf_op jit(solution)/shard_map/ppermute | solution.py:433
  (5 other events, 18.4 us)

commit v6 on v5

--- a/solution.py
+++ b/solution.py
@@ -377,38 +377,47 @@
         Packed(quad_low.at[quad], quad_high.at[quad], WIN).store(ref)
 
 
-def finish_kernel(upper_left, upper_right, lower_left, lower_right, out_ref, low_ref, high_ref, line_low, line_high):
+def finish_kernel(
+    upper_left, upper_right, lower_left, lower_right, out_hbm, low_ref, high_ref, line_low, line_high, out_ref, sems
+):
     levels, rows, columns, width = out_ref.shape
     half = rows // 2
-    for quad, ref in enumerate((upper_left, upper_right, lower_left, lower_right)):
-        pack = Packed(low_ref.at[quad], high_ref.at[quad], WIN).load(ref)
-        for p in range(levels // WIN_P):
-            for lev, level in enumerate(pair_levels(p, levels)):
+    packs = [
+        Packed(low_ref.at[quad], high_ref.at[quad], WIN).load(ref)
+        for quad, ref in enumerate((upper_left, upper_right, lower_left, lower_right))
+    ]
+    copies = []
+    for p in range(levels // WIN_P):
+        for lev, level in enumerate(pair_levels(p, levels)):
+            for quad, pack in enumerate(packs):
                 for row in range(half):
                     at = (level * rows + (quad // 2) * half + row) * columns + quad % 2 * WIN_LON
                     here = (lev * half + row) * WIN_LON
                     line_low[at : at + WIN_LON, :] = pack.low[p, here : here + WIN_LON, :]
                     line_high[at : at + WIN_LON, :] = pack.high[p, here : here + WIN_LON, :]
-    for level in range(levels):
-        for row in range(rows):
-            at = (level * rows + row) * columns
-            out_ref[level, row, :, :MAIN] = line_low[at : at + columns, :].astype(BF16)
-            out_ref[level, row, :, MAIN:] = line_high[at : at + columns, : width - MAIN].astype(BF16)
+            for row in range(rows):
+                at = (level * rows + row) * columns
+                out_ref[level, row, :, :MAIN] = line_low[at : at + columns, :].astype(BF16)
+                out_ref[level, row, :, MAIN:] = line_high[at : at + columns, : width - MAIN].astype(BF16)
+            copies.append(pltpu.make_async_copy(out_ref.at[level], out_hbm.at[level], sems.at[level]))
+            copies[-1].start()
+    for copy in copies:
+        copy.wait()
 
 
 MIB = 1024 * 1024
 
 
-def call(kernel, name, operands, outs, scratch, limit, scalars=0, us=1):
+def call(kernel, name, operands, outs, scratch, limit, scalars=0, us=1, results=pltpu.VMEM):
     vmem = pl.BlockSpec(memory_space=pltpu.VMEM)
     smem = pl.BlockSpec(memory_space=pltpu.SMEM)
     moved = sum(x.size * x.dtype.itemsize for x in operands) + sum(math.prod(s) * jnp.dtype(d).itemsize for s, d in outs)
     return pl.pallas_call(
         kernel,
         in_specs=[smem] * scalars + [vmem] * (len(operands) - scalars),
-        out_specs=[vmem] * len(outs),
+        out_specs=[pl.BlockSpec(memory_space=results)] * len(outs),
         out_shape=[jax.ShapeDtypeStruct(s, d) for s, d in outs],
-        scratch_shapes=[pltpu.VMEM(s, F32) for s in scratch],
+        scratch_shapes=[pltpu.VMEM(s, F32) if isinstance(s, tuple) else s for s in scratch],
         compiler_params=pltpu.CompilerParams(vmem_limit_bytes=limit * MIB),
         cost_estimate=pl.CostEstimate(flops=us * 1000 * MIB, bytes_accessed=moved if us else 0, transcendentals=0),
         name=name,
@@ -461,7 +470,7 @@
     square = ((width, width), BF16)
     plain, late, wq, wk, wvt = call(
         fine_table_kernel, "fine_tables", [edge, a_bias, a_project],
-        [((2, WIN, a_heads * WIN), F32)] * 2 + [square] * 3, [], 16, scalars=1, us=0,
+        [((2, WIN, a_heads * WIN), F32)] * 2 + [square] * 3, [], 16, scalars=1, us=3,
     )
     weights = [a_norm_one, wq, wk, wvt, a_output, a_norm_two, a_raise, a_lower.T]
     scratch = [(levels * WIN_LAT, columns, width), (tokens, width), (3,) + staging, (3,) + staging]
@@ -507,7 +516,9 @@
     lon = shift(lon, 0, -1)
     lines = (levels * rows * columns, MAIN)
     (fine_out,) = call(
-        finish_kernel, "finish", [diag, lat, lon, stay], [(field.shape, BF16)], [quads, quads, lines, lines], 24
+        finish_kernel, "finish", [diag, lat, lon, stay], [(field.shape, BF16)],
+        [quads, quads, lines, lines, pltpu.VMEM(field.shape, BF16), pltpu.SemaphoreType.DMA((levels,))],
+        24, results=pl.ANY,
     )
     return fine_out
 

time: 67.9 us -> 66.1 us (0.973)
  Pallas kernels: 33.2 us -> 31.3 us
  starting transfers between devices: 17.2 us -> 16.4 us
  local copies, waits for them, and re-layouts: 1.62 us -> 2.42 us
    pallas_call x10, Pallas kernels: 33.2 us -> 31.3 us  [call(): pl.pallas_call(kernel, in_specs=[smem] * scalars + [vmem] * (len(operands...]
    unnamed x42, local copies, waits for them, and re-layouts: 1.62 us -> 2.42 us
    ppermute x3, starting transfers between devices: 6.66 us -> 5.91 us  [shift(): lax.ppermute(array, 'lat', [((i + lat_by) % lats, i) for i in range(lats)])]
where the time goes in v6:
time: 66.1 us; the launch traced here: 65.9 us
  Pallas kernels  31.3 us (47%)
  starting transfers between devices  16.4 us (25%)
  waiting for transfers between devices  15.2 us (23%)
  local copies, waits for them, and re-layouts  2.42 us (4%)
    pallas_call x10, Pallas kernels, call(): pl.pallas_call(kernel, in_specs=[smem] * scalars + [vmem] * (len(operands...  31.3 us
    ppermute x2, waiting for transfers between devices, shift(): return lax.ppermute(array, ('lat', 'lon'), pairs)  13.1 us
    ppermute x2, starting transfers between devices, shift(): return lax.ppermute(array, ('lat', 'lon'), pairs)  8.35 us
    ppermute x3, starting transfers between devices, shift(): lax.ppermute(array, 'lat', [((i + lat_by) % lats, i) for i in range(lats)])  5.91 us
    unnamed x42, local copies, waits for them, and re-layouts  2.42 us
    ppermute x3, starting transfers between devices, shift(): lax.ppermute(array, 'lon', [((i + lon_by) % lons, i) for i in range(lons)])  2.13 us
    ppermute x3, waiting for transfers between devices, shift(): lax.ppermute(array, 'lat', [((i + lat_by) % lats, i) for i in range(lats)])  2.09 us
  transfers between devices with their start and end apart: 8, of which 2 were waited for; matrix products, arithmetic and copies ran while one was open for 0% of the time, Pallas kernels for 21%

profile of v6, /device:TPU:0, one launch (start us, length us, event | category | flops | bytes accessed | tf_op | source)
XLA Modules:
  0.0 65.9 jit_solution(9630597778055547817)
XLA Ops:
  0.0 1.3 %copy-done.1 = bf16[8,12,24,192]{3,2,1,0:T(8,128)(2,1)S(1)} copy-done((bf16[8,12,24,192]{3,2,1,0:T(8,128)(2,1)S(1)}, bf16[8,12,24,192]{3,2,1,0:T(8,128)(2,1)}, u32[]{:S(2)}) %copy-start.1) | copy-done | bytes 884760
  1.3 0.2 start.1
  1.5 8.3 %collective-permute-start.2 = (bf16[6,48,128]{2,1,0:T(8,128)(2,1)S(1)}, bf16[6,48,128]{2,1,0:T(8,128)(2,1)S(1)}, u32[]{:S(2)}, u32[]{:S(2)}) collective-permute-start(bf16[6,48,128]{2,1,0:T(8,128)(2,1)S(1)} %get-tuple-element.33), channel_id=1, source_target_pairs={{17,0},{18,1},{19,2},{20,3},{21,4},{22,5},{23,6},{24,7},{25,8},{26... | collective-permute-start | bytes 221192 | tf_op jit(solution)/shard_map/ppermute | solution.py:439
  9.8 1.1 %collective-permute-start = (bf16[6,112,128]{2,1,0:T(8,128)(2,1)S(1)}, bf16[6,112,128]{2,1,0:T(8,128)(2,1)S(1)}, u32[]{:S(2)}, u32[]{:S(2)}) collective-permute-start(bf16[6,112,128]{2,1,0:T(8,128)(2,1)S(1)} %get-tuple-element.31), channel_id=1, source_target_pairs={{1,0},{2,1},{3,2},{4,3},{5,4},{6,5},{7,6},{8,7},{9,8},{10,9},{11,1... | collective-permute-start | bytes 516104 | tf_op jit(solution)/shard_map/ppermute | solution.py:442
  10.9 1.4 %collective-permute-start.1 = (bf16[6,112,128]{2,1,0:T(8,128)(2,1)S(1)}, bf16[6,112,128]{2,1,0:T(8,128)(2,1)S(1)}, u32[]{:S(2)}, u32[]{:S(2)}) collective-permute-start(bf16[6,112,128]{2,1,0:T(8,128)(2,1)S(1)} %get-tuple-element.32), channel_id=1, source_target_pairs={{16,0},{32,16},{48,32},{64,48},{80,64},{96,80},{112,96},{0,112},{1... | collective-permute-start | bytes 516104 | tf_op jit(solution)/shard_map/ppermute | solution.py:441
  12.4 0.6 fine_tables.1
  13.0 0.6 copy-done.2
  13.7 0.1 copy-done.10
  13.8 3.9 %fine_00.1.refs_2_.w00 = f32[576,192]{1,0:T(8,128)S(1)} custom-call(bf16[8,12,24,192]{3,2,1,0:T(8,128)(2,1)S(1)} %copy-done.2, f32[2,144,864]{2,1,0:T(8,128)S(1)} %get-tuple-element.34.refs_1_.refs_3_, f32[192]{0:T(256)S(1)} %copy-done.18, bf16[192,192]{1,0:T(8,128)(2,1)S(1)} %get-tuple-element.35.refs_3_.refs_5_.refs_4_.refs_6_, ...), custom_call_target="tpu_custom_call" | custom-call | flops 5242880000 | bytes 3208704 | tf_op jit(solution)/shard_map/fine_00/pallas_call | solution.py:415
  17.7 4.1 %fine_01.1 = (f32[576,192]{1,0:T(8,128)S(1)}, bf16[6,144,128]{2,1,0:T(8,128)(2,1)S(1)}) custom-call(bf16[8,12,24,192]{3,2,1,0:T(8,128)(2,1)S(1)} %copy-done.2, bf16[6,112,128]{2,1,0:T(8,128)(2,1)S(1)} %collective-permute-done.refs_1_.refs_2_, f32[576,192]{1,0:T(8,128)S(1)} %fine_00.1.refs_2_.w00, f32[2,144,864]{2,1,0:T(8,128)S(1)} %get-tuple-element.34.refs_1_.refs_3_, ...), custom_call_target="tpu_custom_call" | custom-call | flops 5242880000 | bytes 4044288 | tf_op jit(solution)/shard_map/fine_01/pallas_call | solution.py:415
  21.8 4.4 %collective-permute-start.3 = (bf16[6,144,128]{2,1,0:T(8,128)(2,1)S(1)}, bf16[6,144,128]{2,1,0:T(8,128)(2,1)S(1)}, u32[]{:S(2)}, u32[]{:S(2)}) collective-permute-start(bf16[6,144,128]{2,1,0:T(8,128)(2,1)S(1)} %get-tuple-element.43), channel_id=1, source_target_pairs={{16,0},{32,16},{48,32},{64,48},{80,64},{96,80},{112,96},{0,112},{1... | collective-permute-start | bytes 663560 | tf_op jit(solution)/shard_map/ppermute | solution.py:441
  26.2 4.0 %fine_10.1.w10 = f32[576,192]{1,0:T(8,128)S(1)} custom-call(bf16[8,12,24,192]{3,2,1,0:T(8,128)(2,1)S(1)} %copy-done.2, bf16[6,112,128]{2,1,0:T(8,128)(2,1)S(1)} %collective-permute-done.1.refs_1_, f32[2,144,864]{2,1,0:T(8,128)S(1)} %get-tuple-element.45.refs_2_.refs_4_, f32[192]{0:T(256)S(1)} %copy-done.18, ...), custom_call_target="tpu_custom_call" | custom-call | flops 5242880000 | bytes 3380736 | tf_op jit(solution)/shard_map/fine_10/pallas_call | solution.py:415
  30.2 0.2 pack_second.1
  30.4 0.9 %collective-permute-start.4 = (bf16[6,144,128]{2,1,0:T(8,128)(2,1)S(1)}, bf16[6,144,128]{2,1,0:T(8,128)(2,1)S(1)}, u32[]{:S(2)}, u32[]{:S(2)}) collective-permute-start(bf16[6,144,128]{2,1,0:T(8,128)(2,1)S(1)} %pack_second.1), channel_id=1, source_target_pairs={{1,0},{2,1},{3,2},{4,3},{5,4},{6,5},{7,6},{8,7},{9,8},{10,9},{11,1... | collective-permute-start | bytes 663560 | tf_op jit(solution)/shard_map/ppermute | solution.py:442
  31.4 0.3 copy-done
  31.7 1.0 %coarse_table.1.table_ref = f32[2,144,1728]{2,1,0:T(8,128)S(1)} custom-call(s32[1]{0:T(128)} %bitcast.edge_ref, f32[12,144,144]{2,1,0:T(8,128)S(1)} %copy-done), custom_call_target="tpu_custom_call" | custom-call | tf_op jit(solution)/shard_map/coarse_table/pallas_call | solution.py:415
  32.8 4.0 %fine_11.1.w11 = f32[576,192]{1,0:T(8,128)S(1)} custom-call(bf16[8,12,24,192]{3,2,1,0:T(8,128)(2,1)S(1)} %copy-done.2, bf16[6,112,128]{2,1,0:T(8,128)(2,1)S(1)} %collective-permute-done.1.refs_1_, bf16[6,112,128]{2,1,0:T(8,128)(2,1)S(1)} %collective-permute-done.refs_1_.refs_2_, bf16[6,48,128]{2,1,0:T(8,128)(2,1)S(1)} %collective-permute-done.2.refs_3_, ...), custom_call_target="tpu_custom_call" | custom-call | flops 5242880000 | bytes 3626496 | tf_op jit(solution)/shard_map/fine_11/pallas_call | solution.py:415
  36.9 12.0 %coarse.1 = (bf16[6,144,128]{2,1,0:T(8,128)(2,1)S(1)}, bf16[6,144,128]{2,1,0:T(8,128)(2,1)S(1)}, bf16[6,144,128]{2,1,0:T(8,128)(2,1)S(1)}, bf16[6,144,128]{2,1,0:T(8,128)(2,1)S(1)}) custom-call(f32[576,192]{1,0:T(8,128)S(1)} %fine_00.1.refs_2_.w00, f32[576,192]{1,0:T(8,128)S(1)} %get-tuple-element.42.w01, f32[576,192]{1,0:T(8,128)S(1)} %fine_10.1.w10, ...), custom_call_target="tpu_custom_call" | custom-call | flops 12582912000 | bytes 9886464 | tf_op jit(solution)/shard_map/coarse/pallas_call | solution.py:415
  48.9 0.1 collective-permute-start.5
  49.0 0.1 collective-permute-start.6
  49.1 0.1 collective-permute-start.7
  49.2 13.1 %collective-permute-done.5.upper_left = bf16[6,144,128]{2,1,0:T(8,128)(2,1)S(1)} collective-permute-done((bf16[6,144,128]{2,1,0:T(8,128)(2,1)S(1)}, bf16[6,144,128]{2,1,0:T(8,128)(2,1)S(1)}, u32[]{:S(2)}, u32[]{:S(2)}) %collective-permute-start.5) | collective-permute-done | bytes 221216 | tf_op jit(solution)/shard_map/ppermute | solution.py:439
  62.3 2.1 %collective-permute-done.6.upper_right = bf16[6,144,128]{2,1,0:T(8,128)(2,1)S(1)} collective-permute-done((bf16[6,144,128]{2,1,0:T(8,128)(2,1)S(1)}, bf16[6,144,128]{2,1,0:T(8,128)(2,1)S(1)}, u32[]{:S(2)}, u32[]{:S(2)}) %collective-permute-start.6) | collective-permute-done | bytes 221216 | tf_op jit(solution)/shard_map/ppermute | solution.py:441
  64.4 1.3 %finish.1 = bf16[8,12,24,192]{3,2,1,0:T(8,128)(2,1)} custom-call(bf16[6,144,128]{2,1,0:T(8,128)(2,1)S(1)} %collective-permute-done.5.upper_left, bf16[6,144,128]{2,1,0:T(8,128)(2,1)S(1)} %collective-permute-done.6.upper_right, bf16[6,144,128]{2,1,0:T(8,128)(2,1)S(1)} %collective-permute-done.7.lower_left, bf16[6,144,128]{2,1,0:T(8,128)(2,1)S(1)} %get-tuple-element.56.lower_right), custom_call_target="tpu_custom_call" | custom-call | flops 1048576000 | bytes 1769472 | tf_op jit(solution)/shard_map/finish/pallas_call | solution.py:415
  (44 shorter events, 0.2 us)
Async XLA Ops:
  1.3 11.1 %copy-start.5 = (f32[6,144,144]{2,1,0:T(8,128)S(1)}, f32[6,144,144]{2,1,0:T(8,128)}, u32[]{:S(2)}) copy-start(f32[6,144,144]{2,1,0:T(8,128)} %bias.1) | copy-start | bytes 1492996
  1.3 11.1 %copy-start.12 = (bf16[192,576]{1,0:T(8,128)(2,1)S(1)}, bf16[192,576]{1,0:T(8,128)(2,1)}, u32[]{:S(2)}) copy-start(bf16[192,576]{1,0:T(8,128)(2,1)} %project.2) | copy-start | bytes 663556
  1.5 16.2 %collective-permute-start.2 = (bf16[6,48,128]{2,1,0:T(8,128)(2,1)S(1)}, bf16[6,48,128]{2,1,0:T(8,128)(2,1)S(1)}, u32[]{:S(2)}, u32[]{:S(2)}) collective-permute-start(bf16[6,48,128]{2,1,0:T(8,128)(2,1)S(1)} %get-tuple-element.33), channel_id=1, source_target_pairs={{17,0},{18,1},{19,2},{20,3},{21,4},{22,5},{23,6},{24,7},{25,8},{26... | collective-permute-start | bytes 221192 | tf_op jit(solution)/shard_map/ppermute | solution.py:439
  9.8 8.0 %collective-permute-start = (bf16[6,112,128]{2,1,0:T(8,128)(2,1)S(1)}, bf16[6,112,128]{2,1,0:T(8,128)(2,1)S(1)}, u32[]{:S(2)}, u32[]{:S(2)}) collective-permute-start(bf16[6,112,128]{2,1,0:T(8,128)(2,1)S(1)} %get-tuple-element.31), channel_id=1, source_target_pairs={{1,0},{2,1},{3,2},{4,3},{5,4},{6,5},{7,6},{8,7},{9,8},{10,9},{11,1... | collective-permute-start | bytes 516104 | tf_op jit(solution)/shard_map/ppermute | solution.py:442
  10.9 6.8 %collective-permute-start.1 = (bf16[6,112,128]{2,1,0:T(8,128)(2,1)S(1)}, bf16[6,112,128]{2,1,0:T(8,128)(2,1)S(1)}, u32[]{:S(2)}, u32[]{:S(2)}) collective-permute-start(bf16[6,112,128]{2,1,0:T(8,128)(2,1)S(1)} %get-tuple-element.32), channel_id=1, source_target_pairs={{16,0},{32,16},{48,32},{64,48},{80,64},{96,80},{112,96},{0,112},{1... | collective-permute-start | bytes 516104 | tf_op jit(solution)/shard_map/ppermute | solution.py:441
  12.4 1.4 %copy-start.10 = (bf16[768,192]{0,1:T(8,128)(2,1)S(1)}, bf16[768,192]{0,1:T(8,128)(2,1)}, u32[]{:S(2)}) copy-start(bf16[768,192]{0,1:T(8,128)(2,1)} %param.27) | copy-start | bytes 884740
  12.4 1.4 %copy-start.13 = (bf16[192,192]{1,0:T(8,128)(2,1)S(1)}, bf16[192,192]{1,0:T(8,128)(2,1)}, u32[]{:S(2)}) copy-start(bf16[192,192]{1,0:T(8,128)(2,1)} %refs_9_.5) | copy-start | bytes 221188
  21.8 8.4 %collective-permute-start.3 = (bf16[6,144,128]{2,1,0:T(8,128)(2,1)S(1)}, bf16[6,144,128]{2,1,0:T(8,128)(2,1)S(1)}, u32[]{:S(2)}, u32[]{:S(2)}) collective-permute-start(bf16[6,144,128]{2,1,0:T(8,128)(2,1)S(1)} %get-tuple-element.43), channel_id=1, source_target_pairs={{16,0},{32,16},{48,32},{64,48},{80,64},{96,80},{112,96},{0,112},{1... | collective-permute-start | bytes 663560 | tf_op jit(solution)/shard_map/ppermute | solution.py:441
  30.2 1.5 %copy-start = (f32[12,144,144]{2,1,0:T(8,128)S(1)}, f32[12,144,144]{2,1,0:T(8,128)}, u32[]{:S(2)}) copy-start(f32[12,144,144]{2,1,0:T(8,128)} %bias.2) | copy-start | bytes 2985988
  30.4 6.4 %collective-permute-start.4 = (bf16[6,144,128]{2,1,0:T(8,128)(2,1)S(1)}, bf16[6,144,128]{2,1,0:T(8,128)(2,1)S(1)}, u32[]{:S(2)}, u32[]{:S(2)}) collective-permute-start(bf16[6,144,128]{2,1,0:T(8,128)(2,1)S(1)} %pack_second.1), channel_id=1, source_target_pairs={{1,0},{2,1},{3,2},{4,3},{5,4},{6,5},{7,6},{8,7},{9,8},{10,9},{11,1... | collective-permute-start | bytes 663560 | tf_op jit(solution)/shard_map/ppermute | solution.py:442
  32.7 4.2 %copy-start.3 = (bf16[384,1536]{1,0:T(8,128)(2,1)S(1)}, bf16[384,1536]{1,0:T(8,128)(2,1)}, u32[]{:S(2)}) copy-start(bf16[384,1536]{1,0:T(8,128)(2,1)} %w1.1) | copy-start | bytes 3538948
  32.7 4.2 %copy-start.4 = (bf16[1536,384]{1,0:T(8,128)(2,1)S(1)}, bf16[1536,384]{1,0:T(8,128)(2,1)}, u32[]{:S(2)}) copy-start(bf16[1536,384]{1,0:T(8,128)(2,1)} %w2.1) | copy-start | bytes 3538948
  32.7 4.2 %copy-start.6 = (bf16[384,1152]{1,0:T(8,128)(2,1)S(1)}, bf16[384,1152]{1,0:T(8,128)(2,1)}, u32[]{:S(2)}) copy-start(bf16[384,1152]{1,0:T(8,128)(2,1)} %project.3) | copy-start | bytes 2654212
  32.7 4.2 %copy-start.7 = (bf16[768,384]{1,0:T(8,128)(2,1)S(1)}, bf16[768,384]{1,0:T(8,128)(2,1)}, u32[]{:S(2)}) copy-start(bf16[768,384]{1,0:T(8,128)(2,1)} %merge_weight.1) | copy-start | bytes 1769476
  32.7 4.2 %copy-start.8 = (bf16[384,768]{1,0:T(8,128)(2,1)S(1)}, bf16[384,768]{1,0:T(8,128)(2,1)}, u32[]{:S(2)}) copy-start(bf16[384,768]{1,0:T(8,128)(2,1)} %up_first.1) | copy-start | bytes 1769476
  32.7 4.2 %copy-start.11 = (bf16[384,384]{1,0:T(8,128)(2,1)S(1)}, bf16[384,384]{1,0:T(8,128)(2,1)}, u32[]{:S(2)}) copy-start(bf16[384,384]{1,0:T(8,128)(2,1)} %wo.1) | copy-start | bytes 884740
  32.7 4.2 %copy-start.14 = (bf16[192,192]{1,0:T(8,128)(2,1)S(1)}, bf16[192,192]{1,0:T(8,128)(2,1)}, u32[]{:S(2)}) copy-start(bf16[192,192]{1,0:T(8,128)(2,1)} %up_second.1) | copy-start | bytes 221188
  32.7 4.2 %copy-start.15 = (f32[768]{0:T(1024)S(1)}, f32[768]{0:T(1024)}, u32[]{:S(2)}) copy-start(f32[768]{0:T(1024)} %merge_gain.1) | copy-start | bytes 9220
  32.7 4.2 %copy-start.16 = (f32[384]{0:T(512)S(1)}, f32[384]{0:T(512)}, u32[]{:S(2)}) copy-start(f32[384]{0:T(512)} %gain_one.1) | copy-start | bytes 4612
  32.8 4.2 %copy-start.17 = (f32[384]{0:T(512)S(1)}, f32[384]{0:T(512)}, u32[]{:S(2)}) copy-start(f32[384]{0:T(512)} %gain_two.1) | copy-start | bytes 4612
  32.8 4.2 %copy-start.20 = (f32[192]{0:T(256)S(1)}, f32[192]{0:T(256)}, u32[]{:S(2)}) copy-start(f32[192]{0:T(256)} %up_norm.1) | copy-start | bytes 2308
  48.9 13.4 %collective-permute-start.5 = (bf16[6,144,128]{2,1,0:T(8,128)(2,1)S(1)}, bf16[6,144,128]{2,1,0:T(8,128)(2,1)S(1)}, u32[]{:S(2)}, u32[]{:S(2)}) collective-permute-start(bf16[6,144,128]{2,1,0:T(8,128)(2,1)S(1)} %get-tuple-element.53), channel_id=1, source_target_pairs={{127,0},{112,1},{113,2},{114,3},{115,4},{116,5},{117,6},{118,7},{1... | collective-permute-start | bytes 663560 | tf_op jit(solution)/shard_map/ppermute | solution.py:439
  49.0 15.4 %collective-permute-start.6 = (bf16[6,144,128]{2,1,0:T(8,128)(2,1)S(1)}, bf16[6,144,128]{2,1,0:T(8,128)(2,1)S(1)}, u32[]{:S(2)}, u32[]{:S(2)}) collective-permute-start(bf16[6,144,128]{2,1,0:T(8,128)(2,1)S(1)} %get-tuple-element.54), channel_id=1, source_target_pairs={{112,0},{0,16},{16,32},{32,48},{48,64},{64,80},{80,96},{96,112},{1... | collective-permute-start | bytes 663560 | tf_op jit(solution)/shard_map/ppermute | solution.py:441
  49.1 15.3 %collective-permute-start.7 = (bf16[6,144,128]{2,1,0:T(8,128)(2,1)S(1)}, bf16[6,144,128]{2,1,0:T(8,128)(2,1)S(1)}, u32[]{:S(2)}, u32[]{:S(2)}) collective-permute-start(bf16[6,144,128]{2,1,0:T(8,128)(2,1)S(1)} %get-tuple-element.55), channel_id=1, source_target_pairs={{15,0},{0,1},{1,2},{2,3},{3,4},{4,5},{5,6},{6,7},{7,8},{8,9},{9,10... | collective-permute-start | bytes 663560 | tf_op jit(solution)/shard_map/ppermute | solution.py:442
  (5 other events, 6.6 us)

commit v7 on v6

--- a/solution.py
+++ b/solution.py
@@ -484,7 +484,7 @@
         return call(kernel, f"fine_{i}{j}", operands, [out] + outs, scratch, 20, us=5)
 
     (w00,) = fine(0, 0, [], [])
-    lon, lat, diag, w00 = lax.optimization_barrier((lon, lat, diag, w00))
+    lon, diag, w00 = lax.optimization_barrier((lon, diag, w00))
     w01, lat_two = fine(0, 1, [lon, w00], [(halo, BF16)])
     lat_two = shift(lat_two, 1, 0)
     lat, w01 = lax.optimization_barrier((lat, w01))

time: 66.1 us -> 63.9 us (0.967)
  starting transfers between devices: 16.4 us -> 14.5 us
    ppermute x3, starting transfers between devices: 5.91 us -> 3.01 us  [shift(): lax.ppermute(array, 'lat', [((i + lat_by) % lats, i) for i in range(lats)])]
    ppermute x3, starting transfers between devices: 2.13 us -> 3.19 us  [shift(): lax.ppermute(array, 'lon', [((i + lon_by) % lons, i) for i in range(lons)])]
  transfers between devices with their start and end apart: 8 -> 8, of which waited for: 2 -> 3; matrix products, arithmetic and copies ran while one was open for 0% -> 0% of each run, Pallas kernels for 21% -> 28%
where the time goes in v7:
time: 63.9 us; the launch traced here: 63.5 us
  Pallas kernels  31.3 us (49%)
  waiting for transfers between devices  15 us (23%)
  starting transfers between devices  14.5 us (23%)
  local copies, waits for them, and re-layouts  2.1 us (3%)
    pallas_call x10, Pallas kernels, call(): pl.pallas_call(kernel, in_specs=[smem] * scalars + [vmem] * (len(operands...  31.3 us
    ppermute x2, waiting for transfers between devices, shift(): return lax.ppermute(array, ('lat', 'lon'), pairs)  13.4 us
    ppermute x2, starting transfers between devices, shift(): return lax.ppermute(array, ('lat', 'lon'), pairs)  8.35 us
    ppermute x3, starting transfers between devices, shift(): lax.ppermute(array, 'lon', [((i + lon_by) % lons, i) for i in range(lons)])  3.19 us
    ppermute x3, starting transfers between devices, shift(): lax.ppermute(array, 'lat', [((i + lat_by) % lats, i) for i in range(lats)])  3.01 us
    unnamed x42, local copies, waits for them, and re-layouts  2.1 us
    ppermute x3, waiting for transfers between devices, shift(): lax.ppermute(array, 'lat', [((i + lat_by) % lats, i) for i in range(lats)])  1.62 us
  transfers between devices with their start and end apart: 8, of which 3 were waited for; matrix products, arithmetic and copies ran while one was open for 0% of the time, Pallas kernels for 28%

profile of v7, /device:TPU:0, one launch (start us, length us, event | category | flops | bytes accessed | tf_op | source)
XLA Modules:
  0.0 63.5 jit_solution(12369307032737718753)
XLA Ops:
  0.0 1.3 %copy-done.1 = bf16[8,12,24,192]{3,2,1,0:T(8,128)(2,1)S(1)} copy-done((bf16[8,12,24,192]{3,2,1,0:T(8,128)(2,1)S(1)}, bf16[8,12,24,192]{3,2,1,0:T(8,128)(2,1)}, u32[]{:S(2)}) %copy-start.1) | copy-done | bytes 884760
  1.3 0.2 start.1
  1.5 8.3 %collective-permute-start.1 = (bf16[6,48,128]{2,1,0:T(8,128)(2,1)S(1)}, bf16[6,48,128]{2,1,0:T(8,128)(2,1)S(1)}, u32[]{:S(2)}, u32[]{:S(2)}) collective-permute-start(bf16[6,48,128]{2,1,0:T(8,128)(2,1)S(1)} %get-tuple-element.31), channel_id=1, source_target_pairs={{17,0},{18,1},{19,2},{20,3},{21,4},{22,5},{23,6},{24,7},{25,8},{26... | collective-permute-start | bytes 221192 | tf_op jit(solution)/shard_map/ppermute | solution.py:439
  9.8 1.1 %collective-permute-start = (bf16[6,112,128]{2,1,0:T(8,128)(2,1)S(1)}, bf16[6,112,128]{2,1,0:T(8,128)(2,1)S(1)}, u32[]{:S(2)}, u32[]{:S(2)}) collective-permute-start(bf16[6,112,128]{2,1,0:T(8,128)(2,1)S(1)} %get-tuple-element.30), channel_id=1, source_target_pairs={{1,0},{2,1},{3,2},{4,3},{5,4},{6,5},{7,6},{8,7},{9,8},{10,9},{11,1... | collective-permute-start | bytes 516104 | tf_op jit(solution)/shard_map/ppermute | solution.py:442
  10.9 1.4 %collective-permute-start.2 = (bf16[6,112,128]{2,1,0:T(8,128)(2,1)S(1)}, bf16[6,112,128]{2,1,0:T(8,128)(2,1)S(1)}, u32[]{:S(2)}, u32[]{:S(2)}) collective-permute-start(bf16[6,112,128]{2,1,0:T(8,128)(2,1)S(1)} %get-tuple-element.37), channel_id=1, source_target_pairs={{16,0},{32,16},{48,32},{64,48},{80,64},{96,80},{112,96},{0,112},{1... | collective-permute-start | bytes 516104 | tf_op jit(solution)/shard_map/ppermute | solution.py:441
  12.4 0.6 fine_tables.1
  13.0 0.6 copy-done.2
  13.7 0.1 copy-done.10
  13.8 3.9 %fine_00.1.refs_2_.w00 = f32[576,192]{1,0:T(8,128)S(1)} custom-call(bf16[8,12,24,192]{3,2,1,0:T(8,128)(2,1)S(1)} %copy-done.2, f32[2,144,864]{2,1,0:T(8,128)S(1)} %get-tuple-element.32.refs_1_.refs_3_, f32[192]{0:T(256)S(1)} %copy-done.18, bf16[192,192]{1,0:T(8,128)(2,1)S(1)} %get-tuple-element.33.refs_3_.refs_5_.refs_4_.refs_6_, ...), custom_call_target="tpu_custom_call" | custom-call | flops 5242880000 | bytes 3208704 | tf_op jit(solution)/shard_map/fine_00/pallas_call | solution.py:415
  17.7 4.1 %fine_01.1 = (f32[576,192]{1,0:T(8,128)S(1)}, bf16[6,144,128]{2,1,0:T(8,128)(2,1)S(1)}) custom-call(bf16[8,12,24,192]{3,2,1,0:T(8,128)(2,1)S(1)} %copy-done.2, bf16[6,112,128]{2,1,0:T(8,128)(2,1)S(1)} %collective-permute-done.refs_1_.refs_2_, f32[576,192]{1,0:T(8,128)S(1)} %fine_00.1.refs_2_.w00, f32[2,144,864]{2,1,0:T(8,128)S(1)} %get-tuple-element.32.refs_1_.refs_3_, ...), custom_call_target="tpu_custom_call" | custom-call | flops 5242880000 | bytes 4044288 | tf_op jit(solution)/shard_map/fine_01/pallas_call | solution.py:415
  21.8 1.5 %collective-permute-start.3 = (bf16[6,144,128]{2,1,0:T(8,128)(2,1)S(1)}, bf16[6,144,128]{2,1,0:T(8,128)(2,1)S(1)}, u32[]{:S(2)}, u32[]{:S(2)}) collective-permute-start(bf16[6,144,128]{2,1,0:T(8,128)(2,1)S(1)} %get-tuple-element.41), channel_id=1, source_target_pairs={{16,0},{32,16},{48,32},{64,48},{80,64},{96,80},{112,96},{0,112},{1... | collective-permute-start | bytes 663560 | tf_op jit(solution)/shard_map/ppermute | solution.py:441
  23.3 4.0 %fine_10.1.w10 = f32[576,192]{1,0:T(8,128)S(1)} custom-call(bf16[8,12,24,192]{3,2,1,0:T(8,128)(2,1)S(1)} %copy-done.2, bf16[6,112,128]{2,1,0:T(8,128)(2,1)S(1)} %collective-permute-done.2.refs_1_, f32[2,144,864]{2,1,0:T(8,128)S(1)} %get-tuple-element.43.refs_2_.refs_4_, f32[192]{0:T(256)S(1)} %copy-done.18, ...), custom_call_target="tpu_custom_call" | custom-call | flops 5242880000 | bytes 3380736 | tf_op jit(solution)/shard_map/fine_10/pallas_call | solution.py:415
  27.3 1.5 %collective-permute-done.3.lat_in = bf16[6,144,128]{2,1,0:T(8,128)(2,1)S(1)} collective-permute-done((bf16[6,144,128]{2,1,0:T(8,128)(2,1)S(1)}, bf16[6,144,128]{2,1,0:T(8,128)(2,1)S(1)}, u32[]{:S(2)}, u32[]{:S(2)}) %collective-permute-start.3) | collective-permute-done | bytes 221216 | tf_op jit(solution)/shard_map/ppermute | solution.py:441
  28.8 0.2 pack_second.1
  29.0 2.0 %collective-permute-start.4 = (bf16[6,144,128]{2,1,0:T(8,128)(2,1)S(1)}, bf16[6,144,128]{2,1,0:T(8,128)(2,1)S(1)}, u32[]{:S(2)}, u32[]{:S(2)}) collective-permute-start(bf16[6,144,128]{2,1,0:T(8,128)(2,1)S(1)} %pack_second.1), channel_id=1, source_target_pairs={{1,0},{2,1},{3,2},{4,3},{5,4},{6,5},{7,6},{8,7},{9,8},{10,9},{11,1... | collective-permute-start | bytes 663560 | tf_op jit(solution)/shard_map/ppermute | solution.py:442
  31.0 1.0 %coarse_table.1.table_ref = f32[2,144,1728]{2,1,0:T(8,128)S(1)} custom-call(s32[1]{0:T(128)} %bitcast.edge_ref, f32[12,144,144]{2,1,0:T(8,128)S(1)} %copy-done), custom_call_target="tpu_custom_call" | custom-call | tf_op jit(solution)/shard_map/coarse_table/pallas_call | solution.py:415
  32.1 4.0 %fine_11.1.w11 = f32[576,192]{1,0:T(8,128)S(1)} custom-call(bf16[8,12,24,192]{3,2,1,0:T(8,128)(2,1)S(1)} %copy-done.2, bf16[6,112,128]{2,1,0:T(8,128)(2,1)S(1)} %collective-permute-done.2.refs_1_, bf16[6,112,128]{2,1,0:T(8,128)(2,1)S(1)} %collective-permute-done.refs_1_.refs_2_, bf16[6,48,128]{2,1,0:T(8,128)(2,1)S(1)} %collective-permute-done.1.refs_3_, ...), custom_call_target="tpu_custom_call" | custom-call | flops 5242880000 | bytes 3626496 | tf_op jit(solution)/shard_map/fine_11/pallas_call | solution.py:415
  36.2 12.0 %coarse.1 = (bf16[6,144,128]{2,1,0:T(8,128)(2,1)S(1)}, bf16[6,144,128]{2,1,0:T(8,128)(2,1)S(1)}, bf16[6,144,128]{2,1,0:T(8,128)(2,1)S(1)}, bf16[6,144,128]{2,1,0:T(8,128)(2,1)S(1)}) custom-call(f32[576,192]{1,0:T(8,128)S(1)} %fine_00.1.refs_2_.w00, f32[576,192]{1,0:T(8,128)S(1)} %get-tuple-element.40.w01, f32[576,192]{1,0:T(8,128)S(1)} %fine_10.1.w10, ...), custom_call_target="tpu_custom_call" | custom-call | flops 12582912000 | bytes 9886464 | tf_op jit(solution)/shard_map/coarse/pallas_call | solution.py:415
  48.2 0.1 collective-permute-start.5
  48.3 0.1 collective-permute-start.6
  48.4 0.1 collective-permute-start.7
  48.5 13.4 %collective-permute-done.5.upper_left = bf16[6,144,128]{2,1,0:T(8,128)(2,1)S(1)} collective-permute-done((bf16[6,144,128]{2,1,0:T(8,128)(2,1)S(1)}, bf16[6,144,128]{2,1,0:T(8,128)(2,1)S(1)}, u32[]{:S(2)}, u32[]{:S(2)}) %collective-permute-start.5) | collective-permute-done | bytes 221216 | tf_op jit(solution)/shard_map/ppermute | solution.py:439
  61.9 0.1 collective-permute-done.6.upper_right
  62.0 1.3 %finish.1 = bf16[8,12,24,192]{3,2,1,0:T(8,128)(2,1)} custom-call(bf16[6,144,128]{2,1,0:T(8,128)(2,1)S(1)} %collective-permute-done.5.upper_left, bf16[6,144,128]{2,1,0:T(8,128)(2,1)S(1)} %collective-permute-done.6.upper_right, bf16[6,144,128]{2,1,0:T(8,128)(2,1)S(1)} %collective-permute-done.7.lower_left, bf16[6,144,128]{2,1,0:T(8,128)(2,1)S(1)} %get-tuple-element.54.lower_right), custom_call_target="tpu_custom_call" | custom-call | flops 1048576000 | bytes 1769472 | tf_op jit(solution)/shard_map/finish/pallas_call | solution.py:415
  (44 shorter events, 0.2 us)
Async XLA Ops:
  1.3 11.1 %copy-start.5 = (f32[6,144,144]{2,1,0:T(8,128)S(1)}, f32[6,144,144]{2,1,0:T(8,128)}, u32[]{:S(2)}) copy-start(f32[6,144,144]{2,1,0:T(8,128)} %bias.1) | copy-start | bytes 1492996
  1.3 11.1 %copy-start.12 = (bf16[192,576]{1,0:T(8,128)(2,1)S(1)}, bf16[192,576]{1,0:T(8,128)(2,1)}, u32[]{:S(2)}) copy-start(bf16[192,576]{1,0:T(8,128)(2,1)} %project.2) | copy-start | bytes 663556
  1.5 16.2 %collective-permute-start.1 = (bf16[6,48,128]{2,1,0:T(8,128)(2,1)S(1)}, bf16[6,48,128]{2,1,0:T(8,128)(2,1)S(1)}, u32[]{:S(2)}, u32[]{:S(2)}) collective-permute-start(bf16[6,48,128]{2,1,0:T(8,128)(2,1)S(1)} %get-tuple-element.31), channel_id=1, source_target_pairs={{17,0},{18,1},{19,2},{20,3},{21,4},{22,5},{23,6},{24,7},{25,8},{26... | collective-permute-start | bytes 221192 | tf_op jit(solution)/shard_map/ppermute | solution.py:439
  9.8 8.0 %collective-permute-start = (bf16[6,112,128]{2,1,0:T(8,128)(2,1)S(1)}, bf16[6,112,128]{2,1,0:T(8,128)(2,1)S(1)}, u32[]{:S(2)}, u32[]{:S(2)}) collective-permute-start(bf16[6,112,128]{2,1,0:T(8,128)(2,1)S(1)} %get-tuple-element.30), channel_id=1, source_target_pairs={{1,0},{2,1},{3,2},{4,3},{5,4},{6,5},{7,6},{8,7},{9,8},{10,9},{11,1... | collective-permute-start | bytes 516104 | tf_op jit(solution)/shard_map/ppermute | solution.py:442
  10.9 10.9 %collective-permute-start.2 = (bf16[6,112,128]{2,1,0:T(8,128)(2,1)S(1)}, bf16[6,112,128]{2,1,0:T(8,128)(2,1)S(1)}, u32[]{:S(2)}, u32[]{:S(2)}) collective-permute-start(bf16[6,112,128]{2,1,0:T(8,128)(2,1)S(1)} %get-tuple-element.37), channel_id=1, source_target_pairs={{16,0},{32,16},{48,32},{64,48},{80,64},{96,80},{112,96},{0,112},{1... | collective-permute-start | bytes 516104 | tf_op jit(solution)/shard_map/ppermute | solution.py:441
  12.4 1.4 %copy-start.10 = (bf16[768,192]{0,1:T(8,128)(2,1)S(1)}, bf16[768,192]{0,1:T(8,128)(2,1)}, u32[]{:S(2)}) copy-start(bf16[768,192]{0,1:T(8,128)(2,1)} %param.27) | copy-start | bytes 884740
  12.4 1.4 %copy-start.13 = (bf16[192,192]{1,0:T(8,128)(2,1)S(1)}, bf16[192,192]{1,0:T(8,128)(2,1)}, u32[]{:S(2)}) copy-start(bf16[192,192]{1,0:T(8,128)(2,1)} %refs_9_.5) | copy-start | bytes 221188
  21.8 7.0 %collective-permute-start.3 = (bf16[6,144,128]{2,1,0:T(8,128)(2,1)S(1)}, bf16[6,144,128]{2,1,0:T(8,128)(2,1)S(1)}, u32[]{:S(2)}, u32[]{:S(2)}) collective-permute-start(bf16[6,144,128]{2,1,0:T(8,128)(2,1)S(1)} %get-tuple-element.41), channel_id=1, source_target_pairs={{16,0},{32,16},{48,32},{64,48},{80,64},{96,80},{112,96},{0,112},{1... | collective-permute-start | bytes 663560 | tf_op jit(solution)/shard_map/ppermute | solution.py:441
  27.3 3.7 %copy-start = (f32[12,144,144]{2,1,0:T(8,128)S(1)}, f32[12,144,144]{2,1,0:T(8,128)}, u32[]{:S(2)}) copy-start(f32[12,144,144]{2,1,0:T(8,128)} %bias.2) | copy-start | bytes 2985988
  29.0 7.1 %collective-permute-start.4 = (bf16[6,144,128]{2,1,0:T(8,128)(2,1)S(1)}, bf16[6,144,128]{2,1,0:T(8,128)(2,1)S(1)}, u32[]{:S(2)}, u32[]{:S(2)}) collective-permute-start(bf16[6,144,128]{2,1,0:T(8,128)(2,1)S(1)} %pack_second.1), channel_id=1, source_target_pairs={{1,0},{2,1},{3,2},{4,3},{5,4},{6,5},{7,6},{8,7},{9,8},{10,9},{11,1... | collective-permute-start | bytes 663560 | tf_op jit(solution)/shard_map/ppermute | solution.py:442
  31.9 4.2 %copy-start.3 = (bf16[384,1536]{1,0:T(8,128)(2,1)S(1)}, bf16[384,1536]{1,0:T(8,128)(2,1)}, u32[]{:S(2)}) copy-start(bf16[384,1536]{1,0:T(8,128)(2,1)} %w1.1) | copy-start | bytes 3538948
  32.0 4.2 %copy-start.4 = (bf16[1536,384]{1,0:T(8,128)(2,1)S(1)}, bf16[1536,384]{1,0:T(8,128)(2,1)}, u32[]{:S(2)}) copy-start(bf16[1536,384]{1,0:T(8,128)(2,1)} %w2.1) | copy-start | bytes 3538948
  32.0 4.2 %copy-start.6 = (bf16[384,1152]{1,0:T(8,128)(2,1)S(1)}, bf16[384,1152]{1,0:T(8,128)(2,1)}, u32[]{:S(2)}) copy-start(bf16[384,1152]{1,0:T(8,128)(2,1)} %project.3) | copy-start | bytes 2654212
  32.0 4.2 %copy-start.7 = (bf16[768,384]{1,0:T(8,128)(2,1)S(1)}, bf16[768,384]{1,0:T(8,128)(2,1)}, u32[]{:S(2)}) copy-start(bf16[768,384]{1,0:T(8,128)(2,1)} %merge_weight.1) | copy-start | bytes 1769476
  32.0 4.2 %copy-start.8 = (bf16[384,768]{1,0:T(8,128)(2,1)S(1)}, bf16[384,768]{1,0:T(8,128)(2,1)}, u32[]{:S(2)}) copy-start(bf16[384,768]{1,0:T(8,128)(2,1)} %up_first.1) | copy-start | bytes 1769476
  32.0 4.2 %copy-start.11 = (bf16[384,384]{1,0:T(8,128)(2,1)S(1)}, bf16[384,384]{1,0:T(8,128)(2,1)}, u32[]{:S(2)}) copy-start(bf16[384,384]{1,0:T(8,128)(2,1)} %wo.1) | copy-start | bytes 884740
  32.0 4.2 %copy-start.14 = (bf16[192,192]{1,0:T(8,128)(2,1)S(1)}, bf16[192,192]{1,0:T(8,128)(2,1)}, u32[]{:S(2)}) copy-start(bf16[192,192]{1,0:T(8,128)(2,1)} %up_second.1) | copy-start | bytes 221188
  32.0 4.2 %copy-start.15 = (f32[768]{0:T(1024)S(1)}, f32[768]{0:T(1024)}, u32[]{:S(2)}) copy-start(f32[768]{0:T(1024)} %merge_gain.1) | copy-start | bytes 9220
  32.0 4.2 %copy-start.16 = (f32[384]{0:T(512)S(1)}, f32[384]{0:T(512)}, u32[]{:S(2)}) copy-start(f32[384]{0:T(512)} %gain_one.1) | copy-start | bytes 4612
  32.1 4.2 %copy-start.17 = (f32[384]{0:T(512)S(1)}, f32[384]{0:T(512)}, u32[]{:S(2)}) copy-start(f32[384]{0:T(512)} %gain_two.1) | copy-start | bytes 4612
  32.1 4.2 %copy-start.20 = (f32[192]{0:T(256)S(1)}, f32[192]{0:T(256)}, u32[]{:S(2)}) copy-start(f32[192]{0:T(256)} %up_norm.1) | copy-start | bytes 2308
  48.2 13.6 %collective-permute-start.5 = (bf16[6,144,128]{2,1,0:T(8,128)(2,1)S(1)}, bf16[6,144,128]{2,1,0:T(8,128)(2,1)S(1)}, u32[]{:S(2)}, u32[]{:S(2)}) collective-permute-start(bf16[6,144,128]{2,1,0:T(8,128)(2,1)S(1)} %get-tuple-element.51), channel_id=1, source_target_pairs={{127,0},{112,1},{113,2},{114,3},{115,4},{116,5},{117,6},{118,7},{1... | collective-permute-start | bytes 663560 | tf_op jit(solution)/shard_map/ppermute | solution.py:439
  48.3 13.7 %collective-permute-start.6 = (bf16[6,144,128]{2,1,0:T(8,128)(2,1)S(1)}, bf16[6,144,128]{2,1,0:T(8,128)(2,1)S(1)}, u32[]{:S(2)}, u32[]{:S(2)}) collective-permute-start(bf16[6,144,128]{2,1,0:T(8,128)(2,1)S(1)} %get-tuple-element.52), channel_id=1, source_target_pairs={{112,0},{0,16},{16,32},{32,48},{48,64},{64,80},{80,96},{96,112},{1... | collective-permute-start | bytes 663560 | tf_op jit(solution)/shard_map/ppermute | solution.py:441
  48.4 13.6 %collective-permute-start.7 = (bf16[6,144,128]{2,1,0:T(8,128)(2,1)S(1)}, bf16[6,144,128]{2,1,0:T(8,128)(2,1)S(1)}, u32[]{:S(2)}, u32[]{:S(2)}) collective-permute-start(bf16[6,144,128]{2,1,0:T(8,128)(2,1)S(1)} %get-tuple-element.53), channel_id=1, source_target_pairs={{15,0},{0,1},{1,2},{2,3},{3,4},{4,5},{5,6},{6,7},{7,8},{8,9},{9,10... | collective-permute-start | bytes 663560 | tf_op jit(solution)/shard_map/ppermute | solution.py:442
  (5 other events, 6.6 us)
